TPU v7x, 256 devices: a whole 4x4x8 slice. The times are simulated.
256 devices in a mesh: dp: 64 (over y, z, core), head: 4 (over x).
Axes of the slice: x: 4, y: 4, z: 8, core: 2. Of those that a mesh axis runs over, the one named last changes fastest.
Arguments:
- queries: bfloat16 [256, 2, 128, 576], P('dp', None, 'head'), may hold values from -200 to 200
- new_entries: bfloat16 [256, 2, 576], P('dp'), may hold values from -4 to 4
- cache: bfloat16 [256, 1024, 576], P('dp'), may hold values from -3 to 3
- lengths: int32 [256], P('dp'), may hold values from 64 to 1024, as said below
- hidden: bfloat16 [256, 2, 7168], P(None, None, 'dp'), may hold values from -1.1953125 to 1.1953125
- w_uv: bfloat16 [128, 512, 128], P('head'), may hold values from -0.25 to 0.25
- w_o: bfloat16 [16384, 7168], P('head', 'dp'), may hold values from -0.09375 to 0.09375
- ffn_gain: bfloat16 [7168], replicated, may hold values from 0.099609375 to 1.8984375
- w_gate: bfloat16 [7168, 18432], P('head', 'dp'), may hold values from -0.0625 to 0.0625
- w_up: bfloat16 [7168, 18432], P('head', 'dp'), may hold values from -0.0625 to 0.0625
- w_down: bfloat16 [18432, 7168], P('dp', 'head'), may hold values from -0.09375 to 0.09375
Outputs:
- layer_out: bfloat16 [256, 2, 7168], P('dp', None, 'head')
Inputs may be any that keep to these rules, and one draw needn't show every extreme that they name: Each rollout's cache holds lengths[b] used positions; some rollout has 1024 and some has 64.
All inputs are finite; a program needn't handle non-finite values.
Results may differ from a plain program's by a relative error of at most 0.024.
Values may be sent and summed in bfloat16 or wider, within the bound.
No kernel may reach another device: no remote copies, remote signals or barrier semaphores. Data moves between devices by JAX's collectives and lax.ppermute only.
A program may use at most 128 MiB of HBM per device.

v0:
```python
import jax
import jax.numpy as jnp
from jax import lax
from jax.sharding import PartitionSpec as P

ROPE = 64
NOPE = 128


def on_device(
    queries, new_entries, cache, lengths, hidden, w_uv, w_o, ffn_gain, w_gate, w_up, w_down
):
    roll, steps, heads, entry = queries.shape
    latent = w_uv.shape[1]
    value_width = w_uv.shape[2]
    span = cache.shape[1]
    scale = (NOPE + ROPE) ** (-0.5)
    qrows = queries.reshape(roll, steps * heads, entry)
    cache_scores = (
        jnp.einsum("rqe,rke->rqk", qrows, cache, preferred_element_type=jnp.float32) * scale
    )
    new_scores = (
        jnp.einsum("rqe,rne->rqn", qrows, new_entries, preferred_element_type=jnp.float32) * scale
    )
    valid = lax.iota(jnp.int32, span)[None, :] < lengths[:, None]
    cache_scores = jnp.where(valid[:, None, :], cache_scores, -1e30)
    step_of_row = lax.iota(jnp.int32, steps * heads) // heads
    causal = lax.iota(jnp.int32, steps)[None, :] <= step_of_row[:, None]
    new_scores = jnp.where(causal[None], new_scores, -1e30)
    top = jnp.maximum(jnp.max(cache_scores, axis=2), jnp.max(new_scores, axis=2))
    cache_exp = jnp.exp(cache_scores - top[..., None])
    new_exp = jnp.exp(new_scores - top[..., None])
    total = jnp.sum(cache_exp, axis=2) + jnp.sum(new_exp, axis=2)
    cache_weights = (cache_exp / total[..., None]).astype(jnp.bfloat16)
    new_weights = (new_exp / total[..., None]).astype(jnp.bfloat16)
    latent_out = jnp.einsum(
        "rqk,rkc->rqc", cache_weights, cache[:, :, :latent], preferred_element_type=jnp.float32
    )
    latent_out = latent_out + jnp.einsum(
        "rqn,rnc->rqc", new_weights, new_entries[:, :, :latent], preferred_element_type=jnp.float32
    )
    latent_out = latent_out.astype(jnp.bfloat16).reshape(roll * steps, heads * latent)
    count = latent_out.shape[0]
    split = latent_out.reshape(count, heads, latent)
    projected = jnp.einsum("nhc,hcv->nhv", split, w_uv, preferred_element_type=jnp.float32)
    head_out = projected.astype(jnp.bfloat16).reshape(count, heads * value_width)
    attn_part = jnp.dot(
        lax.all_gather(head_out, "dp", axis=0, tiled=True), w_o, preferred_element_type=jnp.float32
    )
    hidden_rows = hidden.reshape(-1, hidden.shape[2])
    attn = lax.psum(attn_part, "head")
    resid = (hidden_rows.astype(jnp.float32) + attn).astype(jnp.bfloat16)
    whole = lax.all_gather(resid, "dp", axis=1, tiled=True)
    whole_f = whole.astype(jnp.float32)
    mean_sq = jnp.mean(whole_f * whole_f, axis=1, keepdims=True)
    normed = (whole_f * lax.rsqrt(mean_sq + 1e-06) * ffn_gain.astype(jnp.float32)[None, :]).astype(
        jnp.bfloat16
    )
    width = w_gate.shape[0]
    col_start = lax.axis_index("head") * width
    normed_slice = lax.dynamic_slice_in_dim(normed, col_start, width, 1)
    gate_part = jnp.dot(normed_slice, w_gate, preferred_element_type=jnp.float32)
    up_part = jnp.dot(normed_slice, w_up, preferred_element_type=jnp.float32)
    gate, up = (
        lax.psum(gate_part.astype(jnp.bfloat16), "head").astype(jnp.float32),
        lax.psum(up_part.astype(jnp.bfloat16), "head").astype(jnp.float32),
    )
    act = (jax.nn.silu(gate) * up).astype(jnp.bfloat16)
    own_rows = roll * steps
    ffn_out = lax.psum_scatter(
        jnp.dot(act, w_down, preferred_element_type=jnp.float32),
        "dp",
        scatter_dimension=0,
        tiled=True,
    )
    row_start = lax.axis_index("dp") * own_rows
    resid_own = lax.dynamic_slice(whole, (row_start, col_start), (own_rows, width))
    layer_out = (resid_own.astype(jnp.float32) + ffn_out).astype(jnp.bfloat16)
    return layer_out.reshape(roll, steps, width)


def solution(mesh):
    placed = (
        P("dp", None, "head", None),
        P("dp", None, None),
        P("dp", None, None),
        P("dp"),
        P(None, None, "dp"),
        P("head", None, None),
        P("head", "dp"),
        P(),
        P("head", "dp"),
        P("head", "dp"),
        P("dp", "head"),
    )
    return jax.shard_map(
        on_device, mesh=mesh, in_specs=placed, out_specs=P("dp", None, "head"), check_vma=False
    )
```

profile of v0, /device:TPU:2, one launch (start us, length us, event | category | flops | bytes accessed | tf_op | source)
XLA Modules:
  0.0 454.3 jit_solution(2058891164398216584)
XLA Ops:
  6.5 0.0 copy-start
  6.5 0.0 all-gather.3.cloned.1.call-start
  6.6 0.8 iota_compare_fusion
  7.4 0.0 slice-start
  7.4 1.4 fusion.28
  8.7 0.0 slice-start.1
  8.7 3.6 fusion.27
  12.4 0.3 fusion.8
  12.7 0.0 slice-done
  12.7 0.0 slice-done.1
  12.7 0.0 copy-start.5
  12.7 0.0 copy-start.2
  12.7 1.4 fusion
  14.2 0.0 copy-done.5
  14.2 0.0 copy-start.3
  14.2 0.3 fusion.5
  14.5 0.5 copy-done.2
  14.9 0.0 copy-start.4
  14.9 1.4 fusion.6
  16.3 0.0 copy-start.6
  16.3 0.0 all-gather.3.cloned.1.call-update
  16.3 0.0 all-reduce.4.cloned.1.call-start
  16.4 82.1 %all-gather.3.cloned.1.call-done = bf16[512,4096]{1,0:T(8,128)(2,1)} async-done(((bf16[8,4096]{1,0:T(8,128)(2,1)}), bf16[512,4096]{1,0:T(8,128)(2,1)}) %all-gather.3.cloned.1.call-update) | async-done | bytes 4194320 | tf_op jit(solution)/shard_map/all_gather | solution.py:48
  98.5 0.0 copy-done.3
  98.5 4.4 fusion.29
  102.9 0.0 all-reduce.4.cloned.1.call-update
  102.9 0.0 all-gather.5.cloned.1.call-start
  102.9 0.0 copy-done.4
  102.9 0.1 copy.35
  103.1 0.1 copy.38
  103.2 42.7 %all-reduce.4.cloned.1.call-done = f32[512,112]{0,1:T(8,128)} async-done(((f32[512,112]{0,1:T(8,128)}), f32[512,112]{0,1:T(8,128)}) %all-reduce.4.cloned.1.call-update) | async-done | bytes 229392 | tf_op jit(solution)/shard_map/psum | solution.py:51
  145.9 1.6 add_convert_fusion
  147.5 0.0 all-gather.5.cloned.1.call-update
  147.5 0.0 all-reduce.6.cloned.1.call-start
  147.6 0.0 copy-done.6
  147.6 0.1 dynamic-slice
  147.7 85.1 %all-gather.5.cloned.1.call-done = bf16[512,7168]{0,1:T(8,128)(2,1)} async-done(((bf16[512,112]{0,1:T(8,128)(2,1)}), bf16[512,7168]{0,1:T(8,128)(2,1)}) %all-gather.5.cloned.1.call-update) | async-done | bytes 7340048 | tf_op jit(solution)/shard_map/all_gather | solution.py:53
  232.7 0.0 copy-start.1
  232.7 4.8 %multiply_reduce_fusion = f32[512]{0:T(512)S(1)} fusion(bf16[512,7168]{0,1:T(8,128)(2,1)} %all-gather.5.cloned.1.call-done), kind=kLoop, calls=%fused_computation | loop fusion | flops 11009536 | bytes 7342080 | tf_op jit(solution)/shard_map/reduce_sum | solution.py:55
  237.5 0.4 copy-done.1
  237.9 0.0 copy-start.7
  237.9 7.3 %convert_element_type.63 = f32[512,7168]{0,1:T(8,128)} convert(bf16[512,7168]{0,1:T(8,128)(2,1)S(1)} %copy-done.1) | non-fusion elementwise | flops 3670016 | bytes 22020096 | tf_op jit(solution)/shard_map/convert_element_type | solution.py:54
  245.2 0.0 copy-done.7
  245.2 0.0 copy-start.8
  245.2 3.7 convolution_convert_fusion
  248.9 0.0 copy-done.8
  248.9 3.6 convolution_convert_fusion.1
  252.5 0.0 all-reduce.6.cloned.1.call-update
  252.5 0.0 reduce-scatter.4.cloned.1.call-start
  252.6 44.5 %all-reduce.6.cloned.1.call-done = (bf16[512,288]{0,1:T(8,128)(2,1)}, bf16[512,288]{0,1:T(8,128)(2,1)}) async-done(((bf16[512,288]{0,1:T(8,128)(2,1)}, bf16[512,288]{0,1:T(8,128)(2,1)}), (bf16[512,288]{0,1:T(8,128)(2,1)}, bf16[512,288]{0,1:T(8,128)(2,1)})) %all-reduce.6.cloned.1.call-update) | async-done | bytes 589840 | tf_op jit(solution)/shard_map/psum | solution.py:66
  297.1 0.0 copy-done
  297.1 4.0 fusion.16
  301.1 0.0 reduce-scatter.4.cloned.1.call-update
  301.2 1.3 dynamic_slice.6
  302.4 0.2 copy.46
  302.6 143.7 %reduce-scatter.4.cloned.1.call-done = f32[8,1792]{1,0:T(8,128)} async-done(((f32[512,1792]{1,0:T(8,128)}), f32[8,1792]{1,0:T(8,128)}) %reduce-scatter.4.cloned.1.call-update) | async-done | bytes 57360 | tf_op jit(solution)/shard_map/reduce_scatter | solution.py:70
  446.3 0.8 add_convert_fusion.1
  447.1 0.6 reshape.82
  (7 shorter events, 0.1 us)
Async XLA Ops:
  6.5 290.6 %copy-start = (bf16[288,1792]{1,0:T(8,128)(2,1)S(1)}, bf16[288,1792]{1,0:T(8,128)(2,1)}, u32[]{:S(2)}) copy-start(bf16[288,1792]{1,0:T(8,128)(2,1)} %param.21) | copy-start | bytes 3096580
  6.5 91.9 %all-gather.3.cloned.1.call-start = ((), (), s32[]{:S(2)}) async-start(), calls=%async_computation.1 | async-start | bytes 4259840 | tf_op jit(solution)/shard_map/all_gather | solution.py:48
  7.4 5.3 %slice-start = ((s8[4718592]{0:T(1024)(128)(4,1)}), s8[4194304]{0:T(1024)(128)(4,1)S(1)}, s32[]{:S(2)}) async-start(s8[4718592]{0:T(1024)(128)(4,1)} %bitcast.18), calls=%async_computation.6 | async-start | bytes 8388608
  8.7 4.0 slice-start.1
  12.7 1.4 copy-start.5
  12.7 2.2 copy-start.2
  14.2 84.3 %copy-start.3 = (bf16[4096,112]{0,1:T(8,128)(2,1)S(1)}, bf16[4096,112]{0,1:T(8,128)(2,1)}, u32[]{:S(2)}) copy-start(bf16[4096,112]{0,1:T(8,128)(2,1)} %param.17) | copy-start | bytes 2752516
  14.9 88.0 %copy-start.4 = (bf16[256,2,112]{0,2,1:T(8,128)(2,1)S(1)}, bf16[256,2,112]{0,2,1:T(8,128)(2,1)}, u32[]{:S(2)}) copy-start(bf16[256,2,112]{0,2,1:T(8,128)(2,1)} %param.15) | copy-start | bytes 344068
  16.3 131.3 %copy-start.6 = (bf16[7168]{0:T(1024)(128)(2,1)S(1)}, bf16[7168]{0:T(1024)(128)(2,1)}, u32[]{:S(2)}) copy-start(bf16[7168]{0:T(1024)(128)(2,1)} %param.18) | copy-start | bytes 43012
  16.3 129.5 %all-reduce.4.cloned.1.call-start = ((), (), s32[]{:S(2)}) async-start(), calls=%async_computation.2 | async-start | bytes 458752 | tf_op jit(solution)/shard_map/psum | solution.py:51
  102.9 129.8 %all-gather.5.cloned.1.call-start = ((), (), s32[]{:S(2)}) async-start(), calls=%async_computation.3 | async-start | bytes 7454720 | tf_op jit(solution)/shard_map/all_gather | solution.py:53
  147.5 149.6 %all-reduce.6.cloned.1.call-start = ((), (), s32[]{:S(2)}) async-start(), calls=%async_computation.5 | async-start | bytes 1179648 | tf_op jit(solution)/shard_map/psum | solution.py:66
  232.7 5.2 %copy-start.1 = (bf16[512,7168]{0,1:T(8,128)(2,1)S(1)}, bf16[512,7168]{0,1:T(8,128)(2,1)}, u32[]{:S(2)}) copy-start(bf16[512,7168]{0,1:T(8,128)(2,1)} %all-gather.5.cloned.1.call-done) | copy-start | bytes 22020100
  237.9 7.3 %copy-start.7 = (bf16[1792,288]{0,1:T(8,128)(2,1)S(1)}, bf16[1792,288]{0,1:T(8,128)(2,1)}, u32[]{:S(2)}) copy-start(bf16[1792,288]{0,1:T(8,128)(2,1)} %param.20) | copy-start | bytes 3096580
  245.2 3.7 copy-start.8
  252.5 193.8 %reduce-scatter.4.cloned.1.call-start = ((), (), s32[]{:S(2)}) async-start(), calls=%async_computation.4 | async-start | bytes 3727360 | tf_op jit(solution)/shard_map/reduce_scatter | solution.py:70
Sparse Core Ops, SparseCore 0:
  16.4 81.9 all-gather.2
  103.0 42.8 all-reduce.3
  149.0 83.6 all-gather.4
  252.7 44.3 all-reduce.5
  301.7 144.6 reduce-scatter.3
where the time goes:
time: 455 us; the launch traced here: 454 us
  waiting for transfers between devices  398 us (87%)
  matrix products  23.7 us (5%)
  other arithmetic  15.7 us (3%)
  between operations  13.3 us (3%)
    reduce_scatter x1, waiting for transfers between devices, on_device(): lax.psum_scatter(jnp.dot(act, w_down, preferred_element_type=jnp.float32)...  144 us
    all_gather x1, waiting for transfers between devices, on_device(): whole = lax.all_gather(resid, 'dp', axis=1, tiled=True)  85.1 us
    all_gather x1, waiting for transfers between devices, on_device(): lax.all_gather(head_out, 'dp', axis=0, tiled=True)  82.1 us
    psum x1, waiting for transfers between devices, on_device(): lax.psum(up_part.astype(jnp.bfloat16), 'head').astype(jnp.float32)  44.5 us
    psum x1, waiting for transfers between devices, on_device(): attn = lax.psum(attn_part, 'head')  42.7 us
  transfers between devices with their start and end apart: 5, of which 5 were waited for; matrix products, arithmetic and copies ran while one was open for 0% of the time, Pallas kernels for 0%

commit v1 on v0

v1 whole, which is shorter than its diff:
```python
import jax
import jax.numpy as jnp
from jax import lax
from jax.experimental import pallas as pl
from jax.experimental.pallas import tpu as pltpu
from jax.sharding import Mesh
from jax.sharding import PartitionSpec as P

ROPE = 64
NOPE = 128
NY, NZ, NC, NX = 4, 8, 2, 4
F32 = jnp.float32
BF16 = jnp.bfloat16
VMEM = pl.BlockSpec(memory_space=pltpu.VMEM)
ANY = pl.BlockSpec(memory_space=pl.ANY)
HBM = pl.BlockSpec(memory_space=pltpu.HBM)
SMEM = pl.BlockSpec(memory_space=pltpu.SMEM)
LARGE = pltpu.CompilerParams(vmem_limit_bytes=60 * 1024 * 1024)
SMALL = pltpu.CompilerParams(vmem_limit_bytes=16 * 1024 * 1024)


def dot(a, b):
    return jnp.dot(a, b, preferred_element_type=F32)


def dot_t(a, b):
    return lax.dot_general(a, b, (((1,), (1,)), ((), ())), preferred_element_type=F32)


def shift(n, k):
    return [(i, (i + k) % n) for i in range(n)]


def fetch(v, axis, n):
    return [v] + [lax.ppermute(v, axis, shift(n, -k)) for k in range(1, n)]


def ring(v, c, extras, other):
    blocks = [v] + [None] * (NZ - 1)
    up, down = v, v
    done = []
    for k in range(1, NZ // 2):
        up = lax.ppermute(up, "z", shift(NZ, 1))
        down = lax.ppermute(down, "z", shift(NZ, -1))
        blocks[NZ - k], blocks[k] = up, down
        done.append(other(lax.optimization_barrier((extras[k - 1], up))[0]))
    ways = [
        (i * NC + core, (i + way) % NZ * NC + core)
        for i in range(NZ)
        for core, way in ((0, 1), (1, NZ - 1))
    ]
    last = lax.ppermute(jnp.where(c == 0, up, down), ("z", "c"), ways)
    blocks[NZ // 2], done = lax.optimization_barrier((last, done))
    return blocks, done


def moved(rows, source):
    i = lax.broadcasted_iota(jnp.int32, (rows, rows), 0)
    j = lax.broadcasted_iota(jnp.int32, (rows, rows), 1)
    return (source(i) == j).astype(BF16)


def attend_kernel(scale, lengths, queries, new_entries, entries, w_uv, out, latents, cache, w, sems):
    count, entry, span = cache.shape
    steps, heads = queries.shape[1:3]
    latent = latents.shape[2]
    value = w.shape[2]
    loads = [pltpu.make_async_copy(entries.at[r], cache.at[r], sems.at[r]) for r in range(count)]
    loads.append(pltpu.make_async_copy(w_uv, w, sems.at[count]))
    for load in loads:
        load.start()
    for r in range(count):
        rows = queries[r].reshape(steps * heads, entry)
        fresh = new_entries[r].astype(F32)
        step = lax.broadcasted_iota(jnp.int32, (steps * heads, 1), 0) // heads
        late = []
        for n in range(steps):
            s = jnp.sum(rows.astype(F32) * fresh[n : n + 1, :], axis=1, keepdims=True) * scale
            late.append(jnp.where(step >= n, s, -1e30))
        loads[r].wait()
        scores = dot(rows, cache[r]) * scale
        valid = lax.broadcasted_iota(jnp.int32, scores.shape, 1) < lengths[r]
        scores = jnp.where(valid, scores, -1e30)
        top = jnp.max(scores, axis=1, keepdims=True)
        for s in late:
            top = jnp.maximum(top, s)
        weights = jnp.exp(scores - top)
        late = [jnp.exp(s - top) for s in late]
        share = 1.0 / (jnp.sum(weights, axis=1, keepdims=True) + sum(late))
        result = dot_t((weights * share).astype(BF16), cache[r, :latent, :])
        for n in range(steps):
            result = result + (late[n] * share).astype(BF16).astype(F32) * fresh[n : n + 1, :latent]
        result = result.astype(BF16).astype(F32)
        for t in range(steps):
            latents[:, r * steps + t, :] = result[t * heads : (t + 1) * heads]
    loads[count].wait()
    for h in range(heads):
        out[:, h * value : (h + 1) * value] = dot(latents[h].astype(BF16), w[h]).astype(BF16)


def attend(queries, new_entries, cache, lengths, w_uv):
    rolls, steps, heads, entry = queries.shape
    _, latent, value = w_uv.shape
    return pl.pallas_call(
        lambda *refs: attend_kernel((NOPE + ROPE) ** (-0.5), *refs),
        out_shape=jax.ShapeDtypeStruct((rolls * steps, heads * value), BF16),
        in_specs=[SMEM, VMEM, VMEM, HBM, HBM],
        out_specs=VMEM,
        scratch_shapes=[
            pltpu.VMEM((heads, rolls * steps, latent), F32),
            pltpu.VMEM(cache.shape, BF16),
            pltpu.VMEM(w_uv.shape, BF16),
            pltpu.SemaphoreType.DMA((rolls + 1,)),
        ],
        compiler_params=LARGE,
        name="attend",
    )(lengths, queries, new_entries, cache, w_uv)


def project_kernel(count, place, *refs):
    pieces, refs = refs[:count], refs[count:]
    (w_own, w_alien, hidden, hidden_alien), outs = refs[:4], refs[4 : 4 + NX]
    lhs, w, sems = refs[4 + NX :]
    y, z, c, x = place[0], place[1], place[2], place[3]
    cols = w_own.shape[0]
    loads = [
        pltpu.make_async_copy(
            v, w.at[pl.ds(pl.multiple_of(at * cols, 16), cols)], sems.at[count + n]
        )
        for n, (v, at) in enumerate(((w_own, c), (w_alien, 1 - c)))
    ]
    rows = pieces[0].shape[0]
    for n, piece in enumerate(pieces):
        loads.append(
            pltpu.make_async_copy(piece, lhs.at[pl.ds(n * rows, rows)], sems.at[n])
        )
    for load in loads:
        load.start()

    def stream(values):
        steps = values.shape[0] // cols
        i = lax.broadcasted_iota(jnp.int32, (outs[0].shape[0], values.shape[1]), 0)
        j = lax.broadcasted_iota(jnp.int32, (outs[0].shape[0], values.shape[1]), 1)
        here = (lax.shift_right_logical(i, 1) * NC + c) * NX + x == j
        total = 0.0
        for t in range(steps):
            chosen = (here & ((i & 1) == t)).astype(BF16)
            total = total + dot_t(chosen, values[t * cols : (t + 1) * cols])
        return total

    own, alien = stream(hidden), stream(hidden_alien)
    added = jnp.concatenate(
        [jnp.where(c == 0, own, alien), jnp.where(c == 0, alien, own)], axis=1
    )

    def source(i):
        roll = (lax.shift_right_logical(i, 6) + x) & 3
        zz = (lax.shift_right_logical(i, 1) + NZ - z) & 7
        yy = (lax.shift_right_logical(i, 4) + NY - y) & 3
        return zz * 32 + yy * 8 + roll * 2 + (i & 1)

    order = moved(lhs.shape[0], source)
    for load in loads:
        load.wait()
    part = dot_t(lhs[...], w[...]).astype(BF16)
    part = dot(order, part)
    size = outs[0].shape[0]
    outs[0][...] = (part[:size] + added).astype(BF16)
    for n in range(1, NX):
        outs[n][...] = part[n * size : (n + 1) * size].astype(BF16)


def project(place, pieces, weights, hidden):
    rows = sum(p.shape[0] for p in pieces)
    cols, depth = weights[0].shape
    return pl.pallas_call(
        lambda *refs: project_kernel(len(pieces), *refs),
        out_shape=[jax.ShapeDtypeStruct((rows // NX, NC * cols), BF16)] * NX,
        in_specs=[SMEM] + [ANY] * len(pieces) + [HBM] * NC + [VMEM] * NC,
        out_specs=[VMEM] * NX,
        scratch_shapes=[
            pltpu.VMEM((rows, depth), BF16),
            pltpu.VMEM((NC * cols, depth), BF16),
            pltpu.SemaphoreType.DMA((len(pieces) + NC,)),
        ],
        compiler_params=LARGE,
        name="project",
    )(place, *pieces, *weights, *hidden)


def gate_up_kernel(place, gain, blocks, w0, w1, w2, w3, o0, o1, o2, o3, scaled, w, sems):
    hid = w0.shape[0]
    loads = [
        pltpu.make_async_copy(v, w.at[pl.ds(n * hid, hid)], sems.at[n])
        for n, v in enumerate((w0, w1, w2, w3))
    ]
    for load in loads:
        load.start()
    ny, nz, rows, cols = blocks.shape
    x = place[3]
    squares = [0.0] * ny
    for b in range(nz):
        for k in range(ny):
            block = blocks[(x + k) & 3, b].astype(F32)
            squares[k] = squares[k] + jnp.sum(block * block, axis=1, keepdims=True)
            scaled[k * rows : (k + 1) * rows, b * cols : (b + 1) * cols] = (
                block * gain[b : b + 1, :]
            ).astype(BF16)
    outs = (o0, o1, o2, o3)
    for n in range(NC):
        for load in loads[2 * n : 2 * n + 2]:
            load.wait()
        total = dot_t(scaled[...], w[2 * n * hid : 2 * (n + 1) * hid]).astype(BF16)
        for k, out in enumerate(outs):
            out[:, 2 * n * hid : 2 * (n + 1) * hid] = total[k * rows : (k + 1) * rows]
    for k, out in enumerate(outs):
        out[:, 4 * hid :] = jnp.broadcast_to(squares[k].astype(BF16), (rows, 128))


def gate_up(place, gain, blocks, weights):
    ny, nz, rows, cols = blocks.shape
    hid, width = weights[0].shape
    return pl.pallas_call(
        gate_up_kernel,
        out_shape=[jax.ShapeDtypeStruct((rows, 4 * hid + 128), BF16)] * ny,
        in_specs=[SMEM] + [VMEM] * 2 + [HBM] * 4,
        out_specs=[VMEM] * ny,
        scratch_shapes=[
            pltpu.VMEM((ny * rows, width), BF16),
            pltpu.VMEM((4 * hid, width), BF16),
            pltpu.SemaphoreType.DMA((4,)),
        ],
        compiler_params=LARGE,
        name="gate_up",
    )(place, gain, blocks, *weights)


def activate_kernel(features, hid, m0, m1, m2, m3, act):
    both = (m0[...].astype(F32) + m1[...].astype(F32)) + (
        m2[...].astype(F32) + m3[...].astype(F32)
    )
    both = both[:, : 4 * hid] * lax.rsqrt(both[:, 4 * hid : 4 * hid + 1] / features + 1e-06)
    for n in range(NC):
        gate = both[:, 2 * n * hid : (2 * n + 1) * hid]
        up = both[:, (2 * n + 1) * hid : (2 * n + 2) * hid]
        act[:, n * hid : (n + 1) * hid] = (jax.nn.silu(gate) * up).astype(BF16)


def activate(messages, features, hid):
    return pl.pallas_call(
        lambda *refs: activate_kernel(features, hid, *refs),
        out_shape=jax.ShapeDtypeStruct((messages[0].shape[0], NC * hid), BF16),
        in_specs=[VMEM] * NX,
        out_specs=VMEM,
        compiler_params=SMALL,
        name="activate",
    )(*messages)


def down_kernel(place, a0, a1, a2, a3, w_own, w_alien, out, act, w, sems):
    hid = w_own.shape[0]
    loads = [
        pltpu.make_async_copy(v, w.at[pl.ds(n * hid, hid)], sems.at[n])
        for n, v in enumerate((w_own, w_alien))
    ]
    for load in loads:
        load.start()
    x = place[3]
    rows = a0.shape[0]
    for n, a in enumerate((a0, a1, a2, a3)):
        act[n * rows : (n + 1) * rows] = a[...]
    for load in loads:
        load.wait()
    total = dot(act[...], w[...]).astype(BF16)
    part = rows // NY
    for n in range(NX):
        for b in range(NY):
            start = n * rows + b * part
            out[b, (x + n) & 3] = total[start : start + part]


def down(place, blocks, weights):
    rows = blocks[0].shape[0]
    hid, width = weights[0].shape
    return pl.pallas_call(
        down_kernel,
        out_shape=jax.ShapeDtypeStruct((NY, NX, rows // NY, width), BF16),
        in_specs=[SMEM] + [VMEM] * NX + [HBM] * NC,
        out_specs=VMEM,
        scratch_shapes=[
            pltpu.VMEM((NX * rows, NC * hid), BF16),
            pltpu.VMEM((NC * hid, width), BF16),
            pltpu.SemaphoreType.DMA((NC,)),
        ],
        compiler_params=SMALL,
        name="down",
    )(place, *blocks, *weights)


def sum_y_kernel(parts, out):
    total = parts[0].astype(F32)
    for n in range(1, NY):
        total = total + parts[n].astype(F32)

    def source(i):
        return (
            (lax.shift_right_logical(i, 1) & 3) * 16 + lax.shift_right_logical(i, 3) * 2 + (i & 1)
        )

    out[...] = dot(moved(out.shape[0], source), total.astype(BF16)).astype(BF16)


def sum_y(parts):
    return pl.pallas_call(
        sum_y_kernel,
        out_shape=jax.ShapeDtypeStruct(parts.shape[1:], BF16),
        in_specs=[VMEM],
        out_specs=VMEM,
        compiler_params=SMALL,
        name="sum_y",
    )(parts)


def on_device(
    queries, new_entries, cache, lengths, hidden, w_uv, w_o, ffn_gain, w_gate, w_up, w_down
):
    y, z, c, x = (lax.axis_index(a) for a in ("y", "z", "c", "x"))
    place = jnp.stack([y, z, c, x]).astype(jnp.int32)
    rolls, steps = queries.shape[:2]
    pair = NC * w_o.shape[1]
    width, hid = w_gate.shape
    cache = cache.transpose(0, 2, 1)
    hidden = hidden.transpose(1, 2, 0).reshape(-1, hidden.shape[0])
    w_o, w_gate, w_up = w_o.T, w_gate.T, w_up.T

    def other(v):
        return lax.ppermute(v, "c", shift(NC, 1))

    def cross(v, k):
        return lax.ppermute(
            v, ("y", "x"), [(b * NX + a, ((a + k) % NX) * NX + b) for b in range(NY) for a in range(NX)]
        )

    with jax.named_scope("attend"):
        w_o_alien, hidden_alien = other(w_o), other(hidden)
        head_out = attend(queries, new_entries, cache, lengths, w_uv)
        head_out, w_o_alien, hidden_alien = lax.optimization_barrier(
            (head_out, w_o_alien, hidden_alien)
        )

    with jax.named_scope("gather_heads"):
        near = jnp.concatenate(fetch(head_out, "y", NY), axis=0)
        pieces, swapped = ring(near, c, (w_gate, w_up, w_down), other)
        w_gate_alien, w_up_alien, w_down_alien = swapped

    with jax.named_scope("project"):
        parts = project(place, pieces, (w_o, w_o_alien), (hidden, hidden_alien))

    with jax.named_scope("sum_heads"):
        total = 0.0
        for k in range(NX):
            total = total + cross(parts[k], k).astype(F32)
        resid = total.astype(BF16)

    with jax.named_scope("gather_resid"):
        resid = lax.all_to_all(jnp.broadcast_to(resid[None], (NZ,) + resid.shape), "z", 0, 0)
        resid = lax.all_gather(resid, "y")

    with jax.named_scope("gate_up"):
        gain = lax.dynamic_slice_in_dim(ffn_gain, x * width, width, 0).astype(F32)
        messages = gate_up(
            place, gain.reshape(NZ, pair), resid, (w_gate, w_up, w_gate_alien, w_up_alien)
        )

    with jax.named_scope("sum_gate_up"):
        messages = [messages[0]] + [
            lax.ppermute(messages[k], "x", shift(NX, k)) for k in range(1, NX)
        ]
        act = activate(messages, NX * width, hid)

    with jax.named_scope("down"):
        out = down(place, fetch(act, "x", NX), (w_down, w_down_alien))

    with jax.named_scope("sum_y"):
        out = lax.all_to_all(out.reshape(NY, -1, width), "y", 0, 0)
        out = sum_y(out)

    with jax.named_scope("sum_z"):
        out = lax.all_to_all(out.reshape(NZ, rolls * steps, width), "z", 0, 0)
        out = jnp.sum(out.astype(F32), axis=0)

    with jax.named_scope("finish"):
        own = lax.dynamic_slice_in_dim(resid, (y * NZ + z) * steps, steps, 2)
        own = own.transpose(0, 2, 1, 3).reshape(rolls * steps, width)
        out = (own.astype(F32) + out).astype(BF16)
    return out.reshape(rolls, steps, width)


def solution(mesh):
    fine = Mesh(mesh.devices.reshape(NY, NZ, NC, NX), ("y", "z", "c", "x"))
    dp = ("y", "z", "c")
    placed = (
        P(dp, None, "x", None),
        P(dp, None, None),
        P(dp, None, None),
        P(dp),
        P(None, None, dp),
        P("x", None, None),
        P("x", dp),
        P(),
        P("x", dp),
        P("x", dp),
        P(dp, "x"),
    )
    return jax.shard_map(
        on_device, mesh=fine, in_specs=placed, out_specs=P(dp, None, "x"), check_vma=False
    )
```

time: 455 us -> 163 us (0.36)
  waiting for transfers between devices: 398 us -> 57.9 us
  starting transfers between devices: 0.17 us -> 45.8 us
  blocking collectives: 0 us -> 28.3 us
  matrix products: 23.7 us -> 0 us
  Pallas kernels: 0 us -> 21.6 us
  between operations: 13.3 us -> 0.23 us
  other arithmetic: 15.7 us -> 3.78 us
    all_gather x2 -> x0, waiting for transfers between devices: 167 us -> none  [the longest x1 85.1 us: on_device(): whole = lax.all_gather(resid, 'dp', axis=1, tiled=True)]
    reduce_scatter x1 -> x0, waiting for transfers between devices: 144 us -> none  [on_device(): lax.psum_scatter(jnp.dot(act, w_down, preferred_element_type=jnp.float32)...]
    psum x2 -> x0, waiting for transfers between devices: 87.2 us -> none  [the longest x1 44.5 us: on_device(): lax.psum(up_part.astype(jnp.bfloat16), 'head').astype(jnp.float32)]
    ppermute x0 -> x25, waiting for transfers between devices: none -> 39.9 us  [the longest x3 13.3 us: ring(): up = lax.ppermute(up, 'z', shift(NZ, 1))]
    ppermute x0 -> x25, starting transfers between devices: none -> 36.8 us  [the longest x3 10.5 us: ring(): down = lax.ppermute(down, 'z', shift(NZ, -1))]
    pallas_call x0 -> x6, Pallas kernels: none -> 21.6 us  [the longest x1 7.54 us: attend(): pl.pallas_call(lambda *refs: attend_kernel((NOPE + ROPE) ** (-0.5), *refs...]
    dot_general x8 -> x0, matrix products: 19.7 us -> none  [the longest x1 4.37 us: on_device(): jnp.dot(lax.all_gather(head_out, 'dp', axis=0, tiled=True), w_o, preferre...]
    all_to_all x0 -> x2, waiting for transfers between devices: none -> 18 us  [the longest x1 9.04 us: on_device(): lax.all_to_all(jnp.broadcast_to(resid[None], (NZ,) + resid.shape), 'z', 0...]
  transfers between devices with their start and end apart: 5 -> 27, of which waited for: 5 -> 16; matrix products, arithmetic and copies ran while one was open for 0% -> 3% of each run, Pallas kernels for 0% -> 5%
where the time goes in v1:
time: 163 us; the launch traced here: 161 us
  waiting for transfers between devices  57.9 us (36%)
  starting transfers between devices  45.8 us (28%)
  blocking collectives  28.3 us (17%)
  Pallas kernels  21.6 us (13%)
  other arithmetic  3.78 us (2%)
  local copies, waits for them, and re-layouts  3.41 us (2%)
    all_gather x1, blocking collectives, on_device(): resid = lax.all_gather(resid, 'y')  15.5 us
    ppermute x3, waiting for transfers between devices, ring(): up = lax.ppermute(up, 'z', shift(NZ, 1))  13.3 us
    all_to_all x1, blocking collectives, on_device(): out = lax.all_to_all(out.reshape(NY, -1, width), 'y', 0, 0)  12.9 us
    ppermute x3, starting transfers between devices, ring(): down = lax.ppermute(down, 'z', shift(NZ, -1))  10.5 us
    ppermute x6, starting transfers between devices, fetch(): return [v] + [lax.ppermute(v, axis, shift(n, -k)) for k in range(1, n)]  9.67 us
    ppermute x4, starting transfers between devices, cross(): lax.ppermute(v, ('y', 'x'), [(b * NX + a, (a + k) % NX * NX + b) for b in...  9.09 us
    all_to_all x1, waiting for transfers between devices, on_device(): lax.all_to_all(jnp.broadcast_to(resid[None], (NZ,) + resid.shape), 'z', 0...  9.04 us
    all_to_all x1, waiting for transfers between devices, on_device(): out = lax.all_to_all(out.reshape(NZ, rolls * steps, width), 'z', 0, 0)  8.95 us
  transfers between devices with their start and end apart: 27, of which 16 were waited for; matrix products, arithmetic and copies ran while one was open for 3% of the time, Pallas kernels for 5%

profile of v1, /device:TPU:2, one launch (start us, length us, event | category | flops | bytes accessed | tf_op | source)
XLA Modules:
  0.0 161.0 jit_solution(8505536053200045166)
XLA Ops:
  0.0 0.0 collective-permute-start
  0.0 0.5 collective-permute-start.1
  0.5 7.5 %attend.1 = bf16[8,4096]{1,0:T(8,128)(2,1)} custom-call(s32[4]{0:T(128)} %refs_0_.1, bf16[4,2,32,576]{3,2,1,0:T(8,128)(2,1)} %refs_1_.1, bf16[4,2,576]{2,1,0:T(2,128)(2,1)} %refs_2_.1, bf16[4,576,1024]{2,1,0:T(8,128)(2,1)} %bitcast.19, bf16[32,512,128]{2,1,0:T(8,128)(2,1)} %refs_4_.1), custom_call_target="tpu_custom_call" | custom-call | tf_op jit(solution)/shard_map/attend/attend/pallas_call | solution.py:104
  8.1 0.0 collective-permute-done.1.refs_12_
  8.1 0.0 collective-permute-done.refs_10_
  8.1 3.1 %collective-permute-start.2 = (bf16[8,4096]{1,0:T(8,128)(2,1)}, bf16[8,4096]{1,0:T(8,128)(2,1)S(1)}, u32[]{:S(2)}, u32[]{:S(2)}) collective-permute-start(bf16[8,4096]{1,0:T(8,128)(2,1)} %attend.1), channel_id=1, source_target_pairs={{0,192},{64,0},{128,64},{192,128},{1,193},{65,1},{129,65},{193,129... | collective-permute-start | bytes 196616 | tf_op jit(solution)/shard_map/gather_heads/ppermute | solution.py:35
  11.2 0.9 constant_dynamic-update-slice_fusion.3
  12.1 0.6 collective-permute-start.3
  12.7 1.0 collective-permute-start.4
  13.7 4.6 %collective-permute-done.3 = bf16[8,4096]{1,0:T(8,128)(2,1)S(1)} collective-permute-done((bf16[8,4096]{1,0:T(8,128)(2,1)}, bf16[8,4096]{1,0:T(8,128)(2,1)S(1)}, u32[]{:S(2)}, u32[]{:S(2)}) %collective-permute-start.3) | collective-permute-done | bytes 65568 | tf_op jit(solution)/shard_map/gather_heads/ppermute | solution.py:35
  18.3 0.6 collective-permute-done.4
  18.9 2.0 %collective-permute-start.8 = (bf16[32,4096]{1,0:T(8,128)(2,1)S(1)}, bf16[32,4096]{1,0:T(8,128)(2,1)S(1)}, u32[]{:S(2)}, u32[]{:S(2)}) collective-permute-start(bf16[32,4096]{1,0:T(8,128)(2,1)S(1)} %constant_dynamic-update-slice_fusion.refs_1_), channel_id=1, source_target_pairs={{0,8},{8,16},{16,24},{24,32},{32,40},{40,48},{48,56},{56,0},{1,9},... | collective-permute-start | bytes 786440 | tf_op jit(solution)/shard_map/gather_heads/ppermute | solution.py:43
  20.9 4.0 %collective-permute-start.5 = (bf16[32,4096]{1,0:T(8,128)(2,1)S(1)}, bf16[32,4096]{1,0:T(8,128)(2,1)S(1)}, u32[]{:S(2)}, u32[]{:S(2)}) collective-permute-start(bf16[32,4096]{1,0:T(8,128)(2,1)S(1)} %constant_dynamic-update-slice_fusion.refs_1_), channel_id=1, source_target_pairs={{0,56},{8,0},{16,8},{24,16},{32,24},{40,32},{48,40},{56,48},{1,57}... | collective-permute-start | bytes 786440 | tf_op jit(solution)/shard_map/gather_heads/ppermute | solution.py:44
  24.9 5.2 %collective-permute-done.8.refs_8_ = bf16[32,4096]{1,0:T(8,128)(2,1)S(1)} collective-permute-done((bf16[32,4096]{1,0:T(8,128)(2,1)S(1)}, bf16[32,4096]{1,0:T(8,128)(2,1)S(1)}, u32[]{:S(2)}, u32[]{:S(2)}) %collective-permute-start.8) | collective-permute-done | bytes 262176 | tf_op jit(solution)/shard_map/gather_heads/ppermute | solution.py:43
  30.2 3.2 %collective-permute-start.6 = (bf16[32,4096]{1,0:T(8,128)(2,1)S(1)}, bf16[32,4096]{1,0:T(8,128)(2,1)}, u32[]{:S(2)}, u32[]{:S(2)}) collective-permute-start(bf16[32,4096]{1,0:T(8,128)(2,1)S(1)} %collective-permute-done.5.refs_2_), channel_id=1, source_target_pairs={{0,56},{8,0},{16,8},{24,16},{32,24},{40,32},{48,40},{56,48},{1,57}... | collective-permute-start | bytes 786440 | tf_op jit(solution)/shard_map/gather_heads/ppermute | solution.py:44
  33.4 4.4 %collective-permute-done.9.refs_7_ = bf16[32,4096]{1,0:T(8,128)(2,1)S(1)} collective-permute-done((bf16[32,4096]{1,0:T(8,128)(2,1)S(1)}, bf16[32,4096]{1,0:T(8,128)(2,1)S(1)}, u32[]{:S(2)}, u32[]{:S(2)}) %collective-permute-start.9) | collective-permute-done | bytes 262176 | tf_op jit(solution)/shard_map/gather_heads/ppermute | solution.py:43
  37.8 0.0 collective-permute-start.10
  37.8 0.0 collective-permute-done.6.refs_3_
  37.8 3.3 %collective-permute-start.7 = (bf16[32,4096]{1,0:T(8,128)(2,1)}, bf16[32,4096]{1,0:T(8,128)(2,1)S(1)}, u32[]{:S(2)}, u32[]{:S(2)}) collective-permute-start(bf16[32,4096]{1,0:T(8,128)(2,1)} %collective-permute-done.6.refs_3_), channel_id=1, source_target_pairs={{0,56},{8,0},{16,8},{24,16},{32,24},{40,32},{48,40},{56,48},{1,57}... | collective-permute-start | bytes 786440 | tf_op jit(solution)/shard_map/gather_heads/ppermute | solution.py:44
  41.1 0.0 collective-permute-start.12
  41.1 0.5 collective-permute-start.13
  41.6 3.7 %collective-permute-done.10.refs_6_ = bf16[32,4096]{1,0:T(8,128)(2,1)S(1)} collective-permute-done((bf16[32,4096]{1,0:T(8,128)(2,1)S(1)}, bf16[32,4096]{1,0:T(8,128)(2,1)S(1)}, u32[]{:S(2)}, u32[]{:S(2)}) %collective-permute-start.10) | collective-permute-done | bytes 262176 | tf_op jit(solution)/shard_map/gather_heads/ppermute | solution.py:43
  45.4 0.0 collective-permute-start.14
  45.4 0.0 collective-permute-done.7.refs_4_
  45.4 0.8 broadcast_select_fusion
  46.2 0.0 collective-permute-start.11
  46.2 0.6 pad_add_fusion.refs_0_.place
  46.8 7.6 %collective-permute-done.11.refs_5_ = bf16[32,4096]{1,0:T(8,128)(2,1)} collective-permute-done((bf16[32,4096]{1,0:T(8,128)(2,1)}, bf16[32,4096]{1,0:T(8,128)(2,1)}, u32[]{:S(2)}, u32[]{:S(2)}) %collective-permute-start.11) | collective-permute-done | bytes 262176 | tf_op jit(solution)/shard_map/gather_heads/ppermute | solution.py:52
  54.4 0.0 collective-permute-done.12.w2
  54.4 4.7 %project.1 = (bf16[64,224]{1,0:T(8,128)(2,1)}, bf16[64,224]{1,0:T(8,128)(2,1)}, bf16[64,224]{1,0:T(8,128)(2,1)}, bf16[64,224]{1,0:T(8,128)(2,1)}) custom-call(s32[4]{0:T(128)} %pad_add_fusion.refs_0_.place, bf16[32,4096]{1,0:T(8,128)(2,1)} %copy-done.6, bf16[32,4096]{1,0:T(8,128)(2,1)} %copy-done.8, bf16[32,4096]{1,0:T(8,128)(2,1)} %collective-permute-done.6.refs_3_, ...), custom_call_target="tpu_custom_call" | custom-call | tf_op jit(solution)/shard_map/project/project/pallas_call | solution.py:176
  59.1 1.9 %collective-permute-start.15 = (bf16[64,224]{1,0:T(8,128)(2,1)}, bf16[64,224]{1,0:T(8,128)(2,1)S(1)}, u32[]{:S(2)}, u32[]{:S(2)}) collective-permute-start(bf16[64,224]{1,0:T(8,128)(2,1)} %get-tuple-element.30), channel_id=1, source_target_pairs={{0,0},{1,64},{2,128},{3,192},{64,1},{65,65},{66,129},{67,193},{128... | collective-permute-start | bytes 86024 | tf_op jit(solution)/shard_map/sum_heads/ppermute | solution.py:340
  61.1 6.0 %collective-permute-start.16 = (bf16[64,224]{1,0:T(8,128)(2,1)}, bf16[64,224]{1,0:T(8,128)(2,1)S(1)}, u32[]{:S(2)}, u32[]{:S(2)}) collective-permute-start(bf16[64,224]{1,0:T(8,128)(2,1)} %get-tuple-element.31), channel_id=1, source_target_pairs={{0,64},{1,128},{2,192},{3,0},{64,65},{65,129},{66,193},{67,1},{128... | collective-permute-start | bytes 86024 | tf_op jit(solution)/shard_map/sum_heads/ppermute | solution.py:340
  67.1 1.1 collective-permute-start.17
  68.2 0.8 collective-permute-done.16
  69.0 3.1 %collective-permute-done.17 = bf16[64,224]{1,0:T(8,128)(2,1)S(1)} collective-permute-done((bf16[64,224]{1,0:T(8,128)(2,1)}, bf16[64,224]{1,0:T(8,128)(2,1)S(1)}, u32[]{:S(2)}, u32[]{:S(2)}) %collective-permute-start.17) | collective-permute-done | bytes 28704 | tf_op jit(solution)/shard_map/sum_heads/ppermute | solution.py:340
  72.1 0.3 collective-permute-done.18
  72.5 0.7 broadcast_in_dim.2
  73.2 5.5 %all-to-all-start = ((bf16[8,64,224]{2,1,0:T(8,128)(2,1)}), bf16[8,64,224]{2,1,0:T(8,128)(2,1)S(1)}, u32[]{:S(2)}, u32[]{:S(2)}) async-start(bf16[8,64,224]{2,1,0:T(8,128)(2,1)} %broadcast_in_dim.2), calls=%async_computation | async-start | bytes 524288 | tf_op jit(solution)/shard_map/gather_resid/all_to_all | solution.py:366
  78.7 0.8 dynamic-slice_convert_fusion
  79.5 0.7 reshape.28.gain
  80.2 9.0 %all-to-all-done = bf16[8,64,224]{2,1,0:T(8,128)(2,1)S(1)} async-done(((bf16[8,64,224]{2,1,0:T(8,128)(2,1)}), bf16[8,64,224]{2,1,0:T(8,128)(2,1)S(1)}, u32[]{:S(2)}, u32[]{:S(2)}) %all-to-all-start) | async-done | bytes 229408 | tf_op jit(solution)/shard_map/gather_resid/all_to_all | solution.py:366
  89.2 15.5 %all-gather = bf16[32,64,224]{2,1,0:T(8,128)(2,1)} all-gather(bf16[8,64,224]{2,1,0:T(8,128)(2,1)S(1)} %all-to-all-done), channel_id=2, replica_groups=mesh['y'=4,'z'=8,'c'=2,'x'=4] {'y'}, dimensions={0}, use_global_device_ids=true | all-gather | bytes 1146880 | tf_op jit(solution)/shard_map/gather_resid/all_gather | solution.py:367
  104.7 6.0 %gate_up.1 = (bf16[64,1280]{1,0:T(8,128)(2,1)}, bf16[64,1280]{1,0:T(8,128)(2,1)}, bf16[64,1280]{1,0:T(8,128)(2,1)}, bf16[64,1280]{1,0:T(8,128)(2,1)}) custom-call(s32[4]{0:T(128)} %pad_add_fusion.refs_0_.place, f32[8,224]{1,0:T(8,128)} %reshape.28.gain, bf16[4,8,64,224]{3,2,1,0:T(8,128)(2,1)} %bitcast.20, bf16[288,1792]{1,0:T(8,128)(2,1)} %bitcast.8.w0, ...), custom_call_target="tpu_custom_call" | custom-call | tf_op jit(solution)/shard_map/gate_up/gate_up/pallas_call | solution.py:223
  110.7 2.3 %collective-permute-start.19 = (bf16[64,1280]{1,0:T(8,128)(2,1)}, bf16[64,1280]{1,0:T(8,128)(2,1)S(1)}, u32[]{:S(2)}, u32[]{:S(2)}) collective-permute-start(bf16[64,1280]{1,0:T(8,128)(2,1)} %get-tuple-element.37), channel_id=1, source_target_pairs={{0,1},{1,2},{2,3},{3,0},{4,5},{5,6},{6,7},{7,4},{8,9},{9,10},{10,1... | collective-permute-start | bytes 491528 | tf_op jit(solution)/shard_map/sum_gate_up/ppermute | solution.py:377
  113.0 1.2 collective-permute-start.20
  114.2 1.0 collective-permute-start.21
  115.1 1.1 collective-permute-done.19.refs_1_
  116.3 4.2 %collective-permute-done.20.refs_2_ = bf16[64,1280]{1,0:T(8,128)(2,1)S(1)} collective-permute-done((bf16[64,1280]{1,0:T(8,128)(2,1)}, bf16[64,1280]{1,0:T(8,128)(2,1)S(1)}, u32[]{:S(2)}, u32[]{:S(2)}) %collective-permute-start.20) | collective-permute-done | bytes 163872 | tf_op jit(solution)/shard_map/sum_gate_up/ppermute | solution.py:377
  120.5 1.7 %collective-permute-done.21.refs_3_ = bf16[64,1280]{1,0:T(8,128)(2,1)S(1)} collective-permute-done((bf16[64,1280]{1,0:T(8,128)(2,1)}, bf16[64,1280]{1,0:T(8,128)(2,1)S(1)}, u32[]{:S(2)}, u32[]{:S(2)}) %collective-permute-start.21) | collective-permute-done | bytes 163872 | tf_op jit(solution)/shard_map/sum_gate_up/ppermute | solution.py:377
  122.2 0.9 copy-done.1
  123.1 0.2 activate.1.a0
  123.3 0.3 collective-permute-start.22
  123.6 2.2 %collective-permute-start.23 = (bf16[64,576]{1,0:T(8,128)(2,1)S(1)}, bf16[64,576]{1,0:T(8,128)(2,1)S(1)}, u32[]{:S(2)}, u32[]{:S(2)}) collective-permute-start(bf16[64,576]{1,0:T(8,128)(2,1)S(1)} %activate.1.a0), channel_id=1, source_target_pairs={{0,2},{1,3},{2,0},{3,1},{4,6},{5,7},{6,4},{7,5},{8,10},{9,11},{10,... | collective-permute-start | bytes 221192 | tf_op jit(solution)/shard_map/down/ppermute | solution.py:35
  125.8 2.5 %collective-permute-start.24 = (bf16[64,576]{1,0:T(8,128)(2,1)S(1)}, bf16[64,576]{1,0:T(8,128)(2,1)S(1)}, u32[]{:S(2)}, u32[]{:S(2)}) collective-permute-start(bf16[64,576]{1,0:T(8,128)(2,1)S(1)} %activate.1.a0), channel_id=1, source_target_pairs={{0,1},{1,2},{2,3},{3,0},{4,5},{5,6},{6,7},{7,4},{8,9},{9,10},{10,1... | collective-permute-start | bytes 221192 | tf_op jit(solution)/shard_map/down/ppermute | solution.py:35
  128.3 1.2 collective-permute-done.23.a2
  129.6 1.2 collective-permute-done.24.a3
  130.8 2.2 %down.1 = bf16[4,4,16,1792]{3,2,1,0:T(8,128)(2,1)S(1)} custom-call(s32[4]{0:T(128)S(1)} %copy-done.2, bf16[64,576]{1,0:T(8,128)(2,1)S(1)} %activate.1.a0, bf16[64,576]{1,0:T(8,128)(2,1)S(1)} %collective-permute-done.22.a1, bf16[64,576]{1,0:T(8,128)(2,1)S(1)} %collective-permute-done.23.a2, bf16[64,576]{1,0:T(8,128)(2,1)S(1)} %collective-permute-done.24.a3, ...), custom_call_target="tpu_custom_call" | custom-call | tf_op jit(solution)/shard_map/down/down/pallas_call | solution.py:285
  133.0 12.9 %all_to_all.15.parts = bf16[4,64,1792]{2,1,0:T(8,128)(2,1)S(1)} all-to-all(bf16[4,64,1792]{2,1,0:T(8,128)(2,1)S(1)} %bitcast.18), channel_id=1, replica_groups=mesh['y'=4,'z'=8,'c'=2,'x'=4] {'y'}, dimensions={0} | all-to-all | bytes 1835008 | tf_op jit(solution)/shard_map/sum_y/all_to_all | solution.py:385
  145.9 1.0 sum_y.1
  146.9 3.4 %all-to-all-start.2 = ((bf16[8,8,1792]{2,1,0:T(8,128)(2,1)}), bf16[8,8,1792]{2,1,0:T(8,128)(2,1)S(1)}, u32[]{:S(2)}, u32[]{:S(2)}) async-start(bf16[8,8,1792]{2,1,0:T(8,128)(2,1)} %bitcast.13), calls=%async_computation.2 | async-start | bytes 458752 | tf_op jit(solution)/shard_map/sum_z/all_to_all | solution.py:389
  150.3 0.9 convert_bitcast_fusion
  151.2 0.1 reshape.26
  151.4 8.9 %all-to-all-done.2 = bf16[8,8,1792]{2,1,0:T(8,128)(2,1)S(1)} async-done(((bf16[8,8,1792]{2,1,0:T(8,128)(2,1)}), bf16[8,8,1792]{2,1,0:T(8,128)(2,1)S(1)}, u32[]{:S(2)}, u32[]{:S(2)}) %all-to-all-start.2) | async-done | bytes 229408 | tf_op jit(solution)/shard_map/sum_z/all_to_all | solution.py:389
  160.4 0.6 add_convert_fusion.1
  (36 shorter events, 0.2 us)
Async XLA Ops:
  0.0 8.1 %collective-permute-start = (bf16[112,4096]{1,0:T(8,128)(2,1)}, bf16[112,4096]{1,0:T(8,128)(2,1)S(1)}, u32[]{:S(2)}, u32[]{:S(2)}) collective-permute-start(bf16[112,4096]{1,0:T(8,128)(2,1)} %bitcast.22), channel_id=1, source_target_pairs={{0,4},{4,0},{1,5},{5,1},{2,6},{6,2},{3,7},{7,3},{8,12},{12,8},{9,1... | collective-permute-start | bytes 2752520 | tf_op jit(solution)/shard_map/attend/ppermute | solution.py:337
  0.0 8.1 %collective-permute-start.1 = (bf16[224,256]{1,0:T(8,128)(2,1)}, bf16[224,256]{1,0:T(8,128)(2,1)S(1)}, u32[]{:S(2)}, u32[]{:S(2)}) collective-permute-start(bf16[224,256]{1,0:T(8,128)(2,1)} %bitcast.24), channel_id=1, source_target_pairs={{0,4},{4,0},{1,5},{5,1},{2,6},{6,2},{3,7},{7,3},{8,12},{12,8},{9,1... | collective-permute-start | bytes 344072 | tf_op jit(solution)/shard_map/attend/ppermute | solution.py:337
  0.5 44.9 %copy-start = (bf16[288,1792]{1,0:T(8,128)(2,1)S(1)}, bf16[288,1792]{1,0:T(8,128)(2,1)}, u32[]{:S(2)}) copy-start(bf16[288,1792]{1,0:T(8,128)(2,1)} %w_own.1) | copy-start | bytes 3096580
  8.1 29.7 %copy-start.10 = (bf16[224,256]{1,0:T(8,128)(2,1)}, bf16[224,256]{1,0:T(8,128)(2,1)S(1)}, u32[]{:S(2)}) copy-start(bf16[224,256]{1,0:T(8,128)(2,1)S(1)} %collective-permute-done.1.refs_12_) | copy-start | bytes 344068
  8.1 46.3 %copy-start.5 = (bf16[112,4096]{1,0:T(8,128)(2,1)}, bf16[112,4096]{1,0:T(8,128)(2,1)S(1)}, u32[]{:S(2)}) copy-start(bf16[112,4096]{1,0:T(8,128)(2,1)S(1)} %collective-permute-done.refs_10_) | copy-start | bytes 2752516
  8.1 5.6 %collective-permute-start.2 = (bf16[8,4096]{1,0:T(8,128)(2,1)}, bf16[8,4096]{1,0:T(8,128)(2,1)S(1)}, u32[]{:S(2)}, u32[]{:S(2)}) collective-permute-start(bf16[8,4096]{1,0:T(8,128)(2,1)} %attend.1), channel_id=1, source_target_pairs={{0,192},{64,0},{128,64},{192,128},{1,193},{65,1},{129,65},{193,129... | collective-permute-start | bytes 196616 | tf_op jit(solution)/shard_map/gather_heads/ppermute | solution.py:35
  12.1 6.2 %collective-permute-start.3 = (bf16[8,4096]{1,0:T(8,128)(2,1)}, bf16[8,4096]{1,0:T(8,128)(2,1)S(1)}, u32[]{:S(2)}, u32[]{:S(2)}) collective-permute-start(bf16[8,4096]{1,0:T(8,128)(2,1)} %attend.1), channel_id=1, source_target_pairs={{0,128},{64,192},{128,0},{192,64},{1,129},{65,193},{129,1},{193,65... | collective-permute-start | bytes 196616 | tf_op jit(solution)/shard_map/gather_heads/ppermute | solution.py:35
  12.7 6.2 %collective-permute-start.4 = (bf16[8,4096]{1,0:T(8,128)(2,1)}, bf16[8,4096]{1,0:T(8,128)(2,1)S(1)}, u32[]{:S(2)}, u32[]{:S(2)}) collective-permute-start(bf16[8,4096]{1,0:T(8,128)(2,1)} %attend.1), channel_id=1, source_target_pairs={{0,64},{64,128},{128,192},{192,0},{1,65},{65,129},{129,193},{193,1... | collective-permute-start | bytes 196616 | tf_op jit(solution)/shard_map/gather_heads/ppermute | solution.py:35
  18.9 22.7 %copy-start.6 = (bf16[32,4096]{1,0:T(8,128)(2,1)}, bf16[32,4096]{1,0:T(8,128)(2,1)S(1)}, u32[]{:S(2)}) copy-start(bf16[32,4096]{1,0:T(8,128)(2,1)S(1)} %constant_dynamic-update-slice_fusion.refs_1_) | copy-start | bytes 786436
  18.9 11.2 %collective-permute-start.8 = (bf16[32,4096]{1,0:T(8,128)(2,1)S(1)}, bf16[32,4096]{1,0:T(8,128)(2,1)S(1)}, u32[]{:S(2)}, u32[]{:S(2)}) collective-permute-start(bf16[32,4096]{1,0:T(8,128)(2,1)S(1)} %constant_dynamic-update-slice_fusion.refs_1_), channel_id=1, source_target_pairs={{0,8},{8,16},{16,24},{24,32},{32,40},{40,48},{48,56},{56,0},{1,9},... | collective-permute-start | bytes 786440 | tf_op jit(solution)/shard_map/gather_heads/ppermute | solution.py:43
  20.9 9.3 %collective-permute-start.5 = (bf16[32,4096]{1,0:T(8,128)(2,1)S(1)}, bf16[32,4096]{1,0:T(8,128)(2,1)S(1)}, u32[]{:S(2)}, u32[]{:S(2)}) collective-permute-start(bf16[32,4096]{1,0:T(8,128)(2,1)S(1)} %constant_dynamic-update-slice_fusion.refs_1_), channel_id=1, source_target_pairs={{0,56},{8,0},{16,8},{24,16},{32,24},{40,32},{48,40},{56,48},{1,57}... | collective-permute-start | bytes 786440 | tf_op jit(solution)/shard_map/gather_heads/ppermute | solution.py:44
  30.2 11.5 %copy-start.7 = (bf16[32,4096]{1,0:T(8,128)(2,1)}, bf16[32,4096]{1,0:T(8,128)(2,1)S(1)}, u32[]{:S(2)}) copy-start(bf16[32,4096]{1,0:T(8,128)(2,1)S(1)} %collective-permute-done.8.refs_8_) | copy-start | bytes 786436
  30.2 7.6 %collective-permute-start.9 = (bf16[32,4096]{1,0:T(8,128)(2,1)S(1)}, bf16[32,4096]{1,0:T(8,128)(2,1)S(1)}, u32[]{:S(2)}, u32[]{:S(2)}) collective-permute-start(bf16[32,4096]{1,0:T(8,128)(2,1)S(1)} %collective-permute-done.8.refs_8_), channel_id=1, source_target_pairs={{0,8},{8,16},{16,24},{24,32},{32,40},{40,48},{48,56},{56,0},{1,9},... | collective-permute-start | bytes 786440 | tf_op jit(solution)/shard_map/gather_heads/ppermute | solution.py:43
  30.2 7.6 %copy-start.8 = (bf16[32,4096]{1,0:T(8,128)(2,1)}, bf16[32,4096]{1,0:T(8,128)(2,1)S(1)}, u32[]{:S(2)}) copy-start(bf16[32,4096]{1,0:T(8,128)(2,1)S(1)} %collective-permute-done.5.refs_2_) | copy-start | bytes 786436
  30.2 7.6 %collective-permute-start.6 = (bf16[32,4096]{1,0:T(8,128)(2,1)S(1)}, bf16[32,4096]{1,0:T(8,128)(2,1)}, u32[]{:S(2)}, u32[]{:S(2)}) collective-permute-start(bf16[32,4096]{1,0:T(8,128)(2,1)S(1)} %collective-permute-done.5.refs_2_), channel_id=1, source_target_pairs={{0,56},{8,0},{16,8},{24,16},{32,24},{40,32},{48,40},{56,48},{1,57}... | collective-permute-start | bytes 786440 | tf_op jit(solution)/shard_map/gather_heads/ppermute | solution.py:44
  37.8 3.8 %copy-start.9 = (bf16[32,4096]{1,0:T(8,128)(2,1)}, bf16[32,4096]{1,0:T(8,128)(2,1)S(1)}, u32[]{:S(2)}) copy-start(bf16[32,4096]{1,0:T(8,128)(2,1)S(1)} %collective-permute-done.9.refs_7_) | copy-start | bytes 786436
  37.8 7.6 %collective-permute-start.10 = (bf16[32,4096]{1,0:T(8,128)(2,1)S(1)}, bf16[32,4096]{1,0:T(8,128)(2,1)S(1)}, u32[]{:S(2)}, u32[]{:S(2)}) collective-permute-start(bf16[32,4096]{1,0:T(8,128)(2,1)S(1)} %collective-permute-done.9.refs_7_), channel_id=1, source_target_pairs={{0,8},{8,16},{16,24},{24,32},{32,40},{40,48},{48,56},{56,0},{1,9},... | collective-permute-start | bytes 786440 | tf_op jit(solution)/shard_map/gather_heads/ppermute | solution.py:43
  37.8 7.6 %collective-permute-start.7 = (bf16[32,4096]{1,0:T(8,128)(2,1)}, bf16[32,4096]{1,0:T(8,128)(2,1)S(1)}, u32[]{:S(2)}, u32[]{:S(2)}) collective-permute-start(bf16[32,4096]{1,0:T(8,128)(2,1)} %collective-permute-done.6.refs_3_), channel_id=1, source_target_pairs={{0,56},{8,0},{16,8},{24,16},{32,24},{40,32},{48,40},{56,48},{1,57}... | collective-permute-start | bytes 786440 | tf_op jit(solution)/shard_map/gather_heads/ppermute | solution.py:44
  41.1 13.2 %collective-permute-start.12 = (bf16[288,1792]{1,0:T(8,128)(2,1)}, bf16[288,1792]{1,0:T(8,128)(2,1)}, u32[]{:S(2)}, u32[]{:S(2)}) collective-permute-start(bf16[288,1792]{1,0:T(8,128)(2,1)} %bitcast.8.w0), channel_id=1, source_target_pairs={{0,4},{4,0},{1,5},{5,1},{2,6},{6,2},{3,7},{7,3},{8,12},{12,8},{9,1... | collective-permute-start | bytes 3096584 | tf_op jit(solution)/shard_map/gather_heads/ppermute | solution.py:337
  41.1 13.2 %collective-permute-start.13 = (bf16[288,1792]{1,0:T(8,128)(2,1)}, bf16[288,1792]{1,0:T(8,128)(2,1)}, u32[]{:S(2)}, u32[]{:S(2)}) collective-permute-start(bf16[288,1792]{1,0:T(8,128)(2,1)} %bitcast.9.w1), channel_id=1, source_target_pairs={{0,4},{4,0},{1,5},{5,1},{2,6},{6,2},{3,7},{7,3},{8,12},{12,8},{9,1... | collective-permute-start | bytes 3096584 | tf_op jit(solution)/shard_map/gather_heads/ppermute | solution.py:337
  45.4 9.0 %copy-start.3 = (bf16[32,4096]{1,0:T(8,128)(2,1)}, bf16[32,4096]{1,0:T(8,128)(2,1)S(1)}, u32[]{:S(2)}) copy-start(bf16[32,4096]{1,0:T(8,128)(2,1)S(1)} %collective-permute-done.10.refs_6_) | copy-start | bytes 786436
  45.4 9.0 %collective-permute-start.14 = (bf16[288,1792]{1,0:T(8,128)(2,1)S(1)}, bf16[288,1792]{1,0:T(8,128)(2,1)S(1)}, u32[]{:S(2)}, u32[]{:S(2)}) collective-permute-start(bf16[288,1792]{1,0:T(8,128)(2,1)S(1)} %copy-done), channel_id=1, source_target_pairs={{0,4},{4,0},{1,5},{5,1},{2,6},{6,2},{3,7},{7,3},{8,12},{12,8},{9,1... | collective-permute-start | bytes 3096584 | tf_op jit(solution)/shard_map/gather_heads/ppermute | solution.py:337
  45.4 9.0 %copy-start.4 = (bf16[32,4096]{1,0:T(8,128)(2,1)}, bf16[32,4096]{1,0:T(8,128)(2,1)S(1)}, u32[]{:S(2)}) copy-start(bf16[32,4096]{1,0:T(8,128)(2,1)S(1)} %collective-permute-done.7.refs_4_) | copy-start | bytes 786436
  46.2 8.2 %collective-permute-start.11 = (bf16[32,4096]{1,0:T(8,128)(2,1)}, bf16[32,4096]{1,0:T(8,128)(2,1)}, u32[]{:S(2)}, u32[]{:S(2)}) collective-permute-start(bf16[32,4096]{1,0:T(8,128)(2,1)} %broadcast_select_fusion), channel_id=1, source_target_pairs={{0,8},{4,60},{8,16},{12,4},{16,24},{20,12},{24,32},{28,20},{32,40}... | collective-permute-start | bytes 786440 | tf_op jit(solution)/shard_map/gather_heads/ppermute | solution.py:52
  59.1 71.7 %copy-start.2 = (s32[4]{0:T(128)S(1)}, s32[4]{0:T(128)}, u32[]{:S(2)}) copy-start(s32[4]{0:T(128)} %pad_add_fusion.refs_0_.place) | copy-start | bytes 52
  59.1 9.1 %collective-permute-start.15 = (bf16[64,224]{1,0:T(8,128)(2,1)}, bf16[64,224]{1,0:T(8,128)(2,1)S(1)}, u32[]{:S(2)}, u32[]{:S(2)}) collective-permute-start(bf16[64,224]{1,0:T(8,128)(2,1)} %get-tuple-element.30), channel_id=1, source_target_pairs={{0,0},{1,64},{2,128},{3,192},{64,1},{65,65},{66,129},{67,193},{128... | collective-permute-start | bytes 86024 | tf_op jit(solution)/shard_map/sum_heads/ppermute | solution.py:340
  61.1 7.9 %collective-permute-start.16 = (bf16[64,224]{1,0:T(8,128)(2,1)}, bf16[64,224]{1,0:T(8,128)(2,1)S(1)}, u32[]{:S(2)}, u32[]{:S(2)}) collective-permute-start(bf16[64,224]{1,0:T(8,128)(2,1)} %get-tuple-element.31), channel_id=1, source_target_pairs={{0,64},{1,128},{2,192},{3,0},{64,65},{65,129},{66,193},{67,1},{128... | collective-permute-start | bytes 86024 | tf_op jit(solution)/shard_map/sum_heads/ppermute | solution.py:340
  67.1 5.0 %collective-permute-start.17 = (bf16[64,224]{1,0:T(8,128)(2,1)}, bf16[64,224]{1,0:T(8,128)(2,1)S(1)}, u32[]{:S(2)}, u32[]{:S(2)}) collective-permute-start(bf16[64,224]{1,0:T(8,128)(2,1)} %get-tuple-element.32), channel_id=1, source_target_pairs={{0,128},{1,192},{2,0},{3,64},{64,129},{65,193},{66,1},{67,65},{128... | collective-permute-start | bytes 86024 | tf_op jit(solution)/shard_map/sum_heads/ppermute | solution.py:340
  68.2 4.2 %collective-permute-start.18 = (bf16[64,224]{1,0:T(8,128)(2,1)}, bf16[64,224]{1,0:T(8,128)(2,1)S(1)}, u32[]{:S(2)}, u32[]{:S(2)}) collective-permute-start(bf16[64,224]{1,0:T(8,128)(2,1)} %get-tuple-element.33), channel_id=1, source_target_pairs={{0,192},{1,0},{2,64},{3,128},{64,193},{65,1},{66,65},{67,129},{128... | collective-permute-start | bytes 86024 | tf_op jit(solution)/shard_map/sum_heads/ppermute | solution.py:340
  73.2 16.0 %all-to-all-start = ((bf16[8,64,224]{2,1,0:T(8,128)(2,1)}), bf16[8,64,224]{2,1,0:T(8,128)(2,1)S(1)}, u32[]{:S(2)}, u32[]{:S(2)}) async-start(bf16[8,64,224]{2,1,0:T(8,128)(2,1)} %broadcast_in_dim.2), calls=%async_computation | async-start | bytes 524288 | tf_op jit(solution)/shard_map/gather_resid/all_to_all | solution.py:366
  110.7 5.6 %collective-permute-start.19 = (bf16[64,1280]{1,0:T(8,128)(2,1)}, bf16[64,1280]{1,0:T(8,128)(2,1)S(1)}, u32[]{:S(2)}, u32[]{:S(2)}) collective-permute-start(bf16[64,1280]{1,0:T(8,128)(2,1)} %get-tuple-element.37), channel_id=1, source_target_pairs={{0,1},{1,2},{2,3},{3,0},{4,5},{5,6},{6,7},{7,4},{8,9},{9,10},{10,1... | collective-permute-start | bytes 491528 | tf_op jit(solution)/shard_map/sum_gate_up/ppermute | solution.py:377
  113.0 7.5 %collective-permute-start.20 = (bf16[64,1280]{1,0:T(8,128)(2,1)}, bf16[64,1280]{1,0:T(8,128)(2,1)S(1)}, u32[]{:S(2)}, u32[]{:S(2)}) collective-permute-start(bf16[64,1280]{1,0:T(8,128)(2,1)} %get-tuple-element.38), channel_id=1, source_target_pairs={{0,2},{1,3},{2,0},{3,1},{4,6},{5,7},{6,4},{7,5},{8,10},{9,11},{10,... | collective-permute-start | bytes 491528 | tf_op jit(solution)/shard_map/sum_gate_up/ppermute | solution.py:377
  114.2 8.0 %collective-permute-start.21 = (bf16[64,1280]{1,0:T(8,128)(2,1)}, bf16[64,1280]{1,0:T(8,128)(2,1)S(1)}, u32[]{:S(2)}, u32[]{:S(2)}) collective-permute-start(bf16[64,1280]{1,0:T(8,128)(2,1)} %get-tuple-element.39), channel_id=1, source_target_pairs={{0,3},{1,0},{2,1},{3,2},{4,7},{5,4},{6,5},{7,6},{8,11},{9,8},{10,9... | collective-permute-start | bytes 491528 | tf_op jit(solution)/shard_map/sum_gate_up/ppermute | solution.py:377
  122.2 0.9 copy-start.1
  123.3 5.0 %collective-permute-start.22 = (bf16[64,576]{1,0:T(8,128)(2,1)S(1)}, bf16[64,576]{1,0:T(8,128)(2,1)S(1)}, u32[]{:S(2)}, u32[]{:S(2)}) collective-permute-start(bf16[64,576]{1,0:T(8,128)(2,1)S(1)} %activate.1.a0), channel_id=1, source_target_pairs={{0,3},{1,0},{2,1},{3,2},{4,7},{5,4},{6,5},{7,6},{8,11},{9,8},{10,9... | collective-permute-start | bytes 221192 | tf_op jit(solution)/shard_map/down/ppermute | solution.py:35
  123.6 5.9 %collective-permute-start.23 = (bf16[64,576]{1,0:T(8,128)(2,1)S(1)}, bf16[64,576]{1,0:T(8,128)(2,1)S(1)}, u32[]{:S(2)}, u32[]{:S(2)}) collective-permute-start(bf16[64,576]{1,0:T(8,128)(2,1)S(1)} %activate.1.a0), channel_id=1, source_target_pairs={{0,2},{1,3},{2,0},{3,1},{4,6},{5,7},{6,4},{7,5},{8,10},{9,11},{10,... | collective-permute-start | bytes 221192 | tf_op jit(solution)/shard_map/down/ppermute | solution.py:35
  125.8 5.0 %collective-permute-start.24 = (bf16[64,576]{1,0:T(8,128)(2,1)S(1)}, bf16[64,576]{1,0:T(8,128)(2,1)S(1)}, u32[]{:S(2)}, u32[]{:S(2)}) collective-permute-start(bf16[64,576]{1,0:T(8,128)(2,1)S(1)} %activate.1.a0), channel_id=1, source_target_pairs={{0,1},{1,2},{2,3},{3,0},{4,5},{5,6},{6,7},{7,4},{8,9},{9,10},{10,1... | collective-permute-start | bytes 221192 | tf_op jit(solution)/shard_map/down/ppermute | solution.py:35
  146.9 13.4 %all-to-all-start.2 = ((bf16[8,8,1792]{2,1,0:T(8,128)(2,1)}), bf16[8,8,1792]{2,1,0:T(8,128)(2,1)S(1)}, u32[]{:S(2)}, u32[]{:S(2)}) async-start(bf16[8,8,1792]{2,1,0:T(8,128)(2,1)} %bitcast.13), calls=%async_computation.2 | async-start | bytes 458752 | tf_op jit(solution)/shard_map/sum_z/all_to_all | solution.py:389

commit v2 on v1

--- a/solution.py
+++ b/solution.py
@@ -15,7 +15,9 @@
 ANY = pl.BlockSpec(memory_space=pl.ANY)
 HBM = pl.BlockSpec(memory_space=pltpu.HBM)
 SMEM = pl.BlockSpec(memory_space=pltpu.SMEM)
-LARGE = pltpu.CompilerParams(vmem_limit_bytes=60 * 1024 * 1024)
+LARGE = pltpu.CompilerParams(vmem_limit_bytes=52 * 1024 * 1024)
+ATT = pltpu.CompilerParams(vmem_limit_bytes=60 * 1024 * 1024)
+CUT = pltpu.CompilerParams(vmem_limit_bytes=60 * 1024 * 1024)
 SMALL = pltpu.CompilerParams(vmem_limit_bytes=16 * 1024 * 1024)
 
 
@@ -35,23 +37,8 @@
     return [v] + [lax.ppermute(v, axis, shift(n, -k)) for k in range(1, n)]
 
 
-def ring(v, c, extras, other):
-    blocks = [v] + [None] * (NZ - 1)
-    up, down = v, v
-    done = []
-    for k in range(1, NZ // 2):
-        up = lax.ppermute(up, "z", shift(NZ, 1))
-        down = lax.ppermute(down, "z", shift(NZ, -1))
-        blocks[NZ - k], blocks[k] = up, down
-        done.append(other(lax.optimization_barrier((extras[k - 1], up))[0]))
-    ways = [
-        (i * NC + core, (i + way) % NZ * NC + core)
-        for i in range(NZ)
-        for core, way in ((0, 1), (1, NZ - 1))
-    ]
-    last = lax.ppermute(jnp.where(c == 0, up, down), ("z", "c"), ways)
-    blocks[NZ // 2], done = lax.optimization_barrier((last, done))
-    return blocks, done
+def spread(v, axis, n):
+    return lax.all_to_all(jnp.broadcast_to(v[None], (n,) + v.shape), axis, 0, 0)
 
 
 def moved(rows, source):
@@ -60,15 +47,20 @@
     return (source(i) == j).astype(BF16)
 
 
-def attend_kernel(scale, lengths, queries, new_entries, entries, w_uv, out, latents, cache, w, sems):
+def attend_kernel(
+    scale, lengths, q, new_entries, entries, w_uv, out, queries, latents, cache, w, sems
+):
     count, entry, span = cache.shape
     steps, heads = queries.shape[1:3]
     latent = latents.shape[2]
     value = w.shape[2]
     loads = [pltpu.make_async_copy(entries.at[r], cache.at[r], sems.at[r]) for r in range(count)]
     loads.append(pltpu.make_async_copy(w_uv, w, sems.at[count]))
+    first = pltpu.make_async_copy(q, queries, sems.at[count + 1])
+    first.start()
     for load in loads:
         load.start()
+    first.wait()
     for r in range(count):
         rows = queries[r].reshape(steps * heads, entry)
         fresh = new_entries[r].astype(F32)
@@ -95,7 +87,10 @@
             latents[:, r * steps + t, :] = result[t * heads : (t + 1) * heads]
     loads[count].wait()
     for h in range(heads):
-        out[:, h * value : (h + 1) * value] = dot(latents[h].astype(BF16), w[h]).astype(BF16)
+        part, n = divmod(h, heads // NY)
+        result = dot(latents[h].astype(BF16), w[h]).astype(BF16)
+        for b in range(NZ):
+            out[part, b, :, n * value : (n + 1) * value] = result
 
 
 def attend(queries, new_entries, cache, lengths, w_uv):
@@ -103,44 +98,64 @@
     _, latent, value = w_uv.shape
     return pl.pallas_call(
         lambda *refs: attend_kernel((NOPE + ROPE) ** (-0.5), *refs),
-        out_shape=jax.ShapeDtypeStruct((rolls * steps, heads * value), BF16),
-        in_specs=[SMEM, VMEM, VMEM, HBM, HBM],
+        out_shape=jax.ShapeDtypeStruct((NY, NZ, rolls * steps, heads * value // NY), BF16),
+        in_specs=[SMEM, HBM, VMEM, HBM, HBM],
         out_specs=VMEM,
         scratch_shapes=[
+            pltpu.VMEM(queries.shape, BF16),
             pltpu.VMEM((heads, rolls * steps, latent), F32),
             pltpu.VMEM(cache.shape, BF16),
             pltpu.VMEM(w_uv.shape, BF16),
-            pltpu.SemaphoreType.DMA((rolls + 1,)),
+            pltpu.SemaphoreType.DMA((rolls + 2,)),
         ],
-        compiler_params=LARGE,
+        compiler_params=ATT,
         name="attend",
     )(lengths, queries, new_entries, cache, w_uv)
 
 
-def project_kernel(count, place, *refs):
-    pieces, refs = refs[:count], refs[count:]
-    (w_own, w_alien, hidden, hidden_alien), outs = refs[:4], refs[4 : 4 + NX]
-    lhs, w, sems = refs[4 + NX :]
+def cut_kernel(v, out, sems):
+    blocks, _, depth = out.shape
+    moves = [
+        pltpu.make_async_copy(v.at[:, b * depth : (b + 1) * depth], out.at[b], sems.at[b])
+        for b in range(blocks)
+    ]
+    for move in moves:
+        move.start()
+    for move in moves:
+        move.wait()
+
+
+def cut(v, blocks):
+    rows, width = v.shape
+    return pl.pallas_call(
+        cut_kernel,
+        out_shape=jax.ShapeDtypeStruct((blocks, rows, width // blocks), v.dtype),
+        in_specs=[HBM],
+        out_specs=VMEM,
+        scratch_shapes=[pltpu.SemaphoreType.DMA((blocks,))],
+        compiler_params=CUT,
+        name="cut",
+    )(v)
+
+
+def project_kernel(place, lhs_in, w_own, w_alien, hidden, hidden_alien, out, lhs, w, sems):
     y, z, c, x = place[0], place[1], place[2], place[3]
-    cols = w_own.shape[0]
-    loads = [
-        pltpu.make_async_copy(
-            v, w.at[pl.ds(pl.multiple_of(at * cols, 16), cols)], sems.at[count + n]
-        )
-        for n, (v, at) in enumerate(((w_own, c), (w_alien, 1 - c)))
-    ]
-    rows = pieces[0].shape[0]
-    for n, piece in enumerate(pieces):
-        loads.append(
-            pltpu.make_async_copy(piece, lhs.at[pl.ds(n * rows, rows)], sems.at[n])
-        )
+    blocks, cols = w_own.shape[:2]
+    loads = [pltpu.make_async_copy(lhs_in, lhs, sems.at[0])]
+    for n, (v, at) in enumerate(((w_own, c), (w_alien, 1 - c))):
+        for b in range(blocks):
+            to = pl.multiple_of((b * NC + at) * cols, 16)
+            loads.append(
+                pltpu.make_async_copy(v.at[b], w.at[pl.ds(to, cols)], sems.at[1 + n * blocks + b])
+            )
     for load in loads:
         load.start()
+    rows, size = lhs.shape[0], out.shape[1]
 
     def stream(values):
         steps = values.shape[0] // cols
-        i = lax.broadcasted_iota(jnp.int32, (outs[0].shape[0], values.shape[1]), 0)
-        j = lax.broadcasted_iota(jnp.int32, (outs[0].shape[0], values.shape[1]), 1)
+        i = lax.broadcasted_iota(jnp.int32, (size, values.shape[1]), 0)
+        j = lax.broadcasted_iota(jnp.int32, (size, values.shape[1]), 1)
         here = (lax.shift_right_logical(i, 1) * NC + c) * NX + x == j
         total = 0.0
         for t in range(steps):
@@ -154,51 +169,58 @@
     )
 
     def source(i):
-        roll = (lax.shift_right_logical(i, 6) + x) & 3
-        zz = (lax.shift_right_logical(i, 1) + NZ - z) & 7
-        yy = (lax.shift_right_logical(i, 4) + NY - y) & 3
-        return zz * 32 + yy * 8 + roll * 2 + (i & 1)
-
-    order = moved(lhs.shape[0], source)
+        roll = lax.shift_right_logical(i, 6)
+        zz = lax.shift_right_logical(i, 1) & 7
+        yy = lax.shift_right_logical(i, 4) & 3
+        return yy * 64 + zz * 8 + roll * 2 + (i & 1)
+
+    order = moved(rows, source)
     for load in loads:
         load.wait()
-    part = dot_t(lhs[...], w[...]).astype(BF16)
-    part = dot(order, part)
-    size = outs[0].shape[0]
-    outs[0][...] = (part[:size] + added).astype(BF16)
-    for n in range(1, NX):
-        outs[n][...] = part[n * size : (n + 1) * size].astype(BF16)
-
-
-def project(place, pieces, weights, hidden):
-    rows = sum(p.shape[0] for p in pieces)
-    cols, depth = weights[0].shape
-    return pl.pallas_call(
-        lambda *refs: project_kernel(len(pieces), *refs),
-        out_shape=[jax.ShapeDtypeStruct((rows // NX, NC * cols), BF16)] * NX,
-        in_specs=[SMEM] + [ANY] * len(pieces) + [HBM] * NC + [VMEM] * NC,
-        out_specs=[VMEM] * NX,
+    pair = NC * cols
+    for b in range(blocks):
+        part = dot_t(lhs[...], w[b * pair : (b + 1) * pair]).astype(BF16)
+        part = dot(order, part)
+        for j in range(NX):
+            piece = part[j * size : (j + 1) * size]
+            piece = piece + jnp.where((j == x) & (b == y), added, 0.0)
+            out[j * blocks + b] = piece.astype(BF16)
+
+
+def project(place, lhs, weights, hidden):
+    rows, depth = lhs.shape
+    blocks, cols, _ = weights[0].shape
+    return pl.pallas_call(
+        project_kernel,
+        out_shape=jax.ShapeDtypeStruct((NX * blocks, rows // NX, NC * cols), BF16),
+        in_specs=[SMEM, ANY] + [HBM] * NC + [VMEM] * NC,
+        out_specs=VMEM,
         scratch_shapes=[
             pltpu.VMEM((rows, depth), BF16),
-            pltpu.VMEM((NC * cols, depth), BF16),
-            pltpu.SemaphoreType.DMA((len(pieces) + NC,)),
+            pltpu.VMEM((blocks * NC * cols, depth), BF16),
+            pltpu.SemaphoreType.DMA((1 + NC * blocks,)),
         ],
-        compiler_params=LARGE,
+        compiler_params=SMALL,
         name="project",
-    )(place, *pieces, *weights, *hidden)
-
-
-def gate_up_kernel(place, gain, blocks, w0, w1, w2, w3, o0, o1, o2, o3, scaled, w, sems):
+    )(place, lhs, *weights, *hidden)
+
+
+def gate_up_kernel(
+    place, gain, blocks_in, w0, w1, w2, w3, o0, o1, o2, o3, blocks, scaled, w, sems
+):
     hid = w0.shape[0]
     loads = [
         pltpu.make_async_copy(v, w.at[pl.ds(n * hid, hid)], sems.at[n])
         for n, v in enumerate((w0, w1, w2, w3))
     ]
+    first = pltpu.make_async_copy(blocks_in, blocks, sems.at[4])
+    first.start()
     for load in loads:
         load.start()
     ny, nz, rows, cols = blocks.shape
     x = place[3]
     squares = [0.0] * ny
+    first.wait()
     for b in range(nz):
         for k in range(ny):
             block = blocks[(x + k) & 3, b].astype(F32)
@@ -223,12 +245,13 @@
     return pl.pallas_call(
         gate_up_kernel,
         out_shape=[jax.ShapeDtypeStruct((rows, 4 * hid + 128), BF16)] * ny,
-        in_specs=[SMEM] + [VMEM] * 2 + [HBM] * 4,
+        in_specs=[SMEM, VMEM, ANY] + [HBM] * 4,
         out_specs=[VMEM] * ny,
         scratch_shapes=[
+            pltpu.VMEM(blocks.shape, BF16),
             pltpu.VMEM((ny * rows, width), BF16),
             pltpu.VMEM((4 * hid, width), BF16),
-            pltpu.SemaphoreType.DMA((4,)),
+            pltpu.SemaphoreType.DMA((5,)),
         ],
         compiler_params=LARGE,
         name="gate_up",
@@ -336,34 +359,30 @@
     def other(v):
         return lax.ppermute(v, "c", shift(NC, 1))
 
-    def cross(v, k):
-        return lax.ppermute(
-            v, ("y", "x"), [(b * NX + a, ((a + k) % NX) * NX + b) for b in range(NY) for a in range(NX)]
+    with jax.named_scope("attend"):
+        depth = w_o.shape[1] // NY
+        w_o = lax.all_to_all(cut(w_o, NY), "y", 0, 0)
+        swapped = [other(v) for v in (hidden, w_gate, w_up, w_down)]
+        head_out = attend(queries, new_entries, cache, lengths, w_uv)
+        head_out, w_o, swapped = lax.optimization_barrier((head_out, w_o, swapped))
+        hidden_alien, w_gate_alien, w_up_alien, w_down_alien = swapped
+
+    with jax.named_scope("gather_heads"):
+        w_o_alien = other(w_o)
+        near = lax.all_to_all(head_out.reshape(NY * NZ, -1, depth), ("y", "z"), 0, 0)
+        near, w_o_alien = lax.optimization_barrier((near, w_o_alien))
+
+    with jax.named_scope("project"):
+        parts = project(
+            place, near.reshape(-1, depth), (w_o, w_o_alien), (hidden, hidden_alien)
         )
 
-    with jax.named_scope("attend"):
-        w_o_alien, hidden_alien = other(w_o), other(hidden)
-        head_out = attend(queries, new_entries, cache, lengths, w_uv)
-        head_out, w_o_alien, hidden_alien = lax.optimization_barrier(
-            (head_out, w_o_alien, hidden_alien)
-        )
-
-    with jax.named_scope("gather_heads"):
-        near = jnp.concatenate(fetch(head_out, "y", NY), axis=0)
-        pieces, swapped = ring(near, c, (w_gate, w_up, w_down), other)
-        w_gate_alien, w_up_alien, w_down_alien = swapped
-
-    with jax.named_scope("project"):
-        parts = project(place, pieces, (w_o, w_o_alien), (hidden, hidden_alien))
-
     with jax.named_scope("sum_heads"):
-        total = 0.0
-        for k in range(NX):
-            total = total + cross(parts[k], k).astype(F32)
-        resid = total.astype(BF16)
+        parts = lax.all_to_all(parts, ("y", "x"), 0, 0)
+        resid = jnp.sum(parts.astype(F32), axis=0).astype(BF16)
 
     with jax.named_scope("gather_resid"):
-        resid = lax.all_to_all(jnp.broadcast_to(resid[None], (NZ,) + resid.shape), "z", 0, 0)
+        resid = spread(resid, "z", NZ)
         resid = lax.all_gather(resid, "y")
 
     with jax.named_scope("gate_up"):

time: 163 us -> 158 us (0.969)
  blocking collectives: 28.3 us -> 41.9 us
  starting transfers between devices: 45.8 us -> 33.5 us
  waiting for transfers between devices: 57.9 us -> 49.5 us
  Pallas kernels: 21.6 us -> 23.4 us
    ppermute x11 -> x0, waiting for transfers between devices: 25.1 us -> none  [the longest x3 13.3 us: ring(): up = lax.ppermute(up, 'z', shift(NZ, 1))]
    ppermute x11 -> x0, starting transfers between devices: 21.6 us -> none  [the longest x3 10.5 us: ring(): down = lax.ppermute(down, 'z', shift(NZ, -1))]
    all_to_all x1 -> x3, waiting for transfers between devices: 9.04 us -> 29.9 us  [the longest x1 14.2 us: on_device(): lax.all_to_all(head_out.reshape(NY * NZ, -1, depth), ('y', 'z'), 0, 0)]
    all_to_all x0 -> x1, blocking collectives: none -> 14.2 us  [on_device(): parts = lax.all_to_all(parts, ('y', 'x'), 0, 0)]
    all_to_all x1 -> x3, starting transfers between devices: 5.54 us -> 18.9 us  [the longest x1 9.47 us: on_device(): lax.all_to_all(head_out.reshape(NY * NZ, -1, depth), ('y', 'z'), 0, 0)]
    ppermute x6 -> x3, waiting for transfers between devices: 7.71 us -> 2.06 us  [fetch(): return [v] + [lax.ppermute(v, axis, shift(n, -k)) for k in range(1, n)]]
    ppermute x6 -> x3, starting transfers between devices: 9.67 us -> 6.56 us  [fetch(): return [v] + [lax.ppermute(v, axis, shift(n, -k)) for k in range(1, n)]]
    pallas_call x1 -> x2, Pallas kernels: 4.72 us -> 7.23 us  [the longest x1 4.99 us: project(): pl.pallas_call(project_kernel, out_shape=jax.ShapeDtypeStruct((NX * block...]
  transfers between devices with their start and end apart: 27 -> 15, of which waited for: 16 -> 10; matrix products, arithmetic and copies ran while one was open for 3% -> 1% of each run, Pallas kernels for 5% -> 6%
where the time goes in v2:
time: 158 us; the launch traced here: 155 us
  waiting for transfers between devices  49.5 us (31%)
  blocking collectives  41.9 us (27%)
  starting transfers between devices  33.5 us (21%)
  Pallas kernels  23.4 us (15%)
  other arithmetic  3.59 us (2%)
  local copies, waits for them, and re-layouts  3.39 us (2%)
    all_gather x1, blocking collectives, on_device(): resid = lax.all_gather(resid, 'y')  14.6 us
    all_to_all x1, waiting for transfers between devices, on_device(): lax.all_to_all(head_out.reshape(NY * NZ, -1, depth), ('y', 'z'), 0, 0)  14.2 us
    all_to_all x1, blocking collectives, on_device(): parts = lax.all_to_all(parts, ('y', 'x'), 0, 0)  14.2 us
    all_to_all x1, blocking collectives, on_device(): out = lax.all_to_all(out.reshape(NY, -1, width), 'y', 0, 0)  13.1 us
    all_to_all x1, waiting for transfers between devices, spread(): return lax.all_to_all(jnp.broadcast_to(v[None], (n,) + v.shape), axis, 0, 0)  9.64 us
    all_to_all x1, starting transfers between devices, on_device(): lax.all_to_all(head_out.reshape(NY * NZ, -1, depth), ('y', 'z'), 0, 0)  9.47 us
    all_to_all x1, waiting for transfers between devices, on_device(): out = lax.all_to_all(out.reshape(NZ, rolls * steps, width), 'z', 0, 0)  8.95 us
    pallas_call x1, Pallas kernels, attend(): pl.pallas_call(lambda *refs: attend_kernel((NOPE + ROPE) ** (-0.5), *refs...  7.47 us
  transfers between devices with their start and end apart: 15, of which 10 were waited for; matrix products, arithmetic and copies ran while one was open for 1% of the time, Pallas kernels for 6%

profile of v2, /device:TPU:2, one launch (start us, length us, event | category | flops | bytes accessed | tf_op | source)
XLA Modules:
  0.0 155.5 jit_solution(8602581357844299221)
XLA Ops:
  0.0 0.0 collective-permute-start.1
  0.0 0.5 collective-permute-start.2
  0.5 0.0 collective-permute-start.3
  0.5 2.2 %cut.1 = bf16[4,112,1024]{2,1,0:T(8,128)(2,1)} custom-call(bf16[112,4096]{1,0:T(8,128)(2,1)} %bitcast.32), custom_call_target="tpu_custom_call" | custom-call | tf_op jit(solution)/shard_map/attend/cut/pallas_call | solution.py:130
  2.8 4.5 %all-to-all-start = ((bf16[4,112,1024]{2,1,0:T(8,128)(2,1)}), bf16[4,112,1024]{2,1,0:T(8,128)(2,1)S(1)}, u32[]{:S(2)}, u32[]{:S(2)}) async-start(bf16[4,112,1024]{2,1,0:T(8,128)(2,1)} %cut.1), calls=%async_computation | async-start | bytes 1835008 | tf_op jit(solution)/shard_map/attend/all_to_all | solution.py:364
  7.2 0.2 collective-permute-start
  7.5 7.5 %attend.1 = bf16[4,8,8,1024]{3,2,1,0:T(8,128)(2,1)} custom-call(s32[4]{0:T(128)} %refs_0_.1, bf16[4,2,32,576]{3,2,1,0:T(8,128)(2,1)} %refs_1_.1, bf16[4,2,576]{2,1,0:T(2,128)(2,1)} %refs_2_.1, bf16[4,576,1024]{2,1,0:T(8,128)(2,1)} %bitcast.26, bf16[32,512,128]{2,1,0:T(8,128)(2,1)} %refs_4_.1), custom_call_target="tpu_custom_call" | custom-call | tf_op jit(solution)/shard_map/attend/attend/pallas_call | solution.py:99
  14.9 0.0 copy-start.1
  15.0 0.0 collective-permute-done.hidden_alien
  15.0 0.0 copy-start.3
  15.0 0.6 copy-done.3
  15.6 6.0 %all-to-all-done.w_own = bf16[4,112,1024]{2,1,0:T(8,128)(2,1)S(1)} async-done(((bf16[4,112,1024]{2,1,0:T(8,128)(2,1)}), bf16[4,112,1024]{2,1,0:T(8,128)(2,1)S(1)}, u32[]{:S(2)}, u32[]{:S(2)}) %all-to-all-start) | async-done | bytes 917536 | tf_op jit(solution)/shard_map/attend/all_to_all | solution.py:364
  21.6 0.0 collective-permute-done.1.w2
  21.6 0.0 collective-permute-done.2.w3
  21.6 0.0 collective-permute-done.3.w_alien
  21.6 9.5 %all-to-all-start.1 = ((bf16[32,8,1024]{2,1,0:T(8,128)(2,1)}), bf16[32,8,1024]{2,1,0:T(8,128)(2,1)S(1)}, u32[]{:S(2)}, u32[]{:S(2)}) async-start(bf16[32,8,1024]{2,1,0:T(8,128)(2,1)} %bitcast.29), calls=%async_computation.1 | async-start | bytes 1048576 | tf_op jit(solution)/shard_map/gather_heads/all_to_all | solution.py:372
  31.1 0.1 collective-permute-start.4
  31.2 0.1 pad_add_fusion.place
  31.3 2.5 %collective-permute-done.4.w_alien = bf16[4,112,1024]{2,1,0:T(8,128)(2,1)} collective-permute-done((bf16[4,112,1024]{2,1,0:T(8,128)(2,1)S(1)}, bf16[4,112,1024]{2,1,0:T(8,128)(2,1)}, u32[]{:S(2)}, u32[]{:S(2)}) %collective-permute-start.4) | collective-permute-done | bytes 917536 | tf_op jit(solution)/shard_map/gather_heads/ppermute | solution.py:360
  33.8 14.2 %all-to-all-done.1 = bf16[32,8,1024]{2,1,0:T(8,128)(2,1)S(1)} async-done(((bf16[32,8,1024]{2,1,0:T(8,128)(2,1)}), bf16[32,8,1024]{2,1,0:T(8,128)(2,1)S(1)}, u32[]{:S(2)}, u32[]{:S(2)}) %all-to-all-start.1) | async-done | bytes 524320 | tf_op jit(solution)/shard_map/gather_heads/all_to_all | solution.py:372
  48.0 0.0 copy-start.2
  48.0 0.9 copy-done.2
  48.9 0.0 copy-start.4
  48.9 0.9 copy-done.4
  49.8 5.0 %project.1 = bf16[16,64,224]{2,1,0:T(8,128)(2,1)S(1)} custom-call(s32[4]{0:T(128)S(1)} %pad_add_fusion.place, bf16[256,1024]{1,0:T(8,128)(2,1)S(1)} %bitcast.21, bf16[4,112,1024]{2,1,0:T(8,128)(2,1)S(1)} %all-to-all-done.w_own, bf16[4,112,1024]{2,1,0:T(8,128)(2,1)} %collective-permute-done.4.w_alien, bf16[224,256]{1,0:T(8,128)(2,1)S(1)} %bitcast.25, ...), custom_call_target="tpu_custom_call" | custom-call | tf_op jit(solution)/shard_map/project/project/pallas_call | solution.py:193
  54.8 0.0 copy-start
  54.8 14.2 %all_to_all.30 = bf16[16,64,224]{2,1,0:T(8,128)(2,1)} all-to-all(bf16[16,64,224]{2,1,0:T(8,128)(2,1)S(1)} %project.1), channel_id=1, replica_groups=mesh['y'=4,'z'=8,'c'=2,'x'=4] {'y','x'}, dimensions={0} | all-to-all | bytes 917504 | tf_op jit(solution)/shard_map/sum_heads/all_to_all | solution.py:381
  69.1 1.1 reduce_sum.23
  70.2 0.7 broadcast_in_dim.2
  70.9 4.9 %all-to-all-start.3 = ((bf16[8,64,224]{2,1,0:T(8,128)(2,1)}), bf16[8,64,224]{2,1,0:T(8,128)(2,1)S(1)}, u32[]{:S(2)}, u32[]{:S(2)}) async-start(bf16[8,64,224]{2,1,0:T(8,128)(2,1)} %broadcast_in_dim.2), calls=%async_computation.3 | async-start | bytes 524288 | tf_op jit(solution)/shard_map/gather_resid/all_to_all | solution.py:41
  75.8 0.8 dynamic-slice_convert_fusion
  76.6 0.1 reshape.36.gain
  76.7 9.6 %all-to-all-done.3 = bf16[8,64,224]{2,1,0:T(8,128)(2,1)S(1)} async-done(((bf16[8,64,224]{2,1,0:T(8,128)(2,1)}), bf16[8,64,224]{2,1,0:T(8,128)(2,1)S(1)}, u32[]{:S(2)}, u32[]{:S(2)}) %all-to-all-start.3) | async-done | bytes 229408 | tf_op jit(solution)/shard_map/gather_resid/all_to_all | solution.py:41
  86.3 14.6 %all-gather = bf16[32,64,224]{2,1,0:T(8,128)(2,1)} all-gather(bf16[8,64,224]{2,1,0:T(8,128)(2,1)S(1)} %all-to-all-done.3), channel_id=2, replica_groups=mesh['y'=4,'z'=8,'c'=2,'x'=4] {'y'}, dimensions={0}, use_global_device_ids=true | all-gather | bytes 1146880 | tf_op jit(solution)/shard_map/gather_resid/all_gather | solution.py:386
  100.9 0.0 copy-done.1
  100.9 5.3 %gate_up.1 = (bf16[64,1280]{1,0:T(8,128)(2,1)S(1)}, bf16[64,1280]{1,0:T(8,128)(2,1)S(1)}, bf16[64,1280]{1,0:T(8,128)(2,1)S(1)}, bf16[64,1280]{1,0:T(8,128)(2,1)S(1)}) custom-call(s32[4]{0:T(128)S(1)} %pad_add_fusion.place, f32[8,224]{1,0:T(8,128)S(1)} %reshape.36.gain, bf16[4,8,64,224]{3,2,1,0:T(8,128)(2,1)} %bitcast.27, bf16[288,1792]{1,0:T(8,128)(2,1)S(1)} %bitcast.23, ...), custom_call_target="tpu_custom_call" | custom-call | tf_op jit(solution)/shard_map/gate_up/gate_up/pallas_call | solution.py:245
  106.2 0.3 collective-permute-start.5
  106.4 3.3 %collective-permute-start.6 = (bf16[64,1280]{1,0:T(8,128)(2,1)S(1)}, bf16[64,1280]{1,0:T(8,128)(2,1)S(1)}, u32[]{:S(2)}, u32[]{:S(2)}) collective-permute-start(bf16[64,1280]{1,0:T(8,128)(2,1)S(1)} %get-tuple-element.26), channel_id=1, source_target_pairs={{0,2},{1,3},{2,0},{3,1},{4,6},{5,7},{6,4},{7,5},{8,10},{9,11},{10,... | collective-permute-start | bytes 491528 | tf_op jit(solution)/shard_map/sum_gate_up/ppermute | solution.py:396
  109.8 0.3 collective-permute-start.7
  110.0 1.5 collective-permute-done.5.refs_1_
  111.6 1.7 %collective-permute-done.6.refs_2_ = bf16[64,1280]{1,0:T(8,128)(2,1)S(1)} collective-permute-done((bf16[64,1280]{1,0:T(8,128)(2,1)S(1)}, bf16[64,1280]{1,0:T(8,128)(2,1)S(1)}, u32[]{:S(2)}, u32[]{:S(2)}) %collective-permute-start.6) | collective-permute-done | bytes 163872 | tf_op jit(solution)/shard_map/sum_gate_up/ppermute | solution.py:396
  113.3 2.9 %collective-permute-done.7.refs_3_ = bf16[64,1280]{1,0:T(8,128)(2,1)S(1)} collective-permute-done((bf16[64,1280]{1,0:T(8,128)(2,1)S(1)}, bf16[64,1280]{1,0:T(8,128)(2,1)S(1)}, u32[]{:S(2)}, u32[]{:S(2)}) %collective-permute-start.7) | collective-permute-done | bytes 163872 | tf_op jit(solution)/shard_map/sum_gate_up/ppermute | solution.py:396
  116.2 0.2 activate.1.a0
  116.4 2.6 %collective-permute-start.8 = (bf16[64,576]{1,0:T(8,128)(2,1)S(1)}, bf16[64,576]{1,0:T(8,128)(2,1)S(1)}, u32[]{:S(2)}, u32[]{:S(2)}) collective-permute-start(bf16[64,576]{1,0:T(8,128)(2,1)S(1)} %activate.1.a0), channel_id=1, source_target_pairs={{0,3},{1,0},{2,1},{3,2},{4,7},{5,4},{6,5},{7,6},{8,11},{9,8},{10,9... | collective-permute-start | bytes 221192 | tf_op jit(solution)/shard_map/down/ppermute | solution.py:37
  119.0 1.5 collective-permute-start.9
  120.4 2.5 %collective-permute-start.10 = (bf16[64,576]{1,0:T(8,128)(2,1)S(1)}, bf16[64,576]{1,0:T(8,128)(2,1)S(1)}, u32[]{:S(2)}, u32[]{:S(2)}) collective-permute-start(bf16[64,576]{1,0:T(8,128)(2,1)S(1)} %activate.1.a0), channel_id=1, source_target_pairs={{0,1},{1,2},{2,3},{3,0},{4,5},{5,6},{6,7},{7,4},{8,9},{9,10},{10,1... | collective-permute-start | bytes 221192 | tf_op jit(solution)/shard_map/down/ppermute | solution.py:37
  123.0 0.0 collective-permute-done.8.a1
  123.0 1.9 %collective-permute-done.9.a2 = bf16[64,576]{1,0:T(8,128)(2,1)S(1)} collective-permute-done((bf16[64,576]{1,0:T(8,128)(2,1)S(1)}, bf16[64,576]{1,0:T(8,128)(2,1)S(1)}, u32[]{:S(2)}, u32[]{:S(2)}) %collective-permute-start.9) | collective-permute-done | bytes 73760 | tf_op jit(solution)/shard_map/down/ppermute | solution.py:37
  124.9 0.1 collective-permute-done.10.a3
  125.0 0.0 copy-done
  125.0 2.2 %down.1 = bf16[4,4,16,1792]{3,2,1,0:T(8,128)(2,1)S(1)} custom-call(s32[4]{0:T(128)S(1)} %pad_add_fusion.place, bf16[64,576]{1,0:T(8,128)(2,1)S(1)} %activate.1.a0, bf16[64,576]{1,0:T(8,128)(2,1)S(1)} %collective-permute-done.8.a1, bf16[64,576]{1,0:T(8,128)(2,1)S(1)} %collective-permute-done.9.a2, bf16[64,576]{1,0:T(8,128)(2,1)S(1)} %collective-permute-done.10.a3, ...), custom_call_target="tpu_custom_call" | custom-call | tf_op jit(solution)/shard_map/down/down/pallas_call | solution.py:308
  127.3 13.1 %all_to_all.31.parts = bf16[4,64,1792]{2,1,0:T(8,128)(2,1)S(1)} all-to-all(bf16[4,64,1792]{2,1,0:T(8,128)(2,1)S(1)} %bitcast.20), channel_id=1, replica_groups=mesh['y'=4,'z'=8,'c'=2,'x'=4] {'y'}, dimensions={0} | all-to-all | bytes 1835008 | tf_op jit(solution)/shard_map/sum_y/all_to_all | solution.py:404
  140.4 1.0 sum_y.1
  141.3 3.4 %all-to-all-start.5 = ((bf16[8,8,1792]{2,1,0:T(8,128)(2,1)}), bf16[8,8,1792]{2,1,0:T(8,128)(2,1)S(1)}, u32[]{:S(2)}, u32[]{:S(2)}) async-start(bf16[8,8,1792]{2,1,0:T(8,128)(2,1)} %bitcast.15), calls=%async_computation.5 | async-start | bytes 458752 | tf_op jit(solution)/shard_map/sum_z/all_to_all | solution.py:408
  144.7 0.9 convert_bitcast_fusion
  145.7 0.1 reshape.34
  145.8 8.9 %all-to-all-done.5 = bf16[8,8,1792]{2,1,0:T(8,128)(2,1)S(1)} async-done(((bf16[8,8,1792]{2,1,0:T(8,128)(2,1)}), bf16[8,8,1792]{2,1,0:T(8,128)(2,1)S(1)}, u32[]{:S(2)}, u32[]{:S(2)}) %all-to-all-start.5) | async-done | bytes 229408 | tf_op jit(solution)/shard_map/sum_z/all_to_all | solution.py:408
  154.9 0.6 add_convert_fusion
  (3 shorter events, 0.1 us)
Async XLA Ops:
  0.0 21.6 %collective-permute-start.1 = (bf16[288,1792]{1,0:T(8,128)(2,1)}, bf16[288,1792]{1,0:T(8,128)(2,1)}, u32[]{:S(2)}, u32[]{:S(2)}) collective-permute-start(bf16[288,1792]{1,0:T(8,128)(2,1)} %bitcast.22), channel_id=1, source_target_pairs={{0,4},{4,0},{1,5},{5,1},{2,6},{6,2},{3,7},{7,3},{8,12},{12,8},{9,1... | collective-permute-start | bytes 3096584 | tf_op jit(solution)/shard_map/attend/ppermute | solution.py:360
  0.0 21.6 %collective-permute-start.2 = (bf16[288,1792]{1,0:T(8,128)(2,1)}, bf16[288,1792]{1,0:T(8,128)(2,1)}, u32[]{:S(2)}, u32[]{:S(2)}) collective-permute-start(bf16[288,1792]{1,0:T(8,128)(2,1)} %bitcast.30), channel_id=1, source_target_pairs={{0,4},{4,0},{1,5},{5,1},{2,6},{6,2},{3,7},{7,3},{8,12},{12,8},{9,1... | collective-permute-start | bytes 3096584 | tf_op jit(solution)/shard_map/attend/ppermute | solution.py:360
  0.5 21.1 %collective-permute-start.3 = (bf16[288,1792]{1,0:T(8,128)(2,1)}, bf16[288,1792]{1,0:T(8,128)(2,1)S(1)}, u32[]{:S(2)}, u32[]{:S(2)}) collective-permute-start(bf16[288,1792]{1,0:T(8,128)(2,1)} %w_own.1), channel_id=1, source_target_pairs={{0,4},{4,0},{1,5},{5,1},{2,6},{6,2},{3,7},{7,3},{8,12},{12,8},{9,1... | collective-permute-start | bytes 3096584 | tf_op jit(solution)/shard_map/attend/ppermute | solution.py:360
  2.8 18.8 %all-to-all-start = ((bf16[4,112,1024]{2,1,0:T(8,128)(2,1)}), bf16[4,112,1024]{2,1,0:T(8,128)(2,1)S(1)}, u32[]{:S(2)}, u32[]{:S(2)}) async-start(bf16[4,112,1024]{2,1,0:T(8,128)(2,1)} %cut.1), calls=%async_computation | async-start | bytes 1835008 | tf_op jit(solution)/shard_map/attend/all_to_all | solution.py:364
  7.2 7.7 %collective-permute-start = (bf16[224,256]{1,0:T(8,128)(2,1)}, bf16[224,256]{1,0:T(8,128)(2,1)S(1)}, u32[]{:S(2)}, u32[]{:S(2)}) collective-permute-start(bf16[224,256]{1,0:T(8,128)(2,1)} %bitcast.24), channel_id=1, source_target_pairs={{0,4},{4,0},{1,5},{5,1},{2,6},{6,2},{3,7},{7,3},{8,12},{12,8},{9,1... | collective-permute-start | bytes 344072 | tf_op jit(solution)/shard_map/attend/ppermute | solution.py:360
  14.9 85.9 %copy-start.1 = (bf16[1792,288]{0,1:T(8,128)(2,1)S(1)}, bf16[1792,288]{0,1:T(8,128)(2,1)}, u32[]{:S(2)}) copy-start(bf16[1792,288]{0,1:T(8,128)(2,1)} %param.19) | copy-start | bytes 3096580
  15.0 0.6 copy-start.3
  21.6 26.4 %all-to-all-start.1 = ((bf16[32,8,1024]{2,1,0:T(8,128)(2,1)}), bf16[32,8,1024]{2,1,0:T(8,128)(2,1)S(1)}, u32[]{:S(2)}, u32[]{:S(2)}) async-start(bf16[32,8,1024]{2,1,0:T(8,128)(2,1)} %bitcast.29), calls=%async_computation.1 | async-start | bytes 1048576 | tf_op jit(solution)/shard_map/gather_heads/all_to_all | solution.py:372
  31.1 2.7 %collective-permute-start.4 = (bf16[4,112,1024]{2,1,0:T(8,128)(2,1)S(1)}, bf16[4,112,1024]{2,1,0:T(8,128)(2,1)}, u32[]{:S(2)}, u32[]{:S(2)}) collective-permute-start(bf16[4,112,1024]{2,1,0:T(8,128)(2,1)S(1)} %all-to-all-done.w_own), channel_id=1, source_target_pairs={{0,4},{4,0},{1,5},{5,1},{2,6},{6,2},{3,7},{7,3},{8,12},{12,8},{9,1... | collective-permute-start | bytes 2752520 | tf_op jit(solution)/shard_map/gather_heads/ppermute | solution.py:360
  48.0 0.9 copy-start.2
  48.9 0.9 copy-start.4
  54.8 70.2 %copy-start = (bf16[288,1792]{1,0:T(8,128)(2,1)S(1)}, bf16[288,1792]{1,0:T(8,128)(2,1)}, u32[]{:S(2)}) copy-start(bf16[288,1792]{1,0:T(8,128)(2,1)} %w_own.1) | copy-start | bytes 3096580
  70.9 15.4 %all-to-all-start.3 = ((bf16[8,64,224]{2,1,0:T(8,128)(2,1)}), bf16[8,64,224]{2,1,0:T(8,128)(2,1)S(1)}, u32[]{:S(2)}, u32[]{:S(2)}) async-start(bf16[8,64,224]{2,1,0:T(8,128)(2,1)} %broadcast_in_dim.2), calls=%async_computation.3 | async-start | bytes 524288 | tf_op jit(solution)/shard_map/gather_resid/all_to_all | solution.py:41
  106.2 5.4 %collective-permute-start.5 = (bf16[64,1280]{1,0:T(8,128)(2,1)S(1)}, bf16[64,1280]{1,0:T(8,128)(2,1)S(1)}, u32[]{:S(2)}, u32[]{:S(2)}) collective-permute-start(bf16[64,1280]{1,0:T(8,128)(2,1)S(1)} %get-tuple-element.25), channel_id=1, source_target_pairs={{0,1},{1,2},{2,3},{3,0},{4,5},{5,6},{6,7},{7,4},{8,9},{9,10},{10,1... | collective-permute-start | bytes 491528 | tf_op jit(solution)/shard_map/sum_gate_up/ppermute | solution.py:396
  106.4 6.9 %collective-permute-start.6 = (bf16[64,1280]{1,0:T(8,128)(2,1)S(1)}, bf16[64,1280]{1,0:T(8,128)(2,1)S(1)}, u32[]{:S(2)}, u32[]{:S(2)}) collective-permute-start(bf16[64,1280]{1,0:T(8,128)(2,1)S(1)} %get-tuple-element.26), channel_id=1, source_target_pairs={{0,2},{1,3},{2,0},{3,1},{4,6},{5,7},{6,4},{7,5},{8,10},{9,11},{10,... | collective-permute-start | bytes 491528 | tf_op jit(solution)/shard_map/sum_gate_up/ppermute | solution.py:396
  109.8 6.4 %collective-permute-start.7 = (bf16[64,1280]{1,0:T(8,128)(2,1)S(1)}, bf16[64,1280]{1,0:T(8,128)(2,1)S(1)}, u32[]{:S(2)}, u32[]{:S(2)}) collective-permute-start(bf16[64,1280]{1,0:T(8,128)(2,1)S(1)} %get-tuple-element.27), channel_id=1, source_target_pairs={{0,3},{1,0},{2,1},{3,2},{4,7},{5,4},{6,5},{7,6},{8,11},{9,8},{10,9... | collective-permute-start | bytes 491528 | tf_op jit(solution)/shard_map/sum_gate_up/ppermute | solution.py:396
  116.4 6.6 %collective-permute-start.8 = (bf16[64,576]{1,0:T(8,128)(2,1)S(1)}, bf16[64,576]{1,0:T(8,128)(2,1)S(1)}, u32[]{:S(2)}, u32[]{:S(2)}) collective-permute-start(bf16[64,576]{1,0:T(8,128)(2,1)S(1)} %activate.1.a0), channel_id=1, source_target_pairs={{0,3},{1,0},{2,1},{3,2},{4,7},{5,4},{6,5},{7,6},{8,11},{9,8},{10,9... | collective-permute-start | bytes 221192 | tf_op jit(solution)/shard_map/down/ppermute | solution.py:37
  119.0 5.9 %collective-permute-start.9 = (bf16[64,576]{1,0:T(8,128)(2,1)S(1)}, bf16[64,576]{1,0:T(8,128)(2,1)S(1)}, u32[]{:S(2)}, u32[]{:S(2)}) collective-permute-start(bf16[64,576]{1,0:T(8,128)(2,1)S(1)} %activate.1.a0), channel_id=1, source_target_pairs={{0,2},{1,3},{2,0},{3,1},{4,6},{5,7},{6,4},{7,5},{8,10},{9,11},{10,... | collective-permute-start | bytes 221192 | tf_op jit(solution)/shard_map/down/ppermute | solution.py:37
  120.4 4.6 %collective-permute-start.10 = (bf16[64,576]{1,0:T(8,128)(2,1)S(1)}, bf16[64,576]{1,0:T(8,128)(2,1)S(1)}, u32[]{:S(2)}, u32[]{:S(2)}) collective-permute-start(bf16[64,576]{1,0:T(8,128)(2,1)S(1)} %activate.1.a0), channel_id=1, source_target_pairs={{0,1},{1,2},{2,3},{3,0},{4,5},{5,6},{6,7},{7,4},{8,9},{9,10},{10,1... | collective-permute-start | bytes 221192 | tf_op jit(solution)/shard_map/down/ppermute | solution.py:37
  141.3 13.4 %all-to-all-start.5 = ((bf16[8,8,1792]{2,1,0:T(8,128)(2,1)}), bf16[8,8,1792]{2,1,0:T(8,128)(2,1)S(1)}, u32[]{:S(2)}, u32[]{:S(2)}) async-start(bf16[8,8,1792]{2,1,0:T(8,128)(2,1)} %bitcast.15), calls=%async_computation.5 | async-start | bytes 458752 | tf_op jit(solution)/shard_map/sum_z/all_to_all | solution.py:408

commit v3 on v2

--- a/solution.py
+++ b/solution.py
@@ -35,10 +35,6 @@
 
 def fetch(v, axis, n):
     return [v] + [lax.ppermute(v, axis, shift(n, -k)) for k in range(1, n)]
-
-
-def spread(v, axis, n):
-    return lax.all_to_all(jnp.broadcast_to(v[None], (n,) + v.shape), axis, 0, 0)
 
 
 def moved(rows, source):
@@ -138,7 +134,40 @@
     )(v)
 
 
-def project_kernel(place, lhs_in, w_own, w_alien, hidden, hidden_alien, out, lhs, w, sems):
+def stream_kernel(steps, place, hidden, hidden_alien, out):
+    c, x = place[2], place[3]
+    size = out.shape[0]
+
+    def chosen(values):
+        cols = values.shape[0] // steps
+        i = lax.broadcasted_iota(jnp.int32, (size, values.shape[1]), 0)
+        j = lax.broadcasted_iota(jnp.int32, (size, values.shape[1]), 1)
+        here = (lax.shift_right_logical(i, 1) * NC + c) * NX + x == j
+        total = 0.0
+        for t in range(steps):
+            rows = (here & ((i & 1) == t)).astype(BF16)
+            total = total + dot_t(rows, values[t * cols : (t + 1) * cols])
+        return total
+
+    own, alien = chosen(hidden), chosen(hidden_alien)
+    out[...] = jnp.concatenate(
+        [jnp.where(c == 0, own, alien), jnp.where(c == 0, alien, own)], axis=1
+    ).astype(BF16)
+
+
+def stream(place, hidden, hidden_alien, steps):
+    rows = NY * NZ * steps
+    return pl.pallas_call(
+        lambda *refs: stream_kernel(steps, *refs),
+        out_shape=jax.ShapeDtypeStruct((rows, NC * hidden.shape[0] // steps), BF16),
+        in_specs=[SMEM, VMEM, VMEM],
+        out_specs=VMEM,
+        compiler_params=SMALL,
+        name="stream",
+    )(place, hidden, hidden_alien)
+
+
+def project_kernel(place, lhs_in, w_own, w_alien, added, out, lhs, w, sems):
     y, z, c, x = place[0], place[1], place[2], place[3]
     blocks, cols = w_own.shape[:2]
     loads = [pltpu.make_async_copy(lhs_in, lhs, sems.at[0])]
@@ -152,22 +181,6 @@
         load.start()
     rows, size = lhs.shape[0], out.shape[1]
 
-    def stream(values):
-        steps = values.shape[0] // cols
-        i = lax.broadcasted_iota(jnp.int32, (size, values.shape[1]), 0)
-        j = lax.broadcasted_iota(jnp.int32, (size, values.shape[1]), 1)
-        here = (lax.shift_right_logical(i, 1) * NC + c) * NX + x == j
-        total = 0.0
-        for t in range(steps):
-            chosen = (here & ((i & 1) == t)).astype(BF16)
-            total = total + dot_t(chosen, values[t * cols : (t + 1) * cols])
-        return total
-
-    own, alien = stream(hidden), stream(hidden_alien)
-    added = jnp.concatenate(
-        [jnp.where(c == 0, own, alien), jnp.where(c == 0, alien, own)], axis=1
-    )
-
     def source(i):
         roll = lax.shift_right_logical(i, 6)
         zz = lax.shift_right_logical(i, 1) & 7
@@ -183,17 +196,17 @@
         part = dot(order, part)
         for j in range(NX):
             piece = part[j * size : (j + 1) * size]
-            piece = piece + jnp.where((j == x) & (b == y), added, 0.0)
+            piece = piece + jnp.where((j == x) & (b == y), added[...].astype(F32), 0.0)
             out[j * blocks + b] = piece.astype(BF16)
 
 
-def project(place, lhs, weights, hidden):
+def project(place, lhs, weights, added):
     rows, depth = lhs.shape
     blocks, cols, _ = weights[0].shape
     return pl.pallas_call(
         project_kernel,
         out_shape=jax.ShapeDtypeStruct((NX * blocks, rows // NX, NC * cols), BF16),
-        in_specs=[SMEM, ANY] + [HBM] * NC + [VMEM] * NC,
+        in_specs=[SMEM, ANY] + [HBM] * NC + [VMEM],
         out_specs=VMEM,
         scratch_shapes=[
             pltpu.VMEM((rows, depth), BF16),
@@ -202,7 +215,26 @@
         ],
         compiler_params=SMALL,
         name="project",
-    )(place, lhs, *weights, *hidden)
+    )(place, lhs, *weights, added)
+
+
+def sum_heads_kernel(parts, out):
+    total = parts[0].astype(F32)
+    for n in range(1, parts.shape[0]):
+        total = total + parts[n].astype(F32)
+    for b in range(out.shape[0]):
+        out[b] = total.astype(BF16)
+
+
+def sum_heads(parts):
+    return pl.pallas_call(
+        sum_heads_kernel,
+        out_shape=jax.ShapeDtypeStruct((NZ,) + parts.shape[1:], BF16),
+        in_specs=[VMEM],
+        out_specs=VMEM,
+        compiler_params=SMALL,
+        name="sum_heads",
+    )(parts)
 
 
 def gate_up_kernel(
@@ -369,20 +401,19 @@
 
     with jax.named_scope("gather_heads"):
         w_o_alien = other(w_o)
+        added = stream(place, hidden, hidden_alien, steps)
         near = lax.all_to_all(head_out.reshape(NY * NZ, -1, depth), ("y", "z"), 0, 0)
-        near, w_o_alien = lax.optimization_barrier((near, w_o_alien))
+        near, w_o_alien, added = lax.optimization_barrier((near, w_o_alien, added))
 
     with jax.named_scope("project"):
-        parts = project(
-            place, near.reshape(-1, depth), (w_o, w_o_alien), (hidden, hidden_alien)
-        )
+        parts = project(place, near.reshape(-1, depth), (w_o, w_o_alien), added)
 
     with jax.named_scope("sum_heads"):
         parts = lax.all_to_all(parts, ("y", "x"), 0, 0)
-        resid = jnp.sum(parts.astype(F32), axis=0).astype(BF16)
+        resid = sum_heads(parts)
 
     with jax.named_scope("gather_resid"):
-        resid = spread(resid, "z", NZ)
+        resid = lax.all_to_all(resid, "z", 0, 0)
         resid = lax.all_gather(resid, "y")
 
     with jax.named_scope("gate_up"):

time: 158 us -> 155 us (0.981)
  waiting for transfers between devices: 49.5 us -> 46.9 us
    ppermute x5, waiting for transfers between devices: 2.52 us -> 0.01 us  [other(): return lax.ppermute(v, 'c', shift(NC, 1))]
  transfers between devices with their start and end apart: 15 -> 15, of which waited for: 10 -> 9; matrix products, arithmetic and copies ran while one was open for 1% -> 1% of each run, Pallas kernels for 6% -> 7%
where the time goes in v3:
time: 155 us; the launch traced here: 152 us
  waiting for transfers between devices  46.9 us (30%)
  blocking collectives  41.8 us (27%)
  starting transfers between devices  33.5 us (22%)
  Pallas kernels  24.9 us (16%)
  local copies, waits for them, and re-layouts  2.68 us (2%)
  other arithmetic  2.46 us (2%)
    all_gather x1, blocking collectives, on_device(): resid = lax.all_gather(resid, 'y')  14.6 us
    all_to_all x1, blocking collectives, on_device(): parts = lax.all_to_all(parts, ('y', 'x'), 0, 0)  14.1 us
    all_to_all x1, waiting for transfers between devices, on_device(): lax.all_to_all(head_out.reshape(NY * NZ, -1, depth), ('y', 'z'), 0, 0)  14.1 us
    all_to_all x1, blocking collectives, on_device(): out = lax.all_to_all(out.reshape(NY, -1, width), 'y', 0, 0)  13.1 us
    all_to_all x1, waiting for transfers between devices, on_device(): resid = lax.all_to_all(resid, 'z', 0, 0)  9.64 us
    all_to_all x1, starting transfers between devices, on_device(): lax.all_to_all(head_out.reshape(NY * NZ, -1, depth), ('y', 'z'), 0, 0)  9.47 us
    all_to_all x1, waiting for transfers between devices, on_device(): out = lax.all_to_all(out.reshape(NZ, rolls * steps, width), 'z', 0, 0)  8.95 us
    pallas_call x1, Pallas kernels, attend(): pl.pallas_call(lambda *refs: attend_kernel((NOPE + ROPE) ** (-0.5), *refs...  7.47 us
  transfers between devices with their start and end apart: 15, of which 9 were waited for; matrix products, arithmetic and copies ran while one was open for 1% of the time, Pallas kernels for 7%

profile of v3, /device:TPU:2, one launch (start us, length us, event | category | flops | bytes accessed | tf_op | source)
XLA Modules:
  0.0 152.5 jit_solution(4571141231789622849)
XLA Ops:
  0.0 0.0 collective-permute-start.1
  0.0 0.5 collective-permute-start.2
  0.5 0.0 collective-permute-start.3
  0.5 2.3 %cut.1 = bf16[4,112,1024]{2,1,0:T(8,128)(2,1)} custom-call(bf16[112,4096]{1,0:T(8,128)(2,1)} %bitcast.32), custom_call_target="tpu_custom_call" | custom-call | tf_op jit(solution)/shard_map/attend/cut/pallas_call | solution.py:126
  2.8 4.5 %all-to-all-start = ((bf16[4,112,1024]{2,1,0:T(8,128)(2,1)}), bf16[4,112,1024]{2,1,0:T(8,128)(2,1)S(1)}, u32[]{:S(2)}, u32[]{:S(2)}) async-start(bf16[4,112,1024]{2,1,0:T(8,128)(2,1)} %cut.1), calls=%async_computation | async-start | bytes 1835008 | tf_op jit(solution)/shard_map/attend/all_to_all | solution.py:396
  7.3 0.2 collective-permute-start
  7.5 7.5 %attend.1 = bf16[4,8,8,1024]{3,2,1,0:T(8,128)(2,1)} custom-call(s32[4]{0:T(128)} %refs_0_.1, bf16[4,2,32,576]{3,2,1,0:T(8,128)(2,1)} %refs_1_.1, bf16[4,2,576]{2,1,0:T(2,128)(2,1)} %refs_2_.1, bf16[4,576,1024]{2,1,0:T(8,128)(2,1)} %bitcast.26, bf16[32,512,128]{2,1,0:T(8,128)(2,1)} %refs_4_.1), custom_call_target="tpu_custom_call" | custom-call | tf_op jit(solution)/shard_map/attend/attend/pallas_call | solution.py:95
  15.0 0.0 copy-start.1
  15.0 0.0 collective-permute-done.refs_2_
  15.0 0.0 copy-start.3
  15.0 0.6 copy-done.3
  15.6 6.0 %all-to-all-done.w_own = bf16[4,112,1024]{2,1,0:T(8,128)(2,1)S(1)} async-done(((bf16[4,112,1024]{2,1,0:T(8,128)(2,1)}), bf16[4,112,1024]{2,1,0:T(8,128)(2,1)S(1)}, u32[]{:S(2)}, u32[]{:S(2)}) %all-to-all-start) | async-done | bytes 917536 | tf_op jit(solution)/shard_map/attend/all_to_all | solution.py:396
  21.6 0.0 collective-permute-done.1.w2
  21.6 0.0 collective-permute-done.2.w3
  21.6 0.0 collective-permute-done.3.w_alien
  21.6 9.5 %all-to-all-start.1 = ((bf16[32,8,1024]{2,1,0:T(8,128)(2,1)}), bf16[32,8,1024]{2,1,0:T(8,128)(2,1)S(1)}, u32[]{:S(2)}, u32[]{:S(2)}) async-start(bf16[32,8,1024]{2,1,0:T(8,128)(2,1)} %bitcast.29), calls=%async_computation.1 | async-start | bytes 1048576 | tf_op jit(solution)/shard_map/gather_heads/all_to_all | solution.py:405
  31.1 0.1 collective-permute-start.4
  31.2 0.1 pad_add_fusion.refs_0_.place
  31.3 0.0 copy-start.2
  31.3 0.9 copy-done.2
  32.2 0.0 copy-start.4
  32.2 0.9 copy-done.4
  33.1 0.8 stream.1.added
  33.9 0.0 collective-permute-done.4.w_alien
  33.9 14.1 %all-to-all-done.1 = bf16[32,8,1024]{2,1,0:T(8,128)(2,1)S(1)} async-done(((bf16[32,8,1024]{2,1,0:T(8,128)(2,1)}), bf16[32,8,1024]{2,1,0:T(8,128)(2,1)S(1)}, u32[]{:S(2)}, u32[]{:S(2)}) %all-to-all-start.1) | async-done | bytes 524320 | tf_op jit(solution)/shard_map/gather_heads/all_to_all | solution.py:405
  48.0 4.9 %project.1 = bf16[16,64,224]{2,1,0:T(8,128)(2,1)S(1)} custom-call(s32[4]{0:T(128)S(1)} %pad_add_fusion.refs_0_.place, bf16[256,1024]{1,0:T(8,128)(2,1)S(1)} %bitcast.21, bf16[4,112,1024]{2,1,0:T(8,128)(2,1)S(1)} %all-to-all-done.w_own, bf16[4,112,1024]{2,1,0:T(8,128)(2,1)} %collective-permute-done.4.w_alien, bf16[64,224]{1,0:T(8,128)(2,1)S(1)} %stream.1.added), custom_call_target="tpu_custom_call" | custom-call | tf_op jit(solution)/shard_map/project/project/pallas_call | solution.py:206
  53.0 0.0 copy-start
  53.0 14.1 %all_to_all.30.parts = bf16[16,64,224]{2,1,0:T(8,128)(2,1)S(1)} all-to-all(bf16[16,64,224]{2,1,0:T(8,128)(2,1)S(1)} %project.1), channel_id=1, replica_groups=mesh['y'=4,'z'=8,'c'=2,'x'=4] {'y','x'}, dimensions={0} | all-to-all | bytes 917504 | tf_op jit(solution)/shard_map/sum_heads/all_to_all | solution.py:412
  67.1 0.8 sum_heads.1
  67.9 4.9 %all-to-all-start.3 = ((bf16[8,64,224]{2,1,0:T(8,128)(2,1)}), bf16[8,64,224]{2,1,0:T(8,128)(2,1)S(1)}, u32[]{:S(2)}, u32[]{:S(2)}) async-start(bf16[8,64,224]{2,1,0:T(8,128)(2,1)} %sum_heads.1), calls=%async_computation.3 | async-start | bytes 524288 | tf_op jit(solution)/shard_map/gather_resid/all_to_all | solution.py:416
  72.8 0.8 dynamic-slice_convert_fusion
  73.6 0.1 reshape.35.gain
  73.7 9.6 %all-to-all-done.3 = bf16[8,64,224]{2,1,0:T(8,128)(2,1)S(1)} async-done(((bf16[8,64,224]{2,1,0:T(8,128)(2,1)}), bf16[8,64,224]{2,1,0:T(8,128)(2,1)S(1)}, u32[]{:S(2)}, u32[]{:S(2)}) %all-to-all-start.3) | async-done | bytes 229408 | tf_op jit(solution)/shard_map/gather_resid/all_to_all | solution.py:416
  83.3 14.6 %all-gather = bf16[32,64,224]{2,1,0:T(8,128)(2,1)} all-gather(bf16[8,64,224]{2,1,0:T(8,128)(2,1)S(1)} %all-to-all-done.3), channel_id=2, replica_groups=mesh['y'=4,'z'=8,'c'=2,'x'=4] {'y'}, dimensions={0}, use_global_device_ids=true | all-gather | bytes 1146880 | tf_op jit(solution)/shard_map/gather_resid/all_gather | solution.py:417
  97.9 0.0 copy-done.1
  97.9 5.3 %gate_up.1 = (bf16[64,1280]{1,0:T(8,128)(2,1)S(1)}, bf16[64,1280]{1,0:T(8,128)(2,1)S(1)}, bf16[64,1280]{1,0:T(8,128)(2,1)S(1)}, bf16[64,1280]{1,0:T(8,128)(2,1)S(1)}) custom-call(s32[4]{0:T(128)S(1)} %pad_add_fusion.refs_0_.place, f32[8,224]{1,0:T(8,128)S(1)} %reshape.35.gain, bf16[4,8,64,224]{3,2,1,0:T(8,128)(2,1)} %bitcast.27, ...), custom_call_target="tpu_custom_call" | custom-call | tf_op jit(solution)/shard_map/gate_up/gate_up/pallas_call | solution.py:277
  103.2 0.3 collective-permute-start.5
  103.4 3.3 %collective-permute-start.6 = (bf16[64,1280]{1,0:T(8,128)(2,1)S(1)}, bf16[64,1280]{1,0:T(8,128)(2,1)S(1)}, u32[]{:S(2)}, u32[]{:S(2)}) collective-permute-start(bf16[64,1280]{1,0:T(8,128)(2,1)S(1)} %get-tuple-element.28), channel_id=1, source_target_pairs={{0,2},{1,3},{2,0},{3,1},{4,6},{5,7},{6,4},{7,5},{8,10},{9,11},{10,... | collective-permute-start | bytes 491528 | tf_op jit(solution)/shard_map/sum_gate_up/ppermute | solution.py:427
  106.8 0.3 collective-permute-start.7
  107.0 1.5 %collective-permute-done.5.refs_1_ = bf16[64,1280]{1,0:T(8,128)(2,1)S(1)} collective-permute-done((bf16[64,1280]{1,0:T(8,128)(2,1)S(1)}, bf16[64,1280]{1,0:T(8,128)(2,1)S(1)}, u32[]{:S(2)}, u32[]{:S(2)}) %collective-permute-start.5) | collective-permute-done | bytes 163872 | tf_op jit(solution)/shard_map/sum_gate_up/ppermute | solution.py:427
  108.5 1.8 %collective-permute-done.6.refs_2_ = bf16[64,1280]{1,0:T(8,128)(2,1)S(1)} collective-permute-done((bf16[64,1280]{1,0:T(8,128)(2,1)S(1)}, bf16[64,1280]{1,0:T(8,128)(2,1)S(1)}, u32[]{:S(2)}, u32[]{:S(2)}) %collective-permute-start.6) | collective-permute-done | bytes 163872 | tf_op jit(solution)/shard_map/sum_gate_up/ppermute | solution.py:427
  110.3 2.8 %collective-permute-done.7.refs_3_ = bf16[64,1280]{1,0:T(8,128)(2,1)S(1)} collective-permute-done((bf16[64,1280]{1,0:T(8,128)(2,1)S(1)}, bf16[64,1280]{1,0:T(8,128)(2,1)S(1)}, u32[]{:S(2)}, u32[]{:S(2)}) %collective-permute-start.7) | collective-permute-done | bytes 163872 | tf_op jit(solution)/shard_map/sum_gate_up/ppermute | solution.py:427
  113.2 0.2 activate.1.a0
  113.4 2.6 %collective-permute-start.8 = (bf16[64,576]{1,0:T(8,128)(2,1)S(1)}, bf16[64,576]{1,0:T(8,128)(2,1)S(1)}, u32[]{:S(2)}, u32[]{:S(2)}) collective-permute-start(bf16[64,576]{1,0:T(8,128)(2,1)S(1)} %activate.1.a0), channel_id=1, source_target_pairs={{0,3},{1,0},{2,1},{3,2},{4,7},{5,4},{6,5},{7,6},{8,11},{9,8},{10,9... | collective-permute-start | bytes 221192 | tf_op jit(solution)/shard_map/down/ppermute | solution.py:37
  116.0 1.5 collective-permute-start.9
  117.4 2.5 %collective-permute-start.10 = (bf16[64,576]{1,0:T(8,128)(2,1)S(1)}, bf16[64,576]{1,0:T(8,128)(2,1)S(1)}, u32[]{:S(2)}, u32[]{:S(2)}) collective-permute-start(bf16[64,576]{1,0:T(8,128)(2,1)S(1)} %activate.1.a0), channel_id=1, source_target_pairs={{0,1},{1,2},{2,3},{3,0},{4,5},{5,6},{6,7},{7,4},{8,9},{9,10},{10,1... | collective-permute-start | bytes 221192 | tf_op jit(solution)/shard_map/down/ppermute | solution.py:37
  120.0 0.0 collective-permute-done.8.a1
  120.0 1.9 %collective-permute-done.9.a2 = bf16[64,576]{1,0:T(8,128)(2,1)S(1)} collective-permute-done((bf16[64,576]{1,0:T(8,128)(2,1)S(1)}, bf16[64,576]{1,0:T(8,128)(2,1)S(1)}, u32[]{:S(2)}, u32[]{:S(2)}) %collective-permute-start.9) | collective-permute-done | bytes 73760 | tf_op jit(solution)/shard_map/down/ppermute | solution.py:37
  121.9 0.1 collective-permute-done.10.a3
  122.0 0.0 copy-done
  122.0 2.2 %down.1 = bf16[4,4,16,1792]{3,2,1,0:T(8,128)(2,1)S(1)} custom-call(s32[4]{0:T(128)S(1)} %pad_add_fusion.refs_0_.place, bf16[64,576]{1,0:T(8,128)(2,1)S(1)} %activate.1.a0, bf16[64,576]{1,0:T(8,128)(2,1)S(1)} %collective-permute-done.8.a1, bf16[64,576]{1,0:T(8,128)(2,1)S(1)} %collective-permute-done.9.a2, bf16[64,576]{1,0:T(8,128)(2,1)S(1)} %collective-permute-done.10.a3, ...), custom_call_target="tpu_custom_call" | custom-call | tf_op jit(solution)/shard_map/down/down/pallas_call | solution.py:340
  124.2 13.1 %all_to_all.31.parts = bf16[4,64,1792]{2,1,0:T(8,128)(2,1)S(1)} all-to-all(bf16[4,64,1792]{2,1,0:T(8,128)(2,1)S(1)} %bitcast.20), channel_id=1, replica_groups=mesh['y'=4,'z'=8,'c'=2,'x'=4] {'y'}, dimensions={0} | all-to-all | bytes 1835008 | tf_op jit(solution)/shard_map/sum_y/all_to_all | solution.py:435
  137.3 1.0 sum_y.1
  138.3 3.4 %all-to-all-start.5 = ((bf16[8,8,1792]{2,1,0:T(8,128)(2,1)}), bf16[8,8,1792]{2,1,0:T(8,128)(2,1)S(1)}, u32[]{:S(2)}, u32[]{:S(2)}) async-start(bf16[8,8,1792]{2,1,0:T(8,128)(2,1)} %bitcast.16), calls=%async_computation.5 | async-start | bytes 458752 | tf_op jit(solution)/shard_map/sum_z/all_to_all | solution.py:439
  141.7 0.9 convert_bitcast_fusion
  142.7 0.1 reshape.33
  142.8 8.9 %all-to-all-done.5 = bf16[8,8,1792]{2,1,0:T(8,128)(2,1)S(1)} async-done(((bf16[8,8,1792]{2,1,0:T(8,128)(2,1)}), bf16[8,8,1792]{2,1,0:T(8,128)(2,1)S(1)}, u32[]{:S(2)}, u32[]{:S(2)}) %all-to-all-start.5) | async-done | bytes 229408 | tf_op jit(solution)/shard_map/sum_z/all_to_all | solution.py:439
  151.8 0.6 add_convert_fusion
  (3 shorter events, 0.1 us)
Async XLA Ops:
  0.0 21.6 %collective-permute-start.1 = (bf16[288,1792]{1,0:T(8,128)(2,1)}, bf16[288,1792]{1,0:T(8,128)(2,1)}, u32[]{:S(2)}, u32[]{:S(2)}) collective-permute-start(bf16[288,1792]{1,0:T(8,128)(2,1)} %bitcast.22), channel_id=1, source_target_pairs={{0,4},{4,0},{1,5},{5,1},{2,6},{6,2},{3,7},{7,3},{8,12},{12,8},{9,1... | collective-permute-start | bytes 3096584 | tf_op jit(solution)/shard_map/attend/ppermute | solution.py:392
  0.0 21.6 %collective-permute-start.2 = (bf16[288,1792]{1,0:T(8,128)(2,1)}, bf16[288,1792]{1,0:T(8,128)(2,1)}, u32[]{:S(2)}, u32[]{:S(2)}) collective-permute-start(bf16[288,1792]{1,0:T(8,128)(2,1)} %bitcast.30), channel_id=1, source_target_pairs={{0,4},{4,0},{1,5},{5,1},{2,6},{6,2},{3,7},{7,3},{8,12},{12,8},{9,1... | collective-permute-start | bytes 3096584 | tf_op jit(solution)/shard_map/attend/ppermute | solution.py:392
  0.5 21.1 %collective-permute-start.3 = (bf16[288,1792]{1,0:T(8,128)(2,1)}, bf16[288,1792]{1,0:T(8,128)(2,1)S(1)}, u32[]{:S(2)}, u32[]{:S(2)}) collective-permute-start(bf16[288,1792]{1,0:T(8,128)(2,1)} %w_own.1), channel_id=1, source_target_pairs={{0,4},{4,0},{1,5},{5,1},{2,6},{6,2},{3,7},{7,3},{8,12},{12,8},{9,1... | collective-permute-start | bytes 3096584 | tf_op jit(solution)/shard_map/attend/ppermute | solution.py:392
  2.8 18.8 %all-to-all-start = ((bf16[4,112,1024]{2,1,0:T(8,128)(2,1)}), bf16[4,112,1024]{2,1,0:T(8,128)(2,1)S(1)}, u32[]{:S(2)}, u32[]{:S(2)}) async-start(bf16[4,112,1024]{2,1,0:T(8,128)(2,1)} %cut.1), calls=%async_computation | async-start | bytes 1835008 | tf_op jit(solution)/shard_map/attend/all_to_all | solution.py:396
  7.3 7.7 %collective-permute-start = (bf16[224,256]{1,0:T(8,128)(2,1)}, bf16[224,256]{1,0:T(8,128)(2,1)S(1)}, u32[]{:S(2)}, u32[]{:S(2)}) collective-permute-start(bf16[224,256]{1,0:T(8,128)(2,1)} %bitcast.24), channel_id=1, source_target_pairs={{0,4},{4,0},{1,5},{5,1},{2,6},{6,2},{3,7},{7,3},{8,12},{12,8},{9,1... | collective-permute-start | bytes 344072 | tf_op jit(solution)/shard_map/attend/ppermute | solution.py:392
  15.0 82.9 %copy-start.1 = (bf16[1792,288]{0,1:T(8,128)(2,1)S(1)}, bf16[1792,288]{0,1:T(8,128)(2,1)}, u32[]{:S(2)}) copy-start(bf16[1792,288]{0,1:T(8,128)(2,1)} %param.19) | copy-start | bytes 3096580
  15.0 0.6 copy-start.3
  21.6 26.4 %all-to-all-start.1 = ((bf16[32,8,1024]{2,1,0:T(8,128)(2,1)}), bf16[32,8,1024]{2,1,0:T(8,128)(2,1)S(1)}, u32[]{:S(2)}, u32[]{:S(2)}) async-start(bf16[32,8,1024]{2,1,0:T(8,128)(2,1)} %bitcast.29), calls=%async_computation.1 | async-start | bytes 1048576 | tf_op jit(solution)/shard_map/gather_heads/all_to_all | solution.py:405
  31.1 2.8 %collective-permute-start.4 = (bf16[4,112,1024]{2,1,0:T(8,128)(2,1)S(1)}, bf16[4,112,1024]{2,1,0:T(8,128)(2,1)}, u32[]{:S(2)}, u32[]{:S(2)}) collective-permute-start(bf16[4,112,1024]{2,1,0:T(8,128)(2,1)S(1)} %all-to-all-done.w_own), channel_id=1, source_target_pairs={{0,4},{4,0},{1,5},{5,1},{2,6},{6,2},{3,7},{7,3},{8,12},{12,8},{9,1... | collective-permute-start | bytes 2752520 | tf_op jit(solution)/shard_map/gather_heads/ppermute | solution.py:392
  31.3 0.9 copy-start.2
  32.2 0.9 copy-start.4
  53.0 69.0 %copy-start = (bf16[288,1792]{1,0:T(8,128)(2,1)S(1)}, bf16[288,1792]{1,0:T(8,128)(2,1)}, u32[]{:S(2)}) copy-start(bf16[288,1792]{1,0:T(8,128)(2,1)} %w_own.1) | copy-start | bytes 3096580
  67.9 15.4 %all-to-all-start.3 = ((bf16[8,64,224]{2,1,0:T(8,128)(2,1)}), bf16[8,64,224]{2,1,0:T(8,128)(2,1)S(1)}, u32[]{:S(2)}, u32[]{:S(2)}) async-start(bf16[8,64,224]{2,1,0:T(8,128)(2,1)} %sum_heads.1), calls=%async_computation.3 | async-start | bytes 524288 | tf_op jit(solution)/shard_map/gather_resid/all_to_all | solution.py:416
  103.2 5.4 %collective-permute-start.5 = (bf16[64,1280]{1,0:T(8,128)(2,1)S(1)}, bf16[64,1280]{1,0:T(8,128)(2,1)S(1)}, u32[]{:S(2)}, u32[]{:S(2)}) collective-permute-start(bf16[64,1280]{1,0:T(8,128)(2,1)S(1)} %get-tuple-element.27), channel_id=1, source_target_pairs={{0,1},{1,2},{2,3},{3,0},{4,5},{5,6},{6,7},{7,4},{8,9},{9,10},{10,1... | collective-permute-start | bytes 491528 | tf_op jit(solution)/shard_map/sum_gate_up/ppermute | solution.py:427
  103.4 6.9 %collective-permute-start.6 = (bf16[64,1280]{1,0:T(8,128)(2,1)S(1)}, bf16[64,1280]{1,0:T(8,128)(2,1)S(1)}, u32[]{:S(2)}, u32[]{:S(2)}) collective-permute-start(bf16[64,1280]{1,0:T(8,128)(2,1)S(1)} %get-tuple-element.28), channel_id=1, source_target_pairs={{0,2},{1,3},{2,0},{3,1},{4,6},{5,7},{6,4},{7,5},{8,10},{9,11},{10,... | collective-permute-start | bytes 491528 | tf_op jit(solution)/shard_map/sum_gate_up/ppermute | solution.py:427
  106.8 6.4 %collective-permute-start.7 = (bf16[64,1280]{1,0:T(8,128)(2,1)S(1)}, bf16[64,1280]{1,0:T(8,128)(2,1)S(1)}, u32[]{:S(2)}, u32[]{:S(2)}) collective-permute-start(bf16[64,1280]{1,0:T(8,128)(2,1)S(1)} %get-tuple-element.29), channel_id=1, source_target_pairs={{0,3},{1,0},{2,1},{3,2},{4,7},{5,4},{6,5},{7,6},{8,11},{9,8},{10,9... | collective-permute-start | bytes 491528 | tf_op jit(solution)/shard_map/sum_gate_up/ppermute | solution.py:427
  113.4 6.6 %collective-permute-start.8 = (bf16[64,576]{1,0:T(8,128)(2,1)S(1)}, bf16[64,576]{1,0:T(8,128)(2,1)S(1)}, u32[]{:S(2)}, u32[]{:S(2)}) collective-permute-start(bf16[64,576]{1,0:T(8,128)(2,1)S(1)} %activate.1.a0), channel_id=1, source_target_pairs={{0,3},{1,0},{2,1},{3,2},{4,7},{5,4},{6,5},{7,6},{8,11},{9,8},{10,9... | collective-permute-start | bytes 221192 | tf_op jit(solution)/shard_map/down/ppermute | solution.py:37
  116.0 5.9 %collective-permute-start.9 = (bf16[64,576]{1,0:T(8,128)(2,1)S(1)}, bf16[64,576]{1,0:T(8,128)(2,1)S(1)}, u32[]{:S(2)}, u32[]{:S(2)}) collective-permute-start(bf16[64,576]{1,0:T(8,128)(2,1)S(1)} %activate.1.a0), channel_id=1, source_target_pairs={{0,2},{1,3},{2,0},{3,1},{4,6},{5,7},{6,4},{7,5},{8,10},{9,11},{10,... | collective-permute-start | bytes 221192 | tf_op jit(solution)/shard_map/down/ppermute | solution.py:37
  117.4 4.6 %collective-permute-start.10 = (bf16[64,576]{1,0:T(8,128)(2,1)S(1)}, bf16[64,576]{1,0:T(8,128)(2,1)S(1)}, u32[]{:S(2)}, u32[]{:S(2)}) collective-permute-start(bf16[64,576]{1,0:T(8,128)(2,1)S(1)} %activate.1.a0), channel_id=1, source_target_pairs={{0,1},{1,2},{2,3},{3,0},{4,5},{5,6},{6,7},{7,4},{8,9},{9,10},{10,1... | collective-permute-start | bytes 221192 | tf_op jit(solution)/shard_map/down/ppermute | solution.py:37
  138.3 13.4 %all-to-all-start.5 = ((bf16[8,8,1792]{2,1,0:T(8,128)(2,1)}), bf16[8,8,1792]{2,1,0:T(8,128)(2,1)S(1)}, u32[]{:S(2)}, u32[]{:S(2)}) async-start(bf16[8,8,1792]{2,1,0:T(8,128)(2,1)} %bitcast.16), calls=%async_computation.5 | async-start | bytes 458752 | tf_op jit(solution)/shard_map/sum_z/all_to_all | solution.py:439

commit v4 on v3

--- a/solution.py
+++ b/solution.py
@@ -18,6 +18,7 @@
 LARGE = pltpu.CompilerParams(vmem_limit_bytes=52 * 1024 * 1024)
 ATT = pltpu.CompilerParams(vmem_limit_bytes=60 * 1024 * 1024)
 CUT = pltpu.CompilerParams(vmem_limit_bytes=60 * 1024 * 1024)
+MIDDLE = pltpu.CompilerParams(vmem_limit_bytes=44 * 1024 * 1024)
 SMALL = pltpu.CompilerParams(vmem_limit_bytes=16 * 1024 * 1024)
 
 
@@ -237,22 +238,45 @@
     )(parts)
 
 
-def gate_up_kernel(
-    place, gain, blocks_in, w0, w1, w2, w3, o0, o1, o2, o3, blocks, scaled, w, sems
-):
-    hid = w0.shape[0]
+def stacked_kernel(count, *refs):
+    parts, out, sems = refs[:count], refs[count], refs[count + 1]
+    rows = parts[0].shape[0]
     loads = [
-        pltpu.make_async_copy(v, w.at[pl.ds(n * hid, hid)], sems.at[n])
-        for n, v in enumerate((w0, w1, w2, w3))
+        pltpu.make_async_copy(v, out.at[pl.ds(n * rows, rows)], sems.at[n])
+        for n, v in enumerate(parts)
     ]
-    first = pltpu.make_async_copy(blocks_in, blocks, sems.at[4])
-    first.start()
+    for load in loads:
+        load.start()
+    for load in loads:
+        load.wait()
+
+
+def stacked(parts):
+    rows, width = parts[0].shape
+    return pl.pallas_call(
+        lambda *refs: stacked_kernel(len(parts), *refs),
+        out_shape=jax.ShapeDtypeStruct((len(parts) * rows, width), parts[0].dtype),
+        in_specs=[HBM] * len(parts),
+        out_specs=VMEM,
+        scratch_shapes=[pltpu.SemaphoreType.DMA((len(parts),))],
+        compiler_params=MIDDLE,
+        name="stacked",
+    )(*parts)
+
+
+def gate_up_kernel(place, gain, b0, b1, b2, b3, w, o0, o1, o2, o3, blocks, scaled, sems):
+    hid = w.shape[0] // 4
+    y, x = place[0], place[3]
+    loads = [
+        pltpu.make_async_copy(v, blocks.at[(y + n) & 3], sems.at[n])
+        for n, v in enumerate((b0, b1, b2, b3))
+    ]
     for load in loads:
         load.start()
     ny, nz, rows, cols = blocks.shape
-    x = place[3]
+    for load in loads:
+        load.wait()
     squares = [0.0] * ny
-    first.wait()
     for b in range(nz):
         for k in range(ny):
             block = blocks[(x + k) & 3, b].astype(F32)
@@ -260,34 +284,28 @@
             scaled[k * rows : (k + 1) * rows, b * cols : (b + 1) * cols] = (
                 block * gain[b : b + 1, :]
             ).astype(BF16)
-    outs = (o0, o1, o2, o3)
-    for n in range(NC):
-        for load in loads[2 * n : 2 * n + 2]:
-            load.wait()
-        total = dot_t(scaled[...], w[2 * n * hid : 2 * (n + 1) * hid]).astype(BF16)
-        for k, out in enumerate(outs):
-            out[:, 2 * n * hid : 2 * (n + 1) * hid] = total[k * rows : (k + 1) * rows]
-    for k, out in enumerate(outs):
+    total = dot_t(scaled[...], w[...]).astype(BF16)
+    for k, out in enumerate((o0, o1, o2, o3)):
+        out[:, : 4 * hid] = total[k * rows : (k + 1) * rows]
         out[:, 4 * hid :] = jnp.broadcast_to(squares[k].astype(BF16), (rows, 128))
 
 
-def gate_up(place, gain, blocks, weights):
-    ny, nz, rows, cols = blocks.shape
-    hid, width = weights[0].shape
+def gate_up(place, gain, blocks, w):
+    ny, (nz, rows, cols) = len(blocks), blocks[0].shape
+    units, width = w.shape
     return pl.pallas_call(
         gate_up_kernel,
-        out_shape=[jax.ShapeDtypeStruct((rows, 4 * hid + 128), BF16)] * ny,
-        in_specs=[SMEM, VMEM, ANY] + [HBM] * 4,
+        out_shape=[jax.ShapeDtypeStruct((rows, units + 128), BF16)] * ny,
+        in_specs=[SMEM, VMEM] + [ANY] * ny + [VMEM],
         out_specs=[VMEM] * ny,
         scratch_shapes=[
-            pltpu.VMEM(blocks.shape, BF16),
+            pltpu.VMEM((ny,) + blocks[0].shape, BF16),
             pltpu.VMEM((ny * rows, width), BF16),
-            pltpu.VMEM((4 * hid, width), BF16),
-            pltpu.SemaphoreType.DMA((5,)),
+            pltpu.SemaphoreType.DMA((ny,)),
         ],
-        compiler_params=LARGE,
+        compiler_params=SMALL,
         name="gate_up",
-    )(place, gain, blocks, *weights)
+    )(place, gain, *blocks, w)
 
 
 def activate_kernel(features, hid, m0, m1, m2, m3, act):
@@ -414,13 +432,15 @@
 
     with jax.named_scope("gather_resid"):
         resid = lax.all_to_all(resid, "z", 0, 0)
-        resid = lax.all_gather(resid, "y")
+        resid, ready = lax.optimization_barrier(
+            (resid, (w_gate, w_up, w_gate_alien, w_up_alien))
+        )
+        blocks = fetch(resid, "y", NY)
+        weights = stacked(ready)
 
     with jax.named_scope("gate_up"):
         gain = lax.dynamic_slice_in_dim(ffn_gain, x * width, width, 0).astype(F32)
-        messages = gate_up(
-            place, gain.reshape(NZ, pair), resid, (w_gate, w_up, w_gate_alien, w_up_alien)
-        )
+        messages = gate_up(place, gain.reshape(NZ, pair), blocks, weights)
 
     with jax.named_scope("sum_gate_up"):
         messages = [messages[0]] + [
@@ -440,7 +460,10 @@
         out = jnp.sum(out.astype(F32), axis=0)
 
     with jax.named_scope("finish"):
-        own = lax.dynamic_slice_in_dim(resid, (y * NZ + z) * steps, steps, 2)
+        at = (y * NZ + z) * steps
+        own = jnp.stack([lax.dynamic_slice_in_dim(b, at, steps, 1) for b in blocks])
+        own = jnp.concatenate([own, own], axis=0)
+        own = lax.dynamic_slice_in_dim(own, lax.rem(NY - y, NY), NY, 0)
         own = own.transpose(0, 2, 1, 3).reshape(rolls * steps, width)
         out = (own.astype(F32) + out).astype(BF16)
     return out.reshape(rolls, steps, width)

time: 155 us -> 150 us (0.968)
  blocking collectives: 41.8 us -> 14 us
  waiting for transfers between devices: 46.9 us -> 64.7 us
  starting transfers between devices: 33.5 us -> 39.2 us
    all_gather x1 -> x0, blocking collectives: 14.6 us -> none  [on_device(): resid = lax.all_gather(resid, 'y')]
    all_to_all x1 -> x0, blocking collectives: 13.1 us -> none  [on_device(): out = lax.all_to_all(out.reshape(NY, -1, width), 'y', 0, 0)]
    all_to_all x0 -> x1, waiting for transfers between devices: none -> 10.1 us  [on_device(): out = lax.all_to_all(out.reshape(NY, -1, width), 'y', 0, 0)]
    ppermute x3 -> x6, waiting for transfers between devices: 2.06 us -> 10.5 us  [fetch(): return [v] + [lax.ppermute(v, axis, shift(n, -k)) for k in range(1, n)]]
    all_to_all x0 -> x1, starting transfers between devices: none -> 3.52 us  [on_device(): out = lax.all_to_all(out.reshape(NY, -1, width), 'y', 0, 0)]
    ppermute x3, waiting for transfers between devices: 6.13 us -> 4.38 us  [on_device(): lax.ppermute(messages[k], 'x', shift(NX, k))]
    unnamed x10 -> x19, local copies, waits for them, and re-layouts: 2.44 us -> 3.7 us
    pallas_call x1 -> x2, Pallas kernels: 5.26 us -> 4.45 us  [the longest x1 2.3 us: stacked(): pl.pallas_call(lambda *refs: stacked_kernel(len(parts), *refs), out_shape...]
  transfers between devices with their start and end apart: 15 -> 19, of which waited for: 9 -> 12; matrix products, arithmetic and copies ran while one was open for 1% -> 1% of each run, Pallas kernels for 7% -> 9%
where the time goes in v4:
time: 150 us; the launch traced here: 149 us
  waiting for transfers between devices  64.7 us (43%)
  starting transfers between devices  39.2 us (26%)
  Pallas kernels  25.1 us (17%)
  blocking collectives  14 us (9%)
  local copies, waits for them, and re-layouts  4.02 us (3%)
  other arithmetic  1.53 us (1%)
    all_to_all x1, waiting for transfers between devices, on_device(): lax.all_to_all(head_out.reshape(NY * NZ, -1, depth), ('y', 'z'), 0, 0)  14.1 us
    all_to_all x1, blocking collectives, on_device(): parts = lax.all_to_all(parts, ('y', 'x'), 0, 0)  14 us
    ppermute x6, waiting for transfers between devices, fetch(): return [v] + [lax.ppermute(v, axis, shift(n, -k)) for k in range(1, n)]  10.5 us
    all_to_all x1, waiting for transfers between devices, on_device(): out = lax.all_to_all(out.reshape(NY, -1, width), 'y', 0, 0)  10.1 us
    all_to_all x1, waiting for transfers between devices, on_device(): out = lax.all_to_all(out.reshape(NZ, rolls * steps, width), 'z', 0, 0)  9.96 us
    all_to_all x1, waiting for transfers between devices, on_device(): resid = lax.all_to_all(resid, 'z', 0, 0)  9.64 us
    all_to_all x1, starting transfers between devices, on_device(): lax.all_to_all(head_out.reshape(NY * NZ, -1, depth), ('y', 'z'), 0, 0)  9.47 us
    pallas_call x1, Pallas kernels, attend(): pl.pallas_call(lambda *refs: attend_kernel((NOPE + ROPE) ** (-0.5), *refs...  7.48 us
  transfers between devices with their start and end apart: 19, of which 12 were waited for; matrix products, arithmetic and copies ran while one was open for 1% of the time, Pallas kernels for 9%

profile of v4, /device:TPU:2, one launch (start us, length us, event | category | flops | bytes accessed | tf_op | source)
XLA Modules:
  0.0 148.8 jit_solution(16398185325769256162)
XLA Ops:
  0.0 0.0 collective-permute-start.1
  0.0 0.5 collective-permute-start.2
  0.5 0.0 collective-permute-start.3
  0.5 2.2 %cut.1 = bf16[4,112,1024]{2,1,0:T(8,128)(2,1)} custom-call(bf16[112,4096]{1,0:T(8,128)(2,1)} %bitcast.40), custom_call_target="tpu_custom_call" | custom-call | tf_op jit(solution)/shard_map/attend/cut/pallas_call | solution.py:127
  2.8 4.5 %all-to-all-start = ((bf16[4,112,1024]{2,1,0:T(8,128)(2,1)}), bf16[4,112,1024]{2,1,0:T(8,128)(2,1)S(1)}, u32[]{:S(2)}, u32[]{:S(2)}) async-start(bf16[4,112,1024]{2,1,0:T(8,128)(2,1)} %cut.1), calls=%async_computation | async-start | bytes 1835008 | tf_op jit(solution)/shard_map/attend/all_to_all | solution.py:414
  7.2 0.2 collective-permute-start
  7.5 7.5 %attend.1 = bf16[4,8,8,1024]{3,2,1,0:T(8,128)(2,1)} custom-call(s32[4]{0:T(128)} %refs_0_.1, bf16[4,2,32,576]{3,2,1,0:T(8,128)(2,1)} %refs_1_.1, bf16[4,2,576]{2,1,0:T(2,128)(2,1)} %refs_2_.1, bf16[4,576,1024]{2,1,0:T(8,128)(2,1)} %bitcast.38, bf16[32,512,128]{2,1,0:T(8,128)(2,1)} %refs_4_.1), custom_call_target="tpu_custom_call" | custom-call | tf_op jit(solution)/shard_map/attend/attend/pallas_call | solution.py:96
  15.0 0.0 copy-start.1
  15.0 0.0 collective-permute-done.refs_2_
  15.0 0.0 copy-start.4
  15.0 0.6 copy-done.4
  15.6 6.0 %all-to-all-done.w_own = bf16[4,112,1024]{2,1,0:T(8,128)(2,1)S(1)} async-done(((bf16[4,112,1024]{2,1,0:T(8,128)(2,1)}), bf16[4,112,1024]{2,1,0:T(8,128)(2,1)S(1)}, u32[]{:S(2)}, u32[]{:S(2)}) %all-to-all-start) | async-done | bytes 917536 | tf_op jit(solution)/shard_map/attend/all_to_all | solution.py:414
  21.6 0.0 collective-permute-done.1.refs_2_
  21.6 0.0 collective-permute-done.2.refs_3_
  21.6 0.0 collective-permute-done.3.w_alien
  21.6 9.5 %all-to-all-start.1 = ((bf16[32,8,1024]{2,1,0:T(8,128)(2,1)}), bf16[32,8,1024]{2,1,0:T(8,128)(2,1)S(1)}, u32[]{:S(2)}, u32[]{:S(2)}) async-start(bf16[32,8,1024]{2,1,0:T(8,128)(2,1)} %bitcast.39), calls=%async_computation.1 | async-start | bytes 1048576 | tf_op jit(solution)/shard_map/gather_heads/all_to_all | solution.py:423
  31.1 0.1 collective-permute-start.4
  31.2 0.1 pad_add_fusion.refs_0_.place
  31.3 0.9 copy-done.3
  32.2 0.9 copy-done.5
  33.1 0.8 stream.1.added
  33.9 0.0 collective-permute-done.4.w_alien
  33.9 14.1 %all-to-all-done.1 = bf16[32,8,1024]{2,1,0:T(8,128)(2,1)S(1)} async-done(((bf16[32,8,1024]{2,1,0:T(8,128)(2,1)}), bf16[32,8,1024]{2,1,0:T(8,128)(2,1)S(1)}, u32[]{:S(2)}, u32[]{:S(2)}) %all-to-all-start.1) | async-done | bytes 524320 | tf_op jit(solution)/shard_map/gather_heads/all_to_all | solution.py:423
  48.0 4.9 %project.1 = bf16[16,64,224]{2,1,0:T(8,128)(2,1)S(1)} custom-call(s32[4]{0:T(128)S(1)} %pad_add_fusion.refs_0_.place, bf16[256,1024]{1,0:T(8,128)(2,1)S(1)} %bitcast.31, bf16[4,112,1024]{2,1,0:T(8,128)(2,1)S(1)} %all-to-all-done.w_own, bf16[4,112,1024]{2,1,0:T(8,128)(2,1)} %collective-permute-done.4.w_alien, bf16[64,224]{1,0:T(8,128)(2,1)S(1)} %stream.1.added), custom_call_target="tpu_custom_call" | custom-call | tf_op jit(solution)/shard_map/project/project/pallas_call | solution.py:207
  53.0 14.0 %all_to_all.30.parts = bf16[16,64,224]{2,1,0:T(8,128)(2,1)S(1)} all-to-all(bf16[16,64,224]{2,1,0:T(8,128)(2,1)S(1)} %project.1), channel_id=1, replica_groups=mesh['y'=4,'z'=8,'c'=2,'x'=4] {'y','x'}, dimensions={0} | all-to-all | bytes 917504 | tf_op jit(solution)/shard_map/sum_heads/all_to_all | solution.py:430
  67.0 0.8 sum_heads.1
  67.8 4.9 %all-to-all-start.3 = ((bf16[8,64,224]{2,1,0:T(8,128)(2,1)}), bf16[8,64,224]{2,1,0:T(8,128)(2,1)S(1)}, u32[]{:S(2)}, u32[]{:S(2)}) async-start(bf16[8,64,224]{2,1,0:T(8,128)(2,1)} %sum_heads.1), calls=%async_computation.3 | async-start | bytes 524288 | tf_op jit(solution)/shard_map/gather_resid/all_to_all | solution.py:434
  72.7 0.8 dynamic-slice_convert_fusion
  73.5 0.1 reshape.35.gain
  73.5 9.6 %all-to-all-done.3.b0 = bf16[8,64,224]{2,1,0:T(8,128)(2,1)S(1)} async-done(((bf16[8,64,224]{2,1,0:T(8,128)(2,1)}), bf16[8,64,224]{2,1,0:T(8,128)(2,1)S(1)}, u32[]{:S(2)}, u32[]{:S(2)}) %all-to-all-start.3) | async-done | bytes 229408 | tf_op jit(solution)/shard_map/gather_resid/all_to_all | solution.py:434
  83.2 0.9 collective-permute-start.5
  84.0 1.0 collective-permute-start.6
  85.1 0.4 collective-permute-start.7
  85.5 0.0 copy-done.1
  85.5 0.0 copy-start.2
  85.5 1.2 copy-done.2
  86.7 2.3 %stacked.1.w = bf16[1152,1792]{1,0:T(8,128)(2,1)S(1)} custom-call(bf16[288,1792]{1,0:T(8,128)(2,1)S(1)} %bitcast.33, bf16[288,1792]{1,0:T(8,128)(2,1)S(1)} %bitcast.35, bf16[288,1792]{1,0:T(8,128)(2,1)} %collective-permute-done.1.refs_2_, bf16[288,1792]{1,0:T(8,128)(2,1)} %collective-permute-done.2.refs_3_), custom_call_target="tpu_custom_call" | custom-call | tf_op jit(solution)/shard_map/gather_resid/stacked/pallas_call | solution.py:256
  89.0 0.0 copy-start
  89.0 2.2 %collective-permute-done.5.b1 = bf16[8,64,224]{2,1,0:T(8,128)(2,1)S(1)} collective-permute-done((bf16[8,64,224]{2,1,0:T(8,128)(2,1)S(1)}, bf16[8,64,224]{2,1,0:T(8,128)(2,1)S(1)}, u32[]{:S(2)}, u32[]{:S(2)}) %collective-permute-start.5) | collective-permute-done | bytes 229408 | tf_op jit(solution)/shard_map/gather_resid/ppermute | solution.py:38
  91.3 2.2 %collective-permute-done.6.b2 = bf16[8,64,224]{2,1,0:T(8,128)(2,1)S(1)} collective-permute-done((bf16[8,64,224]{2,1,0:T(8,128)(2,1)S(1)}, bf16[8,64,224]{2,1,0:T(8,128)(2,1)S(1)}, u32[]{:S(2)}, u32[]{:S(2)}) %collective-permute-start.6) | collective-permute-done | bytes 229408 | tf_op jit(solution)/shard_map/gather_resid/ppermute | solution.py:38
  93.5 2.7 %collective-permute-done.7.b3 = bf16[8,64,224]{2,1,0:T(8,128)(2,1)S(1)} collective-permute-done((bf16[8,64,224]{2,1,0:T(8,128)(2,1)S(1)}, bf16[8,64,224]{2,1,0:T(8,128)(2,1)S(1)}, u32[]{:S(2)}, u32[]{:S(2)}) %collective-permute-start.7) | collective-permute-done | bytes 229408 | tf_op jit(solution)/shard_map/gather_resid/ppermute | solution.py:38
  96.1 2.2 %gate_up.1 = (bf16[64,1280]{1,0:T(8,128)(2,1)S(1)}, bf16[64,1280]{1,0:T(8,128)(2,1)S(1)}, bf16[64,1280]{1,0:T(8,128)(2,1)S(1)}, bf16[64,1280]{1,0:T(8,128)(2,1)S(1)}) custom-call(s32[4]{0:T(128)S(1)} %pad_add_fusion.refs_0_.place, f32[8,224]{1,0:T(8,128)S(1)} %reshape.35.gain, bf16[8,64,224]{2,1,0:T(8,128)(2,1)S(1)} %all-to-all-done.3.b0, ...), custom_call_target="tpu_custom_call" | custom-call | tf_op jit(solution)/shard_map/gate_up/gate_up/pallas_call | solution.py:296
  98.3 1.8 %collective-permute-start.10 = (bf16[64,1280]{1,0:T(8,128)(2,1)S(1)}, bf16[64,1280]{1,0:T(8,128)(2,1)S(1)}, u32[]{:S(2)}, u32[]{:S(2)}) collective-permute-start(bf16[64,1280]{1,0:T(8,128)(2,1)S(1)} %get-tuple-element.39), channel_id=1, source_target_pairs={{0,3},{1,0},{2,1},{3,2},{4,7},{5,4},{6,5},{7,6},{8,11},{9,8},{10,9... | collective-permute-start | bytes 491528 | tf_op jit(solution)/shard_map/sum_gate_up/ppermute | solution.py:447
  100.1 0.5 collective-permute-start.8
  100.6 2.4 %collective-permute-start.9 = (bf16[64,1280]{1,0:T(8,128)(2,1)S(1)}, bf16[64,1280]{1,0:T(8,128)(2,1)S(1)}, u32[]{:S(2)}, u32[]{:S(2)}) collective-permute-start(bf16[64,1280]{1,0:T(8,128)(2,1)S(1)} %get-tuple-element.38), channel_id=1, source_target_pairs={{0,2},{1,3},{2,0},{3,1},{4,6},{5,7},{6,4},{7,5},{8,10},{9,11},{10,... | collective-permute-start | bytes 491528 | tf_op jit(solution)/shard_map/sum_gate_up/ppermute | solution.py:447
  103.0 2.6 %collective-permute-done.10.refs_3_ = bf16[64,1280]{1,0:T(8,128)(2,1)S(1)} collective-permute-done((bf16[64,1280]{1,0:T(8,128)(2,1)S(1)}, bf16[64,1280]{1,0:T(8,128)(2,1)S(1)}, u32[]{:S(2)}, u32[]{:S(2)}) %collective-permute-start.10) | collective-permute-done | bytes 163872 | tf_op jit(solution)/shard_map/sum_gate_up/ppermute | solution.py:447
  105.6 0.4 collective-permute-done.8.refs_1_
  106.0 1.4 collective-permute-done.9.refs_2_
  107.4 0.2 activate.1.a0
  107.7 2.5 %collective-permute-start.11 = (bf16[64,576]{1,0:T(8,128)(2,1)S(1)}, bf16[64,576]{1,0:T(8,128)(2,1)S(1)}, u32[]{:S(2)}, u32[]{:S(2)}) collective-permute-start(bf16[64,576]{1,0:T(8,128)(2,1)S(1)} %activate.1.a0), channel_id=1, source_target_pairs={{0,3},{1,0},{2,1},{3,2},{4,7},{5,4},{6,5},{7,6},{8,11},{9,8},{10,9... | collective-permute-start | bytes 221192 | tf_op jit(solution)/shard_map/down/ppermute | solution.py:38
  110.2 0.8 collective-permute-start.12
  111.0 1.7 %collective-permute-start.13 = (bf16[64,576]{1,0:T(8,128)(2,1)S(1)}, bf16[64,576]{1,0:T(8,128)(2,1)S(1)}, u32[]{:S(2)}, u32[]{:S(2)}) collective-permute-start(bf16[64,576]{1,0:T(8,128)(2,1)S(1)} %activate.1.a0), channel_id=1, source_target_pairs={{0,1},{1,2},{2,3},{3,0},{4,5},{5,6},{6,7},{7,4},{8,9},{9,10},{10,1... | collective-permute-start | bytes 221192 | tf_op jit(solution)/shard_map/down/ppermute | solution.py:38
  112.8 0.0 collective-permute-done.11.a1
  112.8 3.4 %collective-permute-done.12.a2 = bf16[64,576]{1,0:T(8,128)(2,1)S(1)} collective-permute-done((bf16[64,576]{1,0:T(8,128)(2,1)S(1)}, bf16[64,576]{1,0:T(8,128)(2,1)S(1)}, u32[]{:S(2)}, u32[]{:S(2)}) %collective-permute-start.12) | collective-permute-done | bytes 73760 | tf_op jit(solution)/shard_map/down/ppermute | solution.py:38
  116.1 0.0 collective-permute-done.13.a3
  116.1 0.0 copy-done
  116.1 3.2 %down.1 = bf16[4,4,16,1792]{3,2,1,0:T(8,128)(2,1)} custom-call(s32[4]{0:T(128)S(1)} %pad_add_fusion.refs_0_.place, bf16[64,576]{1,0:T(8,128)(2,1)S(1)} %activate.1.a0, bf16[64,576]{1,0:T(8,128)(2,1)S(1)} %collective-permute-done.11.a1, bf16[64,576]{1,0:T(8,128)(2,1)S(1)} %collective-permute-done.12.a2, bf16[64,576]{1,0:T(8,128)(2,1)S(1)} %collective-permute-done.13.a3, ...), custom_call_target="tpu_custom_call" | custom-call | tf_op jit(solution)/shard_map/down/down/pallas_call | solution.py:358
  119.3 3.5 %all-to-all-start.4 = ((bf16[4,64,1792]{2,1,0:T(8,128)(2,1)}), bf16[4,64,1792]{2,1,0:T(8,128)(2,1)S(1)}, u32[]{:S(2)}, u32[]{:S(2)}) async-start(bf16[4,64,1792]{2,1,0:T(8,128)(2,1)} %bitcast.18), calls=%async_computation.4 | async-start | bytes 1835008 | tf_op jit(solution)/shard_map/sum_y/all_to_all | solution.py:455
  122.9 10.1 %all-to-all-done.4.parts = bf16[4,64,1792]{2,1,0:T(8,128)(2,1)S(1)} async-done(((bf16[4,64,1792]{2,1,0:T(8,128)(2,1)}), bf16[4,64,1792]{2,1,0:T(8,128)(2,1)S(1)}, u32[]{:S(2)}, u32[]{:S(2)}) %all-to-all-start.4) | async-done | bytes 917536 | tf_op jit(solution)/shard_map/sum_y/all_to_all | solution.py:455
  133.0 1.0 sum_y.1
  134.0 4.0 %all-to-all-start.5 = ((bf16[8,8,1792]{2,1,0:T(8,128)(2,1)}), bf16[8,8,1792]{2,1,0:T(8,128)(2,1)S(1)}, u32[]{:S(2)}, u32[]{:S(2)}) async-start(bf16[8,8,1792]{2,1,0:T(8,128)(2,1)} %bitcast.19), calls=%async_computation.5 | async-start | bytes 458752 | tf_op jit(solution)/shard_map/sum_z/all_to_all | solution.py:459
  138.0 0.1 reshape.33
  138.1 10.0 %all-to-all-done.5 = bf16[8,8,1792]{2,1,0:T(8,128)(2,1)S(1)} async-done(((bf16[8,8,1792]{2,1,0:T(8,128)(2,1)}), bf16[8,8,1792]{2,1,0:T(8,128)(2,1)S(1)}, u32[]{:S(2)}, u32[]{:S(2)}) %all-to-all-start.5) | async-done | bytes 229408 | tf_op jit(solution)/shard_map/sum_z/all_to_all | solution.py:459
  148.1 0.6 add_convert_fusion
  (17 shorter events, 0.2 us)
Async XLA Ops:
  0.0 21.6 %collective-permute-start.1 = (bf16[288,1792]{1,0:T(8,128)(2,1)}, bf16[288,1792]{1,0:T(8,128)(2,1)}, u32[]{:S(2)}, u32[]{:S(2)}) collective-permute-start(bf16[288,1792]{1,0:T(8,128)(2,1)} %bitcast.32), channel_id=1, source_target_pairs={{0,4},{4,0},{1,5},{5,1},{2,6},{6,2},{3,7},{7,3},{8,12},{12,8},{9,1... | collective-permute-start | bytes 3096584 | tf_op jit(solution)/shard_map/attend/ppermute | solution.py:410
  0.0 21.6 %collective-permute-start.2 = (bf16[288,1792]{1,0:T(8,128)(2,1)}, bf16[288,1792]{1,0:T(8,128)(2,1)}, u32[]{:S(2)}, u32[]{:S(2)}) collective-permute-start(bf16[288,1792]{1,0:T(8,128)(2,1)} %bitcast.34), channel_id=1, source_target_pairs={{0,4},{4,0},{1,5},{5,1},{2,6},{6,2},{3,7},{7,3},{8,12},{12,8},{9,1... | collective-permute-start | bytes 3096584 | tf_op jit(solution)/shard_map/attend/ppermute | solution.py:410
  0.5 21.1 %collective-permute-start.3 = (bf16[288,1792]{1,0:T(8,128)(2,1)}, bf16[288,1792]{1,0:T(8,128)(2,1)S(1)}, u32[]{:S(2)}, u32[]{:S(2)}) collective-permute-start(bf16[288,1792]{1,0:T(8,128)(2,1)} %w_own.1), channel_id=1, source_target_pairs={{0,4},{4,0},{1,5},{5,1},{2,6},{6,2},{3,7},{7,3},{8,12},{12,8},{9,1... | collective-permute-start | bytes 3096584 | tf_op jit(solution)/shard_map/attend/ppermute | solution.py:410
  2.8 18.8 %all-to-all-start = ((bf16[4,112,1024]{2,1,0:T(8,128)(2,1)}), bf16[4,112,1024]{2,1,0:T(8,128)(2,1)S(1)}, u32[]{:S(2)}, u32[]{:S(2)}) async-start(bf16[4,112,1024]{2,1,0:T(8,128)(2,1)} %cut.1), calls=%async_computation | async-start | bytes 1835008 | tf_op jit(solution)/shard_map/attend/all_to_all | solution.py:414
  7.2 7.7 %collective-permute-start = (bf16[224,256]{1,0:T(8,128)(2,1)}, bf16[224,256]{1,0:T(8,128)(2,1)S(1)}, u32[]{:S(2)}, u32[]{:S(2)}) collective-permute-start(bf16[224,256]{1,0:T(8,128)(2,1)} %bitcast.36), channel_id=1, source_target_pairs={{0,4},{4,0},{1,5},{5,1},{2,6},{6,2},{3,7},{7,3},{8,12},{12,8},{9,1... | collective-permute-start | bytes 344072 | tf_op jit(solution)/shard_map/attend/ppermute | solution.py:410
  15.0 70.5 %copy-start.1 = (bf16[1792,288]{0,1:T(8,128)(2,1)S(1)}, bf16[1792,288]{0,1:T(8,128)(2,1)}, u32[]{:S(2)}) copy-start(bf16[1792,288]{0,1:T(8,128)(2,1)} %param.19) | copy-start | bytes 3096580
  15.0 0.6 copy-start.4
  21.6 26.4 %all-to-all-start.1 = ((bf16[32,8,1024]{2,1,0:T(8,128)(2,1)}), bf16[32,8,1024]{2,1,0:T(8,128)(2,1)S(1)}, u32[]{:S(2)}, u32[]{:S(2)}) async-start(bf16[32,8,1024]{2,1,0:T(8,128)(2,1)} %bitcast.39), calls=%async_computation.1 | async-start | bytes 1048576 | tf_op jit(solution)/shard_map/gather_heads/all_to_all | solution.py:423
  31.1 2.8 %collective-permute-start.4 = (bf16[4,112,1024]{2,1,0:T(8,128)(2,1)S(1)}, bf16[4,112,1024]{2,1,0:T(8,128)(2,1)}, u32[]{:S(2)}, u32[]{:S(2)}) collective-permute-start(bf16[4,112,1024]{2,1,0:T(8,128)(2,1)S(1)} %all-to-all-done.w_own), channel_id=1, source_target_pairs={{0,4},{4,0},{1,5},{5,1},{2,6},{6,2},{3,7},{7,3},{8,12},{12,8},{9,1... | collective-permute-start | bytes 2752520 | tf_op jit(solution)/shard_map/gather_heads/ppermute | solution.py:410
  31.3 0.9 copy-start.3
  32.2 0.9 copy-start.5
  67.8 15.4 %all-to-all-start.3 = ((bf16[8,64,224]{2,1,0:T(8,128)(2,1)}), bf16[8,64,224]{2,1,0:T(8,128)(2,1)S(1)}, u32[]{:S(2)}, u32[]{:S(2)}) async-start(bf16[8,64,224]{2,1,0:T(8,128)(2,1)} %sum_heads.1), calls=%async_computation.3 | async-start | bytes 524288 | tf_op jit(solution)/shard_map/gather_resid/all_to_all | solution.py:434
  83.2 8.1 %collective-permute-start.5 = (bf16[8,64,224]{2,1,0:T(8,128)(2,1)S(1)}, bf16[8,64,224]{2,1,0:T(8,128)(2,1)S(1)}, u32[]{:S(2)}, u32[]{:S(2)}) collective-permute-start(bf16[8,64,224]{2,1,0:T(8,128)(2,1)S(1)} %all-to-all-done.3.b0), channel_id=1, source_target_pairs={{0,192},{64,0},{128,64},{192,128},{1,193},{65,1},{129,65},{193,129... | collective-permute-start | bytes 688136 | tf_op jit(solution)/shard_map/gather_resid/ppermute | solution.py:38
  84.0 9.5 %collective-permute-start.6 = (bf16[8,64,224]{2,1,0:T(8,128)(2,1)S(1)}, bf16[8,64,224]{2,1,0:T(8,128)(2,1)S(1)}, u32[]{:S(2)}, u32[]{:S(2)}) collective-permute-start(bf16[8,64,224]{2,1,0:T(8,128)(2,1)S(1)} %all-to-all-done.3.b0), channel_id=1, source_target_pairs={{0,128},{64,192},{128,0},{192,64},{1,129},{65,193},{129,1},{193,65... | collective-permute-start | bytes 688136 | tf_op jit(solution)/shard_map/gather_resid/ppermute | solution.py:38
  85.1 11.1 %collective-permute-start.7 = (bf16[8,64,224]{2,1,0:T(8,128)(2,1)S(1)}, bf16[8,64,224]{2,1,0:T(8,128)(2,1)S(1)}, u32[]{:S(2)}, u32[]{:S(2)}) collective-permute-start(bf16[8,64,224]{2,1,0:T(8,128)(2,1)S(1)} %all-to-all-done.3.b0), channel_id=1, source_target_pairs={{0,64},{64,128},{128,192},{192,0},{1,65},{65,129},{129,193},{193,1... | collective-permute-start | bytes 688136 | tf_op jit(solution)/shard_map/gather_resid/ppermute | solution.py:38
  85.5 1.2 copy-start.2
  89.0 27.1 %copy-start = (bf16[288,1792]{1,0:T(8,128)(2,1)S(1)}, bf16[288,1792]{1,0:T(8,128)(2,1)}, u32[]{:S(2)}) copy-start(bf16[288,1792]{1,0:T(8,128)(2,1)} %w_own.1) | copy-start | bytes 3096580
  98.3 7.3 %collective-permute-start.10 = (bf16[64,1280]{1,0:T(8,128)(2,1)S(1)}, bf16[64,1280]{1,0:T(8,128)(2,1)S(1)}, u32[]{:S(2)}, u32[]{:S(2)}) collective-permute-start(bf16[64,1280]{1,0:T(8,128)(2,1)S(1)} %get-tuple-element.39), channel_id=1, source_target_pairs={{0,3},{1,0},{2,1},{3,2},{4,7},{5,4},{6,5},{7,6},{8,11},{9,8},{10,9... | collective-permute-start | bytes 491528 | tf_op jit(solution)/shard_map/sum_gate_up/ppermute | solution.py:447
  100.1 6.0 %collective-permute-start.8 = (bf16[64,1280]{1,0:T(8,128)(2,1)S(1)}, bf16[64,1280]{1,0:T(8,128)(2,1)S(1)}, u32[]{:S(2)}, u32[]{:S(2)}) collective-permute-start(bf16[64,1280]{1,0:T(8,128)(2,1)S(1)} %get-tuple-element.37), channel_id=1, source_target_pairs={{0,1},{1,2},{2,3},{3,0},{4,5},{5,6},{6,7},{7,4},{8,9},{9,10},{10,1... | collective-permute-start | bytes 491528 | tf_op jit(solution)/shard_map/sum_gate_up/ppermute | solution.py:447
  100.6 6.8 %collective-permute-start.9 = (bf16[64,1280]{1,0:T(8,128)(2,1)S(1)}, bf16[64,1280]{1,0:T(8,128)(2,1)S(1)}, u32[]{:S(2)}, u32[]{:S(2)}) collective-permute-start(bf16[64,1280]{1,0:T(8,128)(2,1)S(1)} %get-tuple-element.38), channel_id=1, source_target_pairs={{0,2},{1,3},{2,0},{3,1},{4,6},{5,7},{6,4},{7,5},{8,10},{9,11},{10,... | collective-permute-start | bytes 491528 | tf_op jit(solution)/shard_map/sum_gate_up/ppermute | solution.py:447
  107.7 5.1 %collective-permute-start.11 = (bf16[64,576]{1,0:T(8,128)(2,1)S(1)}, bf16[64,576]{1,0:T(8,128)(2,1)S(1)}, u32[]{:S(2)}, u32[]{:S(2)}) collective-permute-start(bf16[64,576]{1,0:T(8,128)(2,1)S(1)} %activate.1.a0), channel_id=1, source_target_pairs={{0,3},{1,0},{2,1},{3,2},{4,7},{5,4},{6,5},{7,6},{8,11},{9,8},{10,9... | collective-permute-start | bytes 221192 | tf_op jit(solution)/shard_map/down/ppermute | solution.py:38
  110.2 5.9 %collective-permute-start.12 = (bf16[64,576]{1,0:T(8,128)(2,1)S(1)}, bf16[64,576]{1,0:T(8,128)(2,1)S(1)}, u32[]{:S(2)}, u32[]{:S(2)}) collective-permute-start(bf16[64,576]{1,0:T(8,128)(2,1)S(1)} %activate.1.a0), channel_id=1, source_target_pairs={{0,2},{1,3},{2,0},{3,1},{4,6},{5,7},{6,4},{7,5},{8,10},{9,11},{10,... | collective-permute-start | bytes 221192 | tf_op jit(solution)/shard_map/down/ppermute | solution.py:38
  111.0 5.1 %collective-permute-start.13 = (bf16[64,576]{1,0:T(8,128)(2,1)S(1)}, bf16[64,576]{1,0:T(8,128)(2,1)S(1)}, u32[]{:S(2)}, u32[]{:S(2)}) collective-permute-start(bf16[64,576]{1,0:T(8,128)(2,1)S(1)} %activate.1.a0), channel_id=1, source_target_pairs={{0,1},{1,2},{2,3},{3,0},{4,5},{5,6},{6,7},{7,4},{8,9},{9,10},{10,1... | collective-permute-start | bytes 221192 | tf_op jit(solution)/shard_map/down/ppermute | solution.py:38
  119.3 13.7 %all-to-all-start.4 = ((bf16[4,64,1792]{2,1,0:T(8,128)(2,1)}), bf16[4,64,1792]{2,1,0:T(8,128)(2,1)S(1)}, u32[]{:S(2)}, u32[]{:S(2)}) async-start(bf16[4,64,1792]{2,1,0:T(8,128)(2,1)} %bitcast.18), calls=%async_computation.4 | async-start | bytes 1835008 | tf_op jit(solution)/shard_map/sum_y/all_to_all | solution.py:455
  134.0 14.1 %all-to-all-start.5 = ((bf16[8,8,1792]{2,1,0:T(8,128)(2,1)}), bf16[8,8,1792]{2,1,0:T(8,128)(2,1)S(1)}, u32[]{:S(2)}, u32[]{:S(2)}) async-start(bf16[8,8,1792]{2,1,0:T(8,128)(2,1)} %bitcast.19), calls=%async_computation.5 | async-start | bytes 458752 | tf_op jit(solution)/shard_map/sum_z/all_to_all | solution.py:459

commit v5 on v4

--- a/solution.py
+++ b/solution.py
@@ -330,20 +330,11 @@
     )(*messages)
 
 
-def down_kernel(place, a0, a1, a2, a3, w_own, w_alien, out, act, w, sems):
-    hid = w_own.shape[0]
-    loads = [
-        pltpu.make_async_copy(v, w.at[pl.ds(n * hid, hid)], sems.at[n])
-        for n, v in enumerate((w_own, w_alien))
-    ]
-    for load in loads:
-        load.start()
+def down_kernel(place, a0, a1, a2, a3, w, out, act):
     x = place[3]
     rows = a0.shape[0]
     for n, a in enumerate((a0, a1, a2, a3)):
         act[n * rows : (n + 1) * rows] = a[...]
-    for load in loads:
-        load.wait()
     total = dot(act[...], w[...]).astype(BF16)
     part = rows // NY
     for n in range(NX):
@@ -352,22 +343,20 @@
             out[b, (x + n) & 3] = total[start : start + part]
 
 
-def down(place, blocks, weights):
+def down(place, blocks, w):
     rows = blocks[0].shape[0]
-    hid, width = weights[0].shape
+    units, width = w.shape
     return pl.pallas_call(
         down_kernel,
         out_shape=jax.ShapeDtypeStruct((NY, NX, rows // NY, width), BF16),
-        in_specs=[SMEM] + [VMEM] * NX + [HBM] * NC,
+        in_specs=[SMEM] + [VMEM] * (NX + 1),
         out_specs=VMEM,
         scratch_shapes=[
-            pltpu.VMEM((NX * rows, NC * hid), BF16),
-            pltpu.VMEM((NC * hid, width), BF16),
-            pltpu.SemaphoreType.DMA((NC,)),
+            pltpu.VMEM((NX * rows, units), BF16),
         ],
         compiler_params=SMALL,
         name="down",
-    )(place, *blocks, *weights)
+    )(place, *blocks, w)
 
 
 def sum_y_kernel(parts, out):
@@ -449,7 +438,9 @@
         act = activate(messages, NX * width, hid)
 
     with jax.named_scope("down"):
-        out = down(place, fetch(act, "x", NX), (w_down, w_down_alien))
+        act, ready = lax.optimization_barrier((act, (w_down, w_down_alien)))
+        act = fetch(act, "x", NX)
+        out = down(place, act, stacked(ready))
 
     with jax.named_scope("sum_y"):
         out = lax.all_to_all(out.reshape(NY, -1, width), "y", 0, 0)

time: 150 us -> 149 us (level)
  waiting for transfers between devices: 64.7 us -> 63.2 us
    pallas_call x1 -> x2, Pallas kernels: 2.3 us -> 3.05 us  [stacked(): pl.pallas_call(lambda *refs: stacked_kernel(len(parts), *refs), out_shape...]
    unnamed x19 -> x21, local copies, waits for them, and re-layouts: 3.7 us -> 3.71 us
where the time goes in v5:
time: 149 us; the launch traced here: 148 us
  waiting for transfers between devices  63.2 us (42%)
  starting transfers between devices  39.2 us (26%)
  Pallas kernels  25 us (17%)
  blocking collectives  14 us (9%)
  local copies, waits for them, and re-layouts  4.78 us (3%)
  other arithmetic  1.53 us (1%)
    all_to_all x1, waiting for transfers between devices, on_device(): lax.all_to_all(head_out.reshape(NY * NZ, -1, depth), ('y', 'z'), 0, 0)  14.1 us
    all_to_all x1, blocking collectives, on_device(): parts = lax.all_to_all(parts, ('y', 'x'), 0, 0)  14 us
    all_to_all x1, waiting for transfers between devices, on_device(): out = lax.all_to_all(out.reshape(NZ, rolls * steps, width), 'z', 0, 0)  9.96 us
    ppermute x6, waiting for transfers between devices, fetch(): return [v] + [lax.ppermute(v, axis, shift(n, -k)) for k in range(1, n)]  9.72 us
    all_to_all x1, waiting for transfers between devices, on_device(): resid = lax.all_to_all(resid, 'z', 0, 0)  9.64 us
    all_to_all x1, starting transfers between devices, on_device(): lax.all_to_all(head_out.reshape(NY * NZ, -1, depth), ('y', 'z'), 0, 0)  9.47 us
    all_to_all x1, waiting for transfers between devices, on_device(): out = lax.all_to_all(out.reshape(NY, -1, width), 'y', 0, 0)  9.34 us
    pallas_call x1, Pallas kernels, attend(): pl.pallas_call(lambda *refs: attend_kernel((NOPE + ROPE) ** (-0.5), *refs...  7.47 us
  transfers between devices with their start and end apart: 19, of which 12 were waited for; matrix products, arithmetic and copies ran while one was open for 1% of the time, Pallas kernels for 9%

profile of v5, /device:TPU:2, one launch (start us, length us, event | category | flops | bytes accessed | tf_op | source)
XLA Modules:
  0.0 147.9 jit_solution(1195865008941079631)
XLA Ops:
  0.0 0.0 collective-permute-start.1
  0.0 0.5 collective-permute-start.2
  0.5 0.0 collective-permute-start.3
  0.5 2.2 %cut.1 = bf16[4,112,1024]{2,1,0:T(8,128)(2,1)} custom-call(bf16[112,4096]{1,0:T(8,128)(2,1)} %bitcast.40), custom_call_target="tpu_custom_call" | custom-call | tf_op jit(solution)/shard_map/attend/cut/pallas_call | solution.py:127
  2.8 4.5 %all-to-all-start = ((bf16[4,112,1024]{2,1,0:T(8,128)(2,1)}), bf16[4,112,1024]{2,1,0:T(8,128)(2,1)S(1)}, u32[]{:S(2)}, u32[]{:S(2)}) async-start(bf16[4,112,1024]{2,1,0:T(8,128)(2,1)} %cut.1), calls=%async_computation | async-start | bytes 1835008 | tf_op jit(solution)/shard_map/attend/all_to_all | solution.py:403
  7.2 0.2 collective-permute-start
  7.5 7.5 %attend.1 = bf16[4,8,8,1024]{3,2,1,0:T(8,128)(2,1)} custom-call(s32[4]{0:T(128)} %refs_0_.1, bf16[4,2,32,576]{3,2,1,0:T(8,128)(2,1)} %refs_1_.1, bf16[4,2,576]{2,1,0:T(2,128)(2,1)} %refs_2_.1, bf16[4,576,1024]{2,1,0:T(8,128)(2,1)} %bitcast.38, bf16[32,512,128]{2,1,0:T(8,128)(2,1)} %refs_4_.1), custom_call_target="tpu_custom_call" | custom-call | tf_op jit(solution)/shard_map/attend/attend/pallas_call | solution.py:96
  14.9 0.0 copy-start.1
  15.0 0.0 collective-permute-done.refs_2_
  15.0 0.6 copy-done.5
  15.6 6.0 %all-to-all-done.w_own = bf16[4,112,1024]{2,1,0:T(8,128)(2,1)S(1)} async-done(((bf16[4,112,1024]{2,1,0:T(8,128)(2,1)}), bf16[4,112,1024]{2,1,0:T(8,128)(2,1)S(1)}, u32[]{:S(2)}, u32[]{:S(2)}) %all-to-all-start) | async-done | bytes 917536 | tf_op jit(solution)/shard_map/attend/all_to_all | solution.py:403
  21.6 0.0 collective-permute-done.1.refs_2_
  21.6 0.0 collective-permute-done.2.refs_3_
  21.6 0.0 collective-permute-done.3.refs_1_
  21.6 9.5 %all-to-all-start.1 = ((bf16[32,8,1024]{2,1,0:T(8,128)(2,1)}), bf16[32,8,1024]{2,1,0:T(8,128)(2,1)S(1)}, u32[]{:S(2)}, u32[]{:S(2)}) async-start(bf16[32,8,1024]{2,1,0:T(8,128)(2,1)} %bitcast.39), calls=%async_computation.1 | async-start | bytes 1048576 | tf_op jit(solution)/shard_map/gather_heads/all_to_all | solution.py:412
  31.1 0.1 collective-permute-start.4
  31.2 0.1 pad_add_fusion.refs_0_.place
  31.3 0.9 copy-done.4
  32.2 0.9 copy-done.6
  33.1 0.8 stream.1.added
  33.9 0.0 collective-permute-done.4.w_alien
  33.9 14.1 %all-to-all-done.1 = bf16[32,8,1024]{2,1,0:T(8,128)(2,1)S(1)} async-done(((bf16[32,8,1024]{2,1,0:T(8,128)(2,1)}), bf16[32,8,1024]{2,1,0:T(8,128)(2,1)S(1)}, u32[]{:S(2)}, u32[]{:S(2)}) %all-to-all-start.1) | async-done | bytes 524320 | tf_op jit(solution)/shard_map/gather_heads/all_to_all | solution.py:412
  48.0 4.9 %project.1 = bf16[16,64,224]{2,1,0:T(8,128)(2,1)S(1)} custom-call(s32[4]{0:T(128)S(1)} %pad_add_fusion.refs_0_.place, bf16[256,1024]{1,0:T(8,128)(2,1)S(1)} %bitcast.31, bf16[4,112,1024]{2,1,0:T(8,128)(2,1)S(1)} %all-to-all-done.w_own, bf16[4,112,1024]{2,1,0:T(8,128)(2,1)} %collective-permute-done.4.w_alien, bf16[64,224]{1,0:T(8,128)(2,1)S(1)} %stream.1.added), custom_call_target="tpu_custom_call" | custom-call | tf_op jit(solution)/shard_map/project/project/pallas_call | solution.py:207
  53.0 14.0 %all_to_all.30.parts = bf16[16,64,224]{2,1,0:T(8,128)(2,1)S(1)} all-to-all(bf16[16,64,224]{2,1,0:T(8,128)(2,1)S(1)} %project.1), channel_id=1, replica_groups=mesh['y'=4,'z'=8,'c'=2,'x'=4] {'y','x'}, dimensions={0} | all-to-all | bytes 917504 | tf_op jit(solution)/shard_map/sum_heads/all_to_all | solution.py:419
  67.0 0.8 sum_heads.1
  67.7 4.9 %all-to-all-start.3 = ((bf16[8,64,224]{2,1,0:T(8,128)(2,1)}), bf16[8,64,224]{2,1,0:T(8,128)(2,1)S(1)}, u32[]{:S(2)}, u32[]{:S(2)}) async-start(bf16[8,64,224]{2,1,0:T(8,128)(2,1)} %sum_heads.1), calls=%async_computation.3 | async-start | bytes 524288 | tf_op jit(solution)/shard_map/gather_resid/all_to_all | solution.py:423
  72.7 0.8 dynamic-slice_convert_fusion
  73.4 0.1 reshape.35.gain
  73.5 9.6 %all-to-all-done.3.b0 = bf16[8,64,224]{2,1,0:T(8,128)(2,1)S(1)} async-done(((bf16[8,64,224]{2,1,0:T(8,128)(2,1)}), bf16[8,64,224]{2,1,0:T(8,128)(2,1)S(1)}, u32[]{:S(2)}, u32[]{:S(2)}) %all-to-all-start.3) | async-done | bytes 229408 | tf_op jit(solution)/shard_map/gather_resid/all_to_all | solution.py:423
  83.2 0.9 collective-permute-start.5
  84.0 1.0 collective-permute-start.6
  85.0 0.4 collective-permute-start.7
  85.4 0.0 copy-done.1
  85.5 0.0 copy-start.2
  85.5 1.2 copy-done.2
  86.7 2.3 %stacked.2.w = bf16[1152,1792]{1,0:T(8,128)(2,1)S(1)} custom-call(bf16[288,1792]{1,0:T(8,128)(2,1)S(1)} %bitcast.33, bf16[288,1792]{1,0:T(8,128)(2,1)S(1)} %bitcast.35, bf16[288,1792]{1,0:T(8,128)(2,1)} %collective-permute-done.1.refs_2_, bf16[288,1792]{1,0:T(8,128)(2,1)} %collective-permute-done.2.refs_3_), custom_call_target="tpu_custom_call" | custom-call | tf_op jit(solution)/shard_map/gather_resid/stacked/pallas_call | solution.py:256
  89.0 0.0 copy-start
  89.0 2.2 %collective-permute-done.5.b1 = bf16[8,64,224]{2,1,0:T(8,128)(2,1)S(1)} collective-permute-done((bf16[8,64,224]{2,1,0:T(8,128)(2,1)S(1)}, bf16[8,64,224]{2,1,0:T(8,128)(2,1)S(1)}, u32[]{:S(2)}, u32[]{:S(2)}) %collective-permute-start.5) | collective-permute-done | bytes 229408 | tf_op jit(solution)/shard_map/gather_resid/ppermute | solution.py:38
  91.3 2.2 %collective-permute-done.6.b2 = bf16[8,64,224]{2,1,0:T(8,128)(2,1)S(1)} collective-permute-done((bf16[8,64,224]{2,1,0:T(8,128)(2,1)S(1)}, bf16[8,64,224]{2,1,0:T(8,128)(2,1)S(1)}, u32[]{:S(2)}, u32[]{:S(2)}) %collective-permute-start.6) | collective-permute-done | bytes 229408 | tf_op jit(solution)/shard_map/gather_resid/ppermute | solution.py:38
  93.5 2.7 %collective-permute-done.7.b3 = bf16[8,64,224]{2,1,0:T(8,128)(2,1)S(1)} collective-permute-done((bf16[8,64,224]{2,1,0:T(8,128)(2,1)S(1)}, bf16[8,64,224]{2,1,0:T(8,128)(2,1)S(1)}, u32[]{:S(2)}, u32[]{:S(2)}) %collective-permute-start.7) | collective-permute-done | bytes 229408 | tf_op jit(solution)/shard_map/gather_resid/ppermute | solution.py:38
  96.1 2.2 %gate_up.1 = (bf16[64,1280]{1,0:T(8,128)(2,1)S(1)}, bf16[64,1280]{1,0:T(8,128)(2,1)S(1)}, bf16[64,1280]{1,0:T(8,128)(2,1)S(1)}, bf16[64,1280]{1,0:T(8,128)(2,1)S(1)}) custom-call(s32[4]{0:T(128)S(1)} %pad_add_fusion.refs_0_.place, f32[8,224]{1,0:T(8,128)S(1)} %reshape.35.gain, bf16[8,64,224]{2,1,0:T(8,128)(2,1)S(1)} %all-to-all-done.3.b0, ...), custom_call_target="tpu_custom_call" | custom-call | tf_op jit(solution)/shard_map/gate_up/gate_up/pallas_call | solution.py:296
  98.3 1.8 %collective-permute-start.10 = (bf16[64,1280]{1,0:T(8,128)(2,1)S(1)}, bf16[64,1280]{1,0:T(8,128)(2,1)S(1)}, u32[]{:S(2)}, u32[]{:S(2)}) collective-permute-start(bf16[64,1280]{1,0:T(8,128)(2,1)S(1)} %get-tuple-element.42), channel_id=1, source_target_pairs={{0,3},{1,0},{2,1},{3,2},{4,7},{5,4},{6,5},{7,6},{8,11},{9,8},{10,9... | collective-permute-start | bytes 491528 | tf_op jit(solution)/shard_map/sum_gate_up/ppermute | solution.py:436
  100.0 0.5 collective-permute-start.8
  100.6 2.4 %collective-permute-start.9 = (bf16[64,1280]{1,0:T(8,128)(2,1)S(1)}, bf16[64,1280]{1,0:T(8,128)(2,1)S(1)}, u32[]{:S(2)}, u32[]{:S(2)}) collective-permute-start(bf16[64,1280]{1,0:T(8,128)(2,1)S(1)} %get-tuple-element.41), channel_id=1, source_target_pairs={{0,2},{1,3},{2,0},{3,1},{4,6},{5,7},{6,4},{7,5},{8,10},{9,11},{10,... | collective-permute-start | bytes 491528 | tf_op jit(solution)/shard_map/sum_gate_up/ppermute | solution.py:436
  103.0 2.6 %collective-permute-done.10.refs_3_ = bf16[64,1280]{1,0:T(8,128)(2,1)S(1)} collective-permute-done((bf16[64,1280]{1,0:T(8,128)(2,1)S(1)}, bf16[64,1280]{1,0:T(8,128)(2,1)S(1)}, u32[]{:S(2)}, u32[]{:S(2)}) %collective-permute-start.10) | collective-permute-done | bytes 163872 | tf_op jit(solution)/shard_map/sum_gate_up/ppermute | solution.py:436
  105.6 0.4 collective-permute-done.8.refs_1_
  106.0 1.4 collective-permute-done.9.refs_2_
  107.4 0.2 activate.1.a0
  107.6 2.5 %collective-permute-start.11 = (bf16[64,576]{1,0:T(8,128)(2,1)S(1)}, bf16[64,576]{1,0:T(8,128)(2,1)S(1)}, u32[]{:S(2)}, u32[]{:S(2)}) collective-permute-start(bf16[64,576]{1,0:T(8,128)(2,1)S(1)} %activate.1.a0), channel_id=1, source_target_pairs={{0,3},{1,0},{2,1},{3,2},{4,7},{5,4},{6,5},{7,6},{8,11},{9,8},{10,9... | collective-permute-start | bytes 221192 | tf_op jit(solution)/shard_map/down/ppermute | solution.py:38
  110.2 0.9 collective-permute-start.12
  111.0 1.7 %collective-permute-start.13 = (bf16[64,576]{1,0:T(8,128)(2,1)S(1)}, bf16[64,576]{1,0:T(8,128)(2,1)S(1)}, u32[]{:S(2)}, u32[]{:S(2)}) collective-permute-start(bf16[64,576]{1,0:T(8,128)(2,1)S(1)} %activate.1.a0), channel_id=1, source_target_pairs={{0,1},{1,2},{2,3},{3,0},{4,5},{5,6},{6,7},{7,4},{8,9},{9,10},{10,1... | collective-permute-start | bytes 221192 | tf_op jit(solution)/shard_map/down/ppermute | solution.py:38
  112.7 0.8 stacked.3.w
  113.5 0.0 collective-permute-done.11.a1
  113.5 2.6 %collective-permute-done.12.a2 = bf16[64,576]{1,0:T(8,128)(2,1)S(1)} collective-permute-done((bf16[64,576]{1,0:T(8,128)(2,1)S(1)}, bf16[64,576]{1,0:T(8,128)(2,1)S(1)}, u32[]{:S(2)}, u32[]{:S(2)}) %collective-permute-start.12) | collective-permute-done | bytes 73760 | tf_op jit(solution)/shard_map/down/ppermute | solution.py:38
  116.1 0.0 collective-permute-done.13.a3
  116.1 2.4 %down.1 = bf16[4,4,16,1792]{3,2,1,0:T(8,128)(2,1)} custom-call(s32[4]{0:T(128)S(1)} %pad_add_fusion.refs_0_.place, bf16[64,576]{1,0:T(8,128)(2,1)S(1)} %activate.1.a0, bf16[64,576]{1,0:T(8,128)(2,1)S(1)} %collective-permute-done.11.a1, bf16[64,576]{1,0:T(8,128)(2,1)S(1)} %collective-permute-done.12.a2, bf16[64,576]{1,0:T(8,128)(2,1)S(1)} %collective-permute-done.13.a3, ...), custom_call_target="tpu_custom_call" | custom-call | tf_op jit(solution)/shard_map/down/down/pallas_call | solution.py:349
  118.5 3.5 %all-to-all-start.4 = ((bf16[4,64,1792]{2,1,0:T(8,128)(2,1)}), bf16[4,64,1792]{2,1,0:T(8,128)(2,1)S(1)}, u32[]{:S(2)}, u32[]{:S(2)}) async-start(bf16[4,64,1792]{2,1,0:T(8,128)(2,1)} %bitcast.18), calls=%async_computation.4 | async-start | bytes 1835008 | tf_op jit(solution)/shard_map/sum_y/all_to_all | solution.py:446
  122.0 0.8 constant_dynamic-slice_fusion
  122.8 9.3 %all-to-all-done.4.parts = bf16[4,64,1792]{2,1,0:T(8,128)(2,1)S(1)} async-done(((bf16[4,64,1792]{2,1,0:T(8,128)(2,1)}), bf16[4,64,1792]{2,1,0:T(8,128)(2,1)S(1)}, u32[]{:S(2)}, u32[]{:S(2)}) %all-to-all-start.4) | async-done | bytes 917536 | tf_op jit(solution)/shard_map/sum_y/all_to_all | solution.py:446
  132.2 1.0 sum_y.1
  133.1 4.0 %all-to-all-start.5 = ((bf16[8,8,1792]{2,1,0:T(8,128)(2,1)}), bf16[8,8,1792]{2,1,0:T(8,128)(2,1)S(1)}, u32[]{:S(2)}, u32[]{:S(2)}) async-start(bf16[8,8,1792]{2,1,0:T(8,128)(2,1)} %bitcast.19), calls=%async_computation.5 | async-start | bytes 458752 | tf_op jit(solution)/shard_map/sum_z/all_to_all | solution.py:450
  137.1 0.1 reshape.33
  137.3 10.0 %all-to-all-done.5 = bf16[8,8,1792]{2,1,0:T(8,128)(2,1)S(1)} async-done(((bf16[8,8,1792]{2,1,0:T(8,128)(2,1)}), bf16[8,8,1792]{2,1,0:T(8,128)(2,1)S(1)}, u32[]{:S(2)}, u32[]{:S(2)}) %all-to-all-start.5) | async-done | bytes 229408 | tf_op jit(solution)/shard_map/sum_z/all_to_all | solution.py:450
  147.3 0.6 add_convert_fusion
  (20 shorter events, 0.2 us)
Async XLA Ops:
  0.0 21.6 %collective-permute-start.1 = (bf16[288,1792]{1,0:T(8,128)(2,1)}, bf16[288,1792]{1,0:T(8,128)(2,1)}, u32[]{:S(2)}, u32[]{:S(2)}) collective-permute-start(bf16[288,1792]{1,0:T(8,128)(2,1)} %bitcast.32), channel_id=1, source_target_pairs={{0,4},{4,0},{1,5},{5,1},{2,6},{6,2},{3,7},{7,3},{8,12},{12,8},{9,1... | collective-permute-start | bytes 3096584 | tf_op jit(solution)/shard_map/attend/ppermute | solution.py:399
  0.0 21.6 %collective-permute-start.2 = (bf16[288,1792]{1,0:T(8,128)(2,1)}, bf16[288,1792]{1,0:T(8,128)(2,1)}, u32[]{:S(2)}, u32[]{:S(2)}) collective-permute-start(bf16[288,1792]{1,0:T(8,128)(2,1)} %bitcast.34), channel_id=1, source_target_pairs={{0,4},{4,0},{1,5},{5,1},{2,6},{6,2},{3,7},{7,3},{8,12},{12,8},{9,1... | collective-permute-start | bytes 3096584 | tf_op jit(solution)/shard_map/attend/ppermute | solution.py:399
  0.5 21.1 %collective-permute-start.3 = (bf16[288,1792]{1,0:T(8,128)(2,1)}, bf16[288,1792]{1,0:T(8,128)(2,1)S(1)}, u32[]{:S(2)}, u32[]{:S(2)}) collective-permute-start(bf16[288,1792]{1,0:T(8,128)(2,1)} %refs_0_.2), channel_id=1, source_target_pairs={{0,4},{4,0},{1,5},{5,1},{2,6},{6,2},{3,7},{7,3},{8,12},{12,8},{9,1... | collective-permute-start | bytes 3096584 | tf_op jit(solution)/shard_map/attend/ppermute | solution.py:399
  2.8 18.8 %all-to-all-start = ((bf16[4,112,1024]{2,1,0:T(8,128)(2,1)}), bf16[4,112,1024]{2,1,0:T(8,128)(2,1)S(1)}, u32[]{:S(2)}, u32[]{:S(2)}) async-start(bf16[4,112,1024]{2,1,0:T(8,128)(2,1)} %cut.1), calls=%async_computation | async-start | bytes 1835008 | tf_op jit(solution)/shard_map/attend/all_to_all | solution.py:403
  7.2 7.7 %collective-permute-start = (bf16[224,256]{1,0:T(8,128)(2,1)}, bf16[224,256]{1,0:T(8,128)(2,1)S(1)}, u32[]{:S(2)}, u32[]{:S(2)}) collective-permute-start(bf16[224,256]{1,0:T(8,128)(2,1)} %bitcast.36), channel_id=1, source_target_pairs={{0,4},{4,0},{1,5},{5,1},{2,6},{6,2},{3,7},{7,3},{8,12},{12,8},{9,1... | collective-permute-start | bytes 344072 | tf_op jit(solution)/shard_map/attend/ppermute | solution.py:399
  14.9 70.5 %copy-start.1 = (bf16[1792,288]{0,1:T(8,128)(2,1)S(1)}, bf16[1792,288]{0,1:T(8,128)(2,1)}, u32[]{:S(2)}) copy-start(bf16[1792,288]{0,1:T(8,128)(2,1)} %param.19) | copy-start | bytes 3096580
  15.0 0.7 copy-start.5
  21.6 26.4 %all-to-all-start.1 = ((bf16[32,8,1024]{2,1,0:T(8,128)(2,1)}), bf16[32,8,1024]{2,1,0:T(8,128)(2,1)S(1)}, u32[]{:S(2)}, u32[]{:S(2)}) async-start(bf16[32,8,1024]{2,1,0:T(8,128)(2,1)} %bitcast.39), calls=%async_computation.1 | async-start | bytes 1048576 | tf_op jit(solution)/shard_map/gather_heads/all_to_all | solution.py:412
  31.1 2.8 %collective-permute-start.4 = (bf16[4,112,1024]{2,1,0:T(8,128)(2,1)S(1)}, bf16[4,112,1024]{2,1,0:T(8,128)(2,1)}, u32[]{:S(2)}, u32[]{:S(2)}) collective-permute-start(bf16[4,112,1024]{2,1,0:T(8,128)(2,1)S(1)} %all-to-all-done.w_own), channel_id=1, source_target_pairs={{0,4},{4,0},{1,5},{5,1},{2,6},{6,2},{3,7},{7,3},{8,12},{12,8},{9,1... | collective-permute-start | bytes 2752520 | tf_op jit(solution)/shard_map/gather_heads/ppermute | solution.py:399
  31.3 0.9 copy-start.4
  32.2 0.9 copy-start.6
  67.7 15.4 %all-to-all-start.3 = ((bf16[8,64,224]{2,1,0:T(8,128)(2,1)}), bf16[8,64,224]{2,1,0:T(8,128)(2,1)S(1)}, u32[]{:S(2)}, u32[]{:S(2)}) async-start(bf16[8,64,224]{2,1,0:T(8,128)(2,1)} %sum_heads.1), calls=%async_computation.3 | async-start | bytes 524288 | tf_op jit(solution)/shard_map/gather_resid/all_to_all | solution.py:423
  83.2 8.1 %collective-permute-start.5 = (bf16[8,64,224]{2,1,0:T(8,128)(2,1)S(1)}, bf16[8,64,224]{2,1,0:T(8,128)(2,1)S(1)}, u32[]{:S(2)}, u32[]{:S(2)}) collective-permute-start(bf16[8,64,224]{2,1,0:T(8,128)(2,1)S(1)} %all-to-all-done.3.b0), channel_id=1, source_target_pairs={{0,192},{64,0},{128,64},{192,128},{1,193},{65,1},{129,65},{193,129... | collective-permute-start | bytes 688136 | tf_op jit(solution)/shard_map/gather_resid/ppermute | solution.py:38
  84.0 9.5 %collective-permute-start.6 = (bf16[8,64,224]{2,1,0:T(8,128)(2,1)S(1)}, bf16[8,64,224]{2,1,0:T(8,128)(2,1)S(1)}, u32[]{:S(2)}, u32[]{:S(2)}) collective-permute-start(bf16[8,64,224]{2,1,0:T(8,128)(2,1)S(1)} %all-to-all-done.3.b0), channel_id=1, source_target_pairs={{0,128},{64,192},{128,0},{192,64},{1,129},{65,193},{129,1},{193,65... | collective-permute-start | bytes 688136 | tf_op jit(solution)/shard_map/gather_resid/ppermute | solution.py:38
  85.0 11.1 %collective-permute-start.7 = (bf16[8,64,224]{2,1,0:T(8,128)(2,1)S(1)}, bf16[8,64,224]{2,1,0:T(8,128)(2,1)S(1)}, u32[]{:S(2)}, u32[]{:S(2)}) collective-permute-start(bf16[8,64,224]{2,1,0:T(8,128)(2,1)S(1)} %all-to-all-done.3.b0), channel_id=1, source_target_pairs={{0,64},{64,128},{128,192},{192,0},{1,65},{65,129},{129,193},{193,1... | collective-permute-start | bytes 688136 | tf_op jit(solution)/shard_map/gather_resid/ppermute | solution.py:38
  85.5 1.2 copy-start.2
  89.0 23.8 %copy-start = (bf16[288,1792]{1,0:T(8,128)(2,1)S(1)}, bf16[288,1792]{1,0:T(8,128)(2,1)}, u32[]{:S(2)}) copy-start(bf16[288,1792]{1,0:T(8,128)(2,1)} %refs_0_.2) | copy-start | bytes 3096580
  96.1 11.3 %copy-start.3 = (bf16[8,64,224]{2,1,0:T(8,128)(2,1)}, bf16[8,64,224]{2,1,0:T(8,128)(2,1)S(1)}, u32[]{:S(2)}) copy-start(bf16[8,64,224]{2,1,0:T(8,128)(2,1)S(1)} %collective-permute-done.7.b3) | copy-start | bytes 688132
  98.3 7.3 %collective-permute-start.10 = (bf16[64,1280]{1,0:T(8,128)(2,1)S(1)}, bf16[64,1280]{1,0:T(8,128)(2,1)S(1)}, u32[]{:S(2)}, u32[]{:S(2)}) collective-permute-start(bf16[64,1280]{1,0:T(8,128)(2,1)S(1)} %get-tuple-element.42), channel_id=1, source_target_pairs={{0,3},{1,0},{2,1},{3,2},{4,7},{5,4},{6,5},{7,6},{8,11},{9,8},{10,9... | collective-permute-start | bytes 491528 | tf_op jit(solution)/shard_map/sum_gate_up/ppermute | solution.py:436
  100.0 6.0 %collective-permute-start.8 = (bf16[64,1280]{1,0:T(8,128)(2,1)S(1)}, bf16[64,1280]{1,0:T(8,128)(2,1)S(1)}, u32[]{:S(2)}, u32[]{:S(2)}) collective-permute-start(bf16[64,1280]{1,0:T(8,128)(2,1)S(1)} %get-tuple-element.40), channel_id=1, source_target_pairs={{0,1},{1,2},{2,3},{3,0},{4,5},{5,6},{6,7},{7,4},{8,9},{9,10},{10,1... | collective-permute-start | bytes 491528 | tf_op jit(solution)/shard_map/sum_gate_up/ppermute | solution.py:436
  100.6 6.8 %collective-permute-start.9 = (bf16[64,1280]{1,0:T(8,128)(2,1)S(1)}, bf16[64,1280]{1,0:T(8,128)(2,1)S(1)}, u32[]{:S(2)}, u32[]{:S(2)}) collective-permute-start(bf16[64,1280]{1,0:T(8,128)(2,1)S(1)} %get-tuple-element.41), channel_id=1, source_target_pairs={{0,2},{1,3},{2,0},{3,1},{4,6},{5,7},{6,4},{7,5},{8,10},{9,11},{10,... | collective-permute-start | bytes 491528 | tf_op jit(solution)/shard_map/sum_gate_up/ppermute | solution.py:436
  107.6 5.9 %collective-permute-start.11 = (bf16[64,576]{1,0:T(8,128)(2,1)S(1)}, bf16[64,576]{1,0:T(8,128)(2,1)S(1)}, u32[]{:S(2)}, u32[]{:S(2)}) collective-permute-start(bf16[64,576]{1,0:T(8,128)(2,1)S(1)} %activate.1.a0), channel_id=1, source_target_pairs={{0,3},{1,0},{2,1},{3,2},{4,7},{5,4},{6,5},{7,6},{8,11},{9,8},{10,9... | collective-permute-start | bytes 221192 | tf_op jit(solution)/shard_map/down/ppermute | solution.py:38
  110.2 5.9 %collective-permute-start.12 = (bf16[64,576]{1,0:T(8,128)(2,1)S(1)}, bf16[64,576]{1,0:T(8,128)(2,1)S(1)}, u32[]{:S(2)}, u32[]{:S(2)}) collective-permute-start(bf16[64,576]{1,0:T(8,128)(2,1)S(1)} %activate.1.a0), channel_id=1, source_target_pairs={{0,2},{1,3},{2,0},{3,1},{4,6},{5,7},{6,4},{7,5},{8,10},{9,11},{10,... | collective-permute-start | bytes 221192 | tf_op jit(solution)/shard_map/down/ppermute | solution.py:38
  111.0 5.1 %collective-permute-start.13 = (bf16[64,576]{1,0:T(8,128)(2,1)S(1)}, bf16[64,576]{1,0:T(8,128)(2,1)S(1)}, u32[]{:S(2)}, u32[]{:S(2)}) collective-permute-start(bf16[64,576]{1,0:T(8,128)(2,1)S(1)} %activate.1.a0), channel_id=1, source_target_pairs={{0,1},{1,2},{2,3},{3,0},{4,5},{5,6},{6,7},{7,4},{8,9},{9,10},{10,1... | collective-permute-start | bytes 221192 | tf_op jit(solution)/shard_map/down/ppermute | solution.py:38
  118.5 13.7 %all-to-all-start.4 = ((bf16[4,64,1792]{2,1,0:T(8,128)(2,1)}), bf16[4,64,1792]{2,1,0:T(8,128)(2,1)S(1)}, u32[]{:S(2)}, u32[]{:S(2)}) async-start(bf16[4,64,1792]{2,1,0:T(8,128)(2,1)} %bitcast.18), calls=%async_computation.4 | async-start | bytes 1835008 | tf_op jit(solution)/shard_map/sum_y/all_to_all | solution.py:446
  133.1 14.1 %all-to-all-start.5 = ((bf16[8,8,1792]{2,1,0:T(8,128)(2,1)}), bf16[8,8,1792]{2,1,0:T(8,128)(2,1)S(1)}, u32[]{:S(2)}, u32[]{:S(2)}) async-start(bf16[8,8,1792]{2,1,0:T(8,128)(2,1)} %bitcast.19), calls=%async_computation.5 | async-start | bytes 458752 | tf_op jit(solution)/shard_map/sum_z/all_to_all | solution.py:450
